TPU v7x, 32 devices: a whole 2x2x4 slice. The times are simulated.
32 devices in a mesh: dp: 32 (over z, y, x, core).
Axes of the slice: x: 2, y: 2, z: 4, core: 2. Of those that a mesh axis runs over, the one named last changes fastest.
Arguments:
- picture_patch_inputs: bfloat16 [19200, 768], P('dp'), may hold values from -6 to 6
- caption_packed_inputs: bfloat16 [7392, 512], P('dp'), may hold values from -6 to 6
- picture_attend_entry_weight: bfloat16 [1, 768, 2304], P(None, 'dp'), may hold values from -0.21875 to 0.21875
- picture_attend_exit_weight: bfloat16 [1, 768, 768], P(None, 'dp'), may hold values from -0.625 to 0.625
- picture_widening_weight: bfloat16 [1, 768, 3072], P(None, 'dp'), may hold values from -0.21875 to 0.21875
- picture_narrowing_weight: bfloat16 [1, 3072, 768], P(None, 'dp'), may hold values from -0.109375 to 0.109375
- picture_affine_entries: bfloat16 [1, 8, 768], P(None, None, 'dp'), as said below
- picture_widening_offset: bfloat16 [1, 3072], P(None, 'dp'), may hold values from -2.5 to 2.5
- caption_attend_entry_weight: bfloat16 [1, 512, 1536], P(None, 'dp'), may hold values from -0.25 to 0.25
- caption_attend_exit_weight: bfloat16 [1, 512, 512], P(None, 'dp'), may hold values from -0.5 to 0.5
- caption_widening_weight: bfloat16 [1, 512, 2048], P(None, 'dp'), may hold values from -0.25 to 0.25
- caption_narrowing_weight: bfloat16 [1, 2048, 512], P(None, 'dp'), may hold values from -0.125 to 0.125
- caption_affine_entries: bfloat16 [1, 8, 512], P(None, None, 'dp'), as said below
- caption_widening_offset: bfloat16 [1, 2048], P(None, 'dp'), may hold values from -2.5 to 2.5
- picture_feature_mapping: bfloat16 [768, 512], P('dp'), may hold values from -0.21875 to 0.21875
- sharpness_exponent: float32 [], replicated, may hold values from 3.4 to 3.9
- caption_token_counts: int32 [96, 4], P('dp'), may hold values from 1 to 32, 77 in all within a row
- matching_picture_index: int32 [384], P('dp'), may hold values from 0 to 383, each once
Outputs:
- loss: float32 [], replicated
- d_logit_scale: float32 [], replicated
- d_x_img: float32 [19200, 768], P('dp')
- d_x_txt: float32 [7392, 512], P('dp')
- d_img_qkv: float32 [1, 768, 2304], P(None, 'dp')
- d_img_out: float32 [1, 768, 768], P(None, 'dp')
- d_img_fc: float32 [1, 768, 3072], P(None, 'dp')
- d_img_proj: float32 [1, 3072, 768], P(None, 'dp')
- d_img_vec: float32 [1, 8, 768], P(None, None, 'dp')
- d_img_fcb: float32 [1, 3072], P(None, 'dp')
- d_txt_qkv: float32 [1, 512, 1536], P(None, 'dp')
- d_txt_out: float32 [1, 512, 512], P(None, 'dp')
- d_txt_fc: float32 [1, 512, 2048], P(None, 'dp')
- d_txt_proj: float32 [1, 2048, 512], P(None, 'dp')
- d_txt_vec: float32 [1, 8, 512], P(None, None, 'dp')
- d_txt_fcb: float32 [1, 2048], P(None, 'dp')
- d_w_img: float32 [768, 512], P('dp')
Inputs may be any that keep to these rules, and one draw needn't show every extreme that they name: `caption_token_counts`: each row's 4 lengths add up to 77, and the longest is 32. `matching_picture_index`: every image is paired with exactly one caption. `picture_affine_entries`: rows 0 and 5 of each layer are gains between 0.7 and 1.3; the other rows are biases. `caption_affine_entries`: as picture_affine_entries.
All inputs are finite; a program needn't handle non-finite values.
Results may differ from a plain program's by a relative error of at most 0.015.
Values may be sent and summed in bfloat16 or wider, within the bound.
A program may use at most 256 MiB of HBM per device.

v0:
```python
import jax
import jax.numpy as jnp
from jax import lax
from jax.sharding import PartitionSpec as P

HD = 64
TOK_I = 50
TOK_T = 77
CAP_ROW = 4


def norm_forward(hidden, norm_gain, norm_shift):
    row_mean = jnp.mean(hidden, -1, keepdims=True)
    centred = hidden - row_mean
    inverse = lax.rsqrt(jnp.mean(centred * centred, -1, keepdims=True) + 1e-05)
    normed = centred * inverse
    return (normed, inverse, normed * norm_gain + norm_shift)


def norm_backward(upstream, normed, inverse, norm_gain):
    scaled = upstream * norm_gain
    inner_sum = (
        scaled
        - jnp.mean(scaled, -1, keepdims=True)
        - normed * jnp.mean(scaled * normed, -1, keepdims=True)
    )
    return (inverse * inner_sum, jnp.sum(upstream * normed, (0, 1)), jnp.sum(upstream, (0, 1)))


def split_heads(values):
    return values.reshape(values.shape[0], values.shape[1], values.shape[2] // HD, HD)


def attention_scores(queries, key_heads, allowed):
    scores = (
        jnp.einsum("sqhd,skhd->shqk", queries, key_heads, preferred_element_type=jnp.float32)
        * 0.125
    )
    return jnp.where(allowed[:, None], scores, -1000000000.0)


def block_forward(hidden, weights, allowed):
    w_qkv, w_out, w_fc, w_proj, vectors, fc_bias = weights
    vectors = vectors.astype(jnp.float32)
    fc_bias = fc_bias.astype(jnp.float32)
    feature_width = hidden.shape[-1]
    normed_first, inverse_first, first = norm_forward(hidden, vectors[0], vectors[1])
    first_low = first.astype(jnp.bfloat16)
    projected = jnp.einsum("std,de->ste", first_low, w_qkv, preferred_element_type=jnp.float32)
    queries = (projected[..., :feature_width] + vectors[2]).astype(jnp.bfloat16)
    key_heads = projected[..., feature_width : 2 * feature_width].astype(jnp.bfloat16)
    values = (projected[..., 2 * feature_width :] + vectors[3]).astype(jnp.bfloat16)
    scores = attention_scores(split_heads(queries), split_heads(key_heads), allowed)
    totals = jax.nn.logsumexp(scores, -1, keepdims=True)
    attn_probs = jnp.exp(scores - totals).astype(jnp.bfloat16)
    context = jnp.einsum(
        "shqk,skhd->sqhd", attn_probs, split_heads(values), preferred_element_type=jnp.float32
    )
    context = context.reshape(hidden.shape).astype(jnp.bfloat16)
    middle = hidden + (
        jnp.einsum("std,de->ste", context, w_out, preferred_element_type=jnp.float32) + vectors[4]
    )
    normed_second, inverse_second, second = norm_forward(middle, vectors[5], vectors[6])
    second_low = second.astype(jnp.bfloat16)
    upward = (
        jnp.einsum("std,df->stf", second_low, w_fc, preferred_element_type=jnp.float32) + fc_bias
    )
    activated = (upward * jax.nn.sigmoid(1.702 * upward)).astype(jnp.bfloat16)
    output = middle + (
        jnp.einsum("stf,fd->std", activated, w_proj, preferred_element_type=jnp.float32)
        + vectors[7]
    )
    stored = (
        normed_first,
        inverse_first,
        first_low,
        queries,
        key_heads,
        values,
        totals,
        context,
        normed_second,
        inverse_second,
        second_low,
        upward,
        activated,
    )
    return (output, stored)


def block_backward(upstream, weights, stored, allowed):
    w_qkv, w_out, w_fc, w_proj, vectors, fc_bias = weights
    vectors = vectors.astype(jnp.float32)
    (
        normed_first,
        inverse_first,
        first_low,
        queries,
        key_heads,
        values,
        totals,
        context,
        normed_second,
        inverse_second,
        second_low,
        upward,
        activated,
    ) = stored
    feature_width = queries.shape[-1]
    branch = upstream.astype(jnp.bfloat16)
    d_proj_bias = jnp.sum(branch.astype(jnp.float32), (0, 1))
    d_w_proj = jnp.einsum("stf,std->fd", activated, branch, preferred_element_type=jnp.float32)
    d_activated = jnp.einsum("std,fd->stf", branch, w_proj, preferred_element_type=jnp.float32)
    sigmoid_up = jax.nn.sigmoid(1.702 * upward)
    d_upward = (
        d_activated * (sigmoid_up + 1.702 * upward * sigmoid_up * (1.0 - sigmoid_up))
    ).astype(jnp.bfloat16)
    d_fc_bias = jnp.sum(d_upward.astype(jnp.float32), (0, 1))
    d_w_fc = jnp.einsum("std,stf->df", second_low, d_upward, preferred_element_type=jnp.float32)
    d_second = jnp.einsum("stf,df->std", d_upward, w_fc, preferred_element_type=jnp.float32)
    d_middle_norm, d_gain_second, d_shift_second = norm_backward(
        d_second, normed_second, inverse_second, vectors[5]
    )
    d_middle = upstream + d_middle_norm
    attn_branch = d_middle.astype(jnp.bfloat16)
    d_out_bias = jnp.sum(attn_branch.astype(jnp.float32), (0, 1))
    d_w_out = jnp.einsum("std,ste->de", context, attn_branch, preferred_element_type=jnp.float32)
    d_context = jnp.einsum("ste,de->std", attn_branch, w_out, preferred_element_type=jnp.float32)
    d_context = split_heads(d_context.astype(jnp.bfloat16))
    query_heads = split_heads(queries)
    key_split = split_heads(key_heads)
    scores = attention_scores(query_heads, key_split, allowed)
    attn_probs = jnp.exp(scores - totals)
    d_probs = jnp.einsum(
        "sqhd,skhd->shqk", d_context, split_heads(values), preferred_element_type=jnp.float32
    )
    d_scores = (attn_probs * (d_probs - jnp.sum(attn_probs * d_probs, -1, keepdims=True))).astype(
        jnp.bfloat16
    )
    d_queries = (
        jnp.einsum("shqk,skhd->sqhd", d_scores, key_split, preferred_element_type=jnp.float32)
        * 0.125
    ).astype(jnp.bfloat16)
    d_keys = (
        jnp.einsum("shqk,sqhd->skhd", d_scores, query_heads, preferred_element_type=jnp.float32)
        * 0.125
    ).astype(jnp.bfloat16)
    d_values = jnp.einsum(
        "shqk,sqhd->skhd",
        attn_probs.astype(jnp.bfloat16),
        d_context,
        preferred_element_type=jnp.float32,
    ).astype(jnp.bfloat16)
    flat_shape = (queries.shape[0], queries.shape[1], feature_width)
    d_queries = d_queries.reshape(flat_shape)
    d_keys = d_keys.reshape(flat_shape)
    d_values = d_values.reshape(flat_shape)
    d_mixed = jnp.concatenate([d_queries, d_keys, d_values], -1)
    d_w_qkv = jnp.einsum("std,ste->de", first_low, d_mixed, preferred_element_type=jnp.float32)
    d_first = jnp.einsum("ste,de->std", d_mixed, w_qkv, preferred_element_type=jnp.float32)
    d_input_norm, d_gain_first, d_shift_first = norm_backward(
        d_first, normed_first, inverse_first, vectors[0]
    )
    d_hidden = d_middle + d_input_norm
    d_vectors = jnp.stack(
        [
            d_gain_first,
            d_shift_first,
            jnp.sum(d_queries.astype(jnp.float32), (0, 1)),
            jnp.sum(d_values.astype(jnp.float32), (0, 1)),
            d_out_bias,
            d_gain_second,
            d_shift_second,
            d_proj_bias,
        ]
    )
    return (d_hidden, (d_w_qkv, d_w_out, d_w_fc, d_w_proj, d_vectors, d_fc_bias))


def gather_first(img_stack, txt_stack, picture_feature_mapping):
    return (
        lax.all_gather(img_stack[0], "dp", axis=1, tiled=True),
        lax.all_gather(img_stack[1], "dp", axis=1, tiled=True),
        lax.all_gather(img_stack[2], "dp", axis=1, tiled=True),
        lax.all_gather(img_stack[3], "dp", axis=1, tiled=True),
        lax.all_gather(img_stack[4], "dp", axis=2, tiled=True),
        lax.all_gather(img_stack[5], "dp", axis=1, tiled=True),
        lax.all_gather(txt_stack[0], "dp", axis=1, tiled=True),
        lax.all_gather(txt_stack[1], "dp", axis=1, tiled=True),
        lax.all_gather(txt_stack[2], "dp", axis=1, tiled=True),
        lax.all_gather(txt_stack[3], "dp", axis=1, tiled=True),
        lax.all_gather(txt_stack[4], "dp", axis=2, tiled=True),
        lax.all_gather(txt_stack[5], "dp", axis=1, tiled=True),
        lax.all_gather(picture_feature_mapping, "dp", axis=0, tiled=True),
    )


def layer_of(stacks, layer_index):
    return tuple((stacked[layer_index] for stacked in stacks))


def local(
    picture_patch_inputs,
    caption_packed_inputs,
    picture_attend_entry_weight,
    picture_attend_exit_weight,
    picture_widening_weight,
    picture_narrowing_weight,
    picture_affine_entries,
    picture_widening_offset,
    caption_attend_entry_weight,
    caption_attend_exit_weight,
    caption_widening_weight,
    caption_narrowing_weight,
    caption_affine_entries,
    caption_widening_offset,
    picture_feature_mapping,
    sharpness_exponent,
    caption_token_counts,
    matching_picture_index,
):
    img_stack = (
        picture_attend_entry_weight,
        picture_attend_exit_weight,
        picture_widening_weight,
        picture_narrowing_weight,
        picture_affine_entries,
        picture_widening_offset,
    )
    txt_stack = (
        caption_attend_entry_weight,
        caption_attend_exit_weight,
        caption_widening_weight,
        caption_narrowing_weight,
        caption_affine_entries,
        caption_widening_offset,
    )
    images = picture_patch_inputs.shape[0] // TOK_I
    row_count = caption_packed_inputs.shape[0] // TOK_T
    img_hidden = picture_patch_inputs.astype(jnp.float32).reshape(images, TOK_I, -1)
    txt_hidden = caption_packed_inputs.astype(jnp.float32).reshape(row_count, TOK_T, -1)
    img_allowed = jnp.ones((images, TOK_I, TOK_I), dtype=jnp.bool_)
    seg_ends = jnp.cumsum(caption_token_counts, axis=1)
    position = jnp.arange(TOK_T, dtype=jnp.int32)
    segment = jnp.sum((position[None, :, None] >= seg_ends[:, None, :]).astype(jnp.int32), -1)
    txt_allowed = (segment[:, :, None] == segment[:, None, :]) & (
        position[None, None, :] <= position[None, :, None]
    )
    pooling = (position[None, None, :] == seg_ends[:, :, None] - 1).astype(jnp.float32)
    gathered = gather_first(img_stack, txt_stack, picture_feature_mapping)
    img_full = gathered[0:6]
    txt_full = gathered[6:12]
    projection = gathered[12]
    img_stored, txt_stored = ([], [])
    layer_index = 0
    img_hidden, stored = block_forward(img_hidden, layer_of(img_full, layer_index), img_allowed)
    img_stored.append(stored)
    layer_index = 0
    txt_hidden, stored = block_forward(txt_hidden, layer_of(txt_full, layer_index), txt_allowed)
    txt_stored.append(stored)
    pooled_img = img_hidden[:, 0, :].astype(jnp.bfloat16)
    raw_img = jnp.dot(pooled_img, projection, preferred_element_type=jnp.float32)
    scale_img = lax.rsqrt(jnp.sum(raw_img * raw_img, -1, keepdims=True) + 1e-06)
    unit_img = raw_img * scale_img
    raw_txt = jnp.einsum("sct,std->scd", pooling, txt_hidden, precision=lax.Precision.HIGHEST)
    raw_txt = raw_txt.reshape(-1, raw_txt.shape[-1])
    scale_txt = lax.rsqrt(jnp.sum(raw_txt * raw_txt, -1, keepdims=True) + 1e-06)
    unit_txt = raw_txt * scale_txt
    image_embedding_rows = unit_img.astype(jnp.bfloat16)
    text_embedding_rows = unit_txt.astype(jnp.bfloat16)
    all_img, all_txt = (
        lax.all_gather(image_embedding_rows, "dp", axis=0, tiled=True),
        lax.all_gather(text_embedding_rows, "dp", axis=0, tiled=True),
    )
    batch_total = all_img.shape[0]
    affinity_sharpness = jnp.exp(sharpness_exponent)
    picture_wise_affinity_table = affinity_sharpness * jnp.einsum(
        "ce,ie->ci", text_embedding_rows, all_img, preferred_element_type=jnp.float32
    )
    caption_wise_affinity_table = affinity_sharpness * jnp.einsum(
        "ce,ie->ci", all_txt, image_embedding_rows, preferred_element_type=jnp.float32
    )
    lse_rows = jax.nn.logsumexp(picture_wise_affinity_table, 1)
    lse_cols = jax.nn.logsumexp(caption_wise_affinity_table, 0)
    columns = jnp.arange(batch_total, dtype=jnp.int32)
    target_rows = (matching_picture_index[:, None] == columns[None, :]).astype(jnp.float32)
    loss_part = (jnp.sum(lse_rows) + jnp.sum(lse_cols)) / (2 * batch_total) - jnp.sum(
        target_rows * picture_wise_affinity_table
    ) / batch_total
    probs_rows = jnp.exp(picture_wise_affinity_table - lse_rows[:, None])
    probs_cols = jnp.exp(caption_wise_affinity_table - lse_cols[None, :])
    gathered_image_matrix = all_img.astype(jnp.float32)
    gathered_text_matrix = all_txt.astype(jnp.float32)
    highest_precision = lax.Precision.HIGHEST
    row_gradient = probs_rows / (2 * batch_total) - target_rows / batch_total
    column_gradient = probs_cols / (2 * batch_total)
    caption_normalized_adjoint = affinity_sharpness * jnp.dot(
        row_gradient, gathered_image_matrix, precision=highest_precision
    )
    picture_normalized_adjoint = affinity_sharpness * jnp.dot(
        column_gradient.T, gathered_text_matrix, precision=highest_precision
    )
    picture_distributed_adjoint = affinity_sharpness * jnp.dot(
        row_gradient.T, text_embedding_rows.astype(jnp.float32), precision=highest_precision
    )
    caption_distributed_adjoint = affinity_sharpness * jnp.dot(
        column_gradient, image_embedding_rows.astype(jnp.float32), precision=highest_precision
    )
    back_img, back_txt = (
        lax.psum_scatter(picture_distributed_adjoint, "dp", scatter_dimension=0, tiled=True),
        lax.psum_scatter(caption_distributed_adjoint, "dp", scatter_dimension=0, tiled=True),
    )
    picture_normalized_adjoint = picture_normalized_adjoint + back_img
    caption_normalized_adjoint = caption_normalized_adjoint + back_txt
    scale_part = jnp.sum(row_gradient * picture_wise_affinity_table) + jnp.sum(
        column_gradient * caption_wise_affinity_table
    )
    loss, d_scale = lax.psum((loss_part, scale_part), "dp")
    img_back = gathered[0:6]
    txt_back = gathered[6:12]
    back_projection = gathered[12]
    d_raw_img = scale_img * (
        picture_normalized_adjoint
        - unit_img * jnp.sum(picture_normalized_adjoint * unit_img, -1, keepdims=True)
    )
    d_raw_low = d_raw_img.astype(jnp.bfloat16)
    d_projection = jnp.dot(pooled_img.T, d_raw_low, preferred_element_type=jnp.float32)
    d_pooled = jnp.dot(d_raw_low, back_projection.T, preferred_element_type=jnp.float32)
    d_img_hidden = jnp.concatenate(
        [d_pooled[:, None, :], jnp.zeros((images, TOK_I - 1, d_pooled.shape[-1]), jnp.float32)], 1
    )
    d_raw_txt = scale_txt * (
        caption_normalized_adjoint
        - unit_txt * jnp.sum(caption_normalized_adjoint * unit_txt, -1, keepdims=True)
    )
    d_txt_hidden = jnp.einsum(
        "sct,scd->std",
        pooling,
        d_raw_txt.reshape(row_count, CAP_ROW, -1),
        precision=highest_precision,
    )
    img_layer_grads, txt_layer_grads = ([], [])
    layer_index = 0
    d_img_hidden, layer_grads = block_backward(
        d_img_hidden, layer_of(img_back, layer_index), img_stored[layer_index], img_allowed
    )
    img_layer_grads.append(layer_grads)
    img_layer_grads = img_layer_grads[::-1]
    img_local = tuple(
        (jnp.stack([grads[member] for grads in img_layer_grads]) for member in range(6))
    )
    layer_index = 0
    d_txt_hidden, layer_grads = block_backward(
        d_txt_hidden, layer_of(txt_back, layer_index), txt_stored[layer_index], txt_allowed
    )
    txt_layer_grads.append(layer_grads)
    txt_layer_grads = txt_layer_grads[::-1]
    txt_local = tuple(
        (jnp.stack([grads[member] for grads in txt_layer_grads]) for member in range(6))
    )
    summed = (
        lax.psum_scatter(img_local[0], "dp", scatter_dimension=1, tiled=True),
        lax.psum_scatter(img_local[1], "dp", scatter_dimension=1, tiled=True),
        lax.psum_scatter(img_local[2], "dp", scatter_dimension=1, tiled=True),
        lax.psum_scatter(img_local[3], "dp", scatter_dimension=1, tiled=True),
        lax.psum_scatter(img_local[4], "dp", scatter_dimension=2, tiled=True),
        lax.psum_scatter(img_local[5], "dp", scatter_dimension=1, tiled=True),
        lax.psum_scatter(txt_local[0], "dp", scatter_dimension=1, tiled=True),
        lax.psum_scatter(txt_local[1], "dp", scatter_dimension=1, tiled=True),
        lax.psum_scatter(txt_local[2], "dp", scatter_dimension=1, tiled=True),
        lax.psum_scatter(txt_local[3], "dp", scatter_dimension=1, tiled=True),
        lax.psum_scatter(txt_local[4], "dp", scatter_dimension=2, tiled=True),
        lax.psum_scatter(txt_local[5], "dp", scatter_dimension=1, tiled=True),
        lax.psum_scatter(d_projection, "dp", scatter_dimension=0, tiled=True),
    )
    return (
        loss,
        d_scale,
        d_img_hidden.reshape(images * TOK_I, -1),
        d_txt_hidden.reshape(row_count * TOK_T, -1),
        summed[0],
        summed[1],
        summed[2],
        summed[3],
        summed[4],
        summed[5],
        summed[6],
        summed[7],
        summed[8],
        summed[9],
        summed[10],
        summed[11],
        summed[12],
    )


def solution(mesh):
    placed = (
        P("dp", None),
        P("dp", None),
        P(None, "dp", None),
        P(None, "dp", None),
        P(None, "dp", None),
        P(None, "dp", None),
        P(None, None, "dp"),
        P(None, "dp"),
        P(None, "dp", None),
        P(None, "dp", None),
        P(None, "dp", None),
        P(None, "dp", None),
        P(None, None, "dp"),
        P(None, "dp"),
        P("dp", None),
        P(),
        P("dp", None),
        P("dp"),
    )
    return jax.shard_map(
        local,
        mesh=mesh,
        in_specs=placed,
        out_specs=(
            P(),
            P(),
            P("dp", None),
            P("dp", None),
            P(None, "dp", None),
            P(None, "dp", None),
            P(None, "dp", None),
            P(None, "dp", None),
            P(None, None, "dp"),
            P(None, "dp"),
            P(None, "dp", None),
            P(None, "dp", None),
            P(None, "dp", None),
            P(None, "dp", None),
            P(None, None, "dp"),
            P(None, "dp"),
            P("dp", None),
        ),
        check_vma=False,
    )
```

profile of v0, /device:TPU:0, one launch (start us, length us, event | category | flops | bytes accessed | tf_op | source)
XLA Modules:
  0.0 2173.5 jit_solution(14360490427655546192)
XLA Ops:
  12.7 44.6 %all_gather.51 = bf16[1,8,768]{1,0,2:T(2,128)(2,1)S(1)} all-gather(bf16[1,8,24]{1,0,2:T(2,128)(2,1)S(1)} %copy.165), channel_id=1, replica_groups=mesh['dp'=32] {'dp'}, dimensions={2}, use_global_device_ids=true | all-gather | bytes 12672 | tf_op jit(solution)/shard_map/all_gather | solution.py:186
  57.7 19.8 slice_reduce_fusion
  78.3 38.0 %all_gather.45 = bf16[1,8,512]{1,0,2:T(2,128)(2,1)S(1)} all-gather(bf16[1,8,16]{1,0,2:T(2,128)(2,1)S(1)} %copy.159), channel_id=1, replica_groups=mesh['dp'=32] {'dp'}, dimensions={2}, use_global_device_ids=true | all-gather | bytes 8448 | tf_op jit(solution)/shard_map/all_gather | solution.py:192
  116.6 13.5 slice_reduce_fusion.10
  130.7 39.8 %all_gather.47 = bf16[1,512,512]{2,1,0:T(8,128)(2,1)S(1)} all-gather(bf16[1,16,512]{2,1,0:T(8,128)(2,1)S(1)} %copy-done.96), channel_id=1, replica_groups=mesh['dp'=32] {'dp'}, dimensions={1}, use_global_device_ids=true | all-gather | bytes 540672 | tf_op jit(solution)/shard_map/all_gather | solution.py:189
  175.2 37.2 %all-reduce.9 = (bf16[2048]{0:T(1024)(128)(2,1)S(1)}, bf16[3072]{0:T(1024)(128)(2,1)S(1)}) all-reduce(bf16[2048]{0:T(1024)(128)(2,1)S(1)} %dynamic-update-slice, bf16[3072]{0:T(1024)(128)(2,1)S(1)} %dynamic-update-slice.1), channel_id=1, replica_groups=mesh['dp'=32] {'dp'}, use_global_device_ids=true, to_apply=%add.1 | all-reduce | flops 5120 | bytes 20480
  213.8 45.9 %all_gather.57 = bf16[768,512]{1,0:T(8,128)(2,1)} all-gather(bf16[24,512]{1,0:T(8,128)(2,1)S(1)} %copy-done.83), channel_id=1, replica_groups=mesh['dp'=32] {'dp'}, dimensions={0}, use_global_device_ids=true | all-gather | bytes 811008 | tf_op jit(solution)/shard_map/all_gather | solution.py:194
  267.1 3.0 fusion.49
  270.7 38.4 %all-gather.1 = bf16[32,12,512]{2,1,0:T(8,128)(2,1)S(1)} all-gather(bf16[1,12,512]{2,1,0:T(8,128)(2,1)S(1)} %fusion.165), channel_id=1, replica_groups=mesh['dp'=32] {'dp'}, dimensions={0}, use_global_device_ids=true | all-gather | bytes 405504 | tf_op jit(solution)/shard_map/all_gather | solution.py:273
  309.9 4.9 fusion.11
  317.6 3.2 reshape.405
  320.8 4.4 reshape.406
  325.2 4.1 reshape.404
  329.3 3.1 multiply_reduce_fusion.1
  337.4 2.5 convert_element_type.255
  340.0 3.3 fusion.122
  343.7 27.9 %all-gather.20.cloned.1.call-done = bf16[1,768,3072]{2,1,0:T(8,128)(2,1)} async-done(((bf16[1,24,3072]{2,1,0:T(8,128)(2,1)}), bf16[1,768,3072]{2,1,0:T(8,128)(2,1)}) %all-gather.20.cloned.1.call-update) | async-done | bytes 4718608 | tf_op jit(solution)/shard_map/all_gather | solution.py:184
  371.6 8.2 fusion.7
  379.8 57.2 %all-gather.22.cloned.1.call-done = bf16[1,3072,768]{2,1,0:T(8,128)(2,1)} async-done(((bf16[1,96,768]{2,1,0:T(8,128)(2,1)}), bf16[1,3072,768]{2,1,0:T(8,128)(2,1)}) %all-gather.22.cloned.1.call-update) | async-done | bytes 4718608 | tf_op jit(solution)/shard_map/all_gather | solution.py:185
  437.0 8.6 fusion.3
  446.4 43.8 %all-gather = bf16[32,12,512]{2,1,0:T(8,128)(2,1)} all-gather(bf16[1,12,512]{2,1,0:T(8,128)(2,1)S(1)} %fusion.164), channel_id=1, replica_groups=mesh['dp'=32] {'dp'}, dimensions={0}, use_global_device_ids=true | all-gather | bytes 405504 | tf_op jit(solution)/shard_map/all_gather | solution.py:272
  500.4 77.6 %fusion.117 = (f32[16,512]{1,0:T(8,128)}, f32[16,512]{1,0:T(8,128)}) fusion(f32[384,512]{1,0:T(8,128)} %convolution_multiply_fusion.5, f32[384,512]{1,0:T(8,128)} %convolution_multiply_fusion.4), kind=kCustom, calls=%all-reduce-scatter.2 | all-reduce-scatter fusion | flops 524289 | bytes 1638400
  587.1 5.0 collective-permute-start.14
  592.1 2.9 collective-permute-start.8
  594.9 3.7 collective-permute-start.9
  602.0 4.3 collective-permute-start
  610.1 2.9 collective-permute-start.3
  614.9 12.7 concatenate.13
  630.9 4.1 convert_reduce_fusion.5
  646.1 2.5 collective-permute-start.5
  652.2 12.7 concatenate.12
  668.5 10.4 convert_reduce_fusion
  687.5 3.8 multiply_reduce_fusion.12
  701.8 8.0 multiply_reduce_fusion.2
  712.6 2.6 convolution_bitcast_fusion.6
  715.2 3.6 convolution_bitcast_fusion.3
  718.9 4.1 convolution_bitcast_fusion.5
  724.1 4.4 convolution_bitcast_fusion.4
  729.3 3.9 convolution_convert_fusion
  733.2 4.1 reshape.407
  737.3 4.3 convert_reduce_fusion.1
  743.5 4.3 reshape.410
  747.7 5.7 multiply_reduce_fusion
  758.3 4.2 reshape.409
  762.5 3.7 convert_reduce_fusion.2
  768.1 4.3 reshape.408
  776.1 5.5 convolution_bitcast_fusion.2
  782.3 8.7 convolution_bitcast_fusion.1
  791.8 11.8 convolution_bitcast_fusion
  809.0 7.8 multiply_reduce_fusion.3
  817.1 39.4 %all-reduce.8 = (f32[]{:T(128)}, f32[]{:T(128)}, f32[1,8,768]{2,1,0:T(8,128)}) all-reduce(f32[]{:T(128)S(6)} %sub.218, f32[]{:T(128)S(6)} %add.378, f32[1,8,768]{2,1,0:T(8,128)S(1)} %bitcast.207), channel_id=1, replica_groups=mesh['dp'=32] {'dp'}, use_global_device_ids=true, to_apply=%region_23.24 | all-reduce | flops 6146 | bytes 49168 | tf_op jit(solution)/shard_map/psum | solution.py:318
  860.0 4.2 multiply_add_fusion
  864.2 2.7 reshape.411
  869.6 31.1 %reduce-scatter.42.cloned.1.call-done = f32[96,1]{1,0:T(8,128)} async-done(((f32[3072,1]{1,0:T(8,128)}), f32[96,1]{1,0:T(8,128)}) %reduce-scatter.42.cloned.1.call-update) | async-done | bytes 400
  902.1 133.3 %reduce-scatter.44.cloned.1.call-done = f32[16,8]{1,0:T(8,128)} async-done(((f32[512,8]{1,0:T(8,128)}), f32[16,8]{1,0:T(8,128)}) %reduce-scatter.44.cloned.1.call-update) | async-done | bytes 528
  1036.8 132.2 %reduce-scatter.34.cloned.1.call-done = f32[1,16,512]{2,1,0:T(8,128)} async-done(((f32[1,512,512]{2,1,0:T(8,128)}), f32[1,16,512]{2,1,0:T(8,128)}) %reduce-scatter.34.cloned.1.call-update) | async-done | bytes 32784 | tf_op jit(solution)/shard_map/reduce_scatter | solution.py:369
  1169.0 99.6 %reduce-scatter.40.cloned.1.call-done = f32[24,512]{1,0:T(8,128)} async-done(((f32[768,512]{1,0:T(8,128)}), f32[24,512]{1,0:T(8,128)}) %reduce-scatter.40.cloned.1.call-update) | async-done | bytes 49168 | tf_op jit(solution)/shard_map/reduce_scatter | solution.py:374
  1268.5 104.8 %reduce-scatter.26.cloned.1.call-done = f32[1,24,768]{2,1,0:T(8,128)} async-done(((f32[1,768,768]{2,1,0:T(8,128)}), f32[1,24,768]{2,1,0:T(8,128)}) %reduce-scatter.26.cloned.1.call-update) | async-done | bytes 73744 | tf_op jit(solution)/shard_map/reduce_scatter | solution.py:363
  1373.3 106.4 %reduce-scatter.32.cloned.1.call-done = f32[1,16,1536]{2,1,0:T(8,128)} async-done(((f32[1,512,1536]{2,1,0:T(8,128)}), f32[1,16,1536]{2,1,0:T(8,128)}) %reduce-scatter.32.cloned.1.call-update) | async-done | bytes 98320 | tf_op jit(solution)/shard_map/reduce_scatter | solution.py:368
  1479.8 142.8 %reduce-scatter.36.cloned.1.call-done = f32[1,16,2048]{2,1,0:T(8,128)} async-done(((f32[1,512,2048]{2,1,0:T(8,128)}), f32[1,16,2048]{2,1,0:T(8,128)}) %reduce-scatter.36.cloned.1.call-update) | async-done | bytes 131088 | tf_op jit(solution)/shard_map/reduce_scatter | solution.py:370
  1622.5 139.7 %reduce-scatter.38.cloned.1.call-done = f32[1,64,512]{2,1,0:T(8,128)} async-done(((f32[1,2048,512]{2,1,0:T(8,128)}), f32[1,64,512]{2,1,0:T(8,128)}) %reduce-scatter.38.cloned.1.call-update) | async-done | bytes 131088 | tf_op jit(solution)/shard_map/reduce_scatter | solution.py:371
  1762.2 121.1 %reduce-scatter.24.cloned.1.call-done = f32[1,24,2304]{2,1,0:T(8,128)} async-done(((f32[1,768,2304]{2,1,0:T(8,128)}), f32[1,24,2304]{2,1,0:T(8,128)}) %reduce-scatter.24.cloned.1.call-update) | async-done | bytes 221200 | tf_op jit(solution)/shard_map/reduce_scatter | solution.py:362
  1883.3 142.2 %reduce-scatter.28.cloned.1.call-done = f32[1,24,3072]{2,1,0:T(8,128)} async-done(((f32[1,768,3072]{2,1,0:T(8,128)}), f32[1,24,3072]{2,1,0:T(8,128)}) %reduce-scatter.28.cloned.1.call-update) | async-done | bytes 294928 | tf_op jit(solution)/shard_map/reduce_scatter | solution.py:364
  2025.5 141.0 %reduce-scatter.30.cloned.1.call-done = f32[1,96,768]{2,1,0:T(8,128)} async-done(((f32[1,3072,768]{2,1,0:T(8,128)}), f32[1,96,768]{2,1,0:T(8,128)}) %reduce-scatter.30.cloned.1.call-update) | async-done | bytes 294928 | tf_op jit(solution)/shard_map/reduce_scatter | solution.py:365
  (453 shorter events, 128.2 us)
Async XLA Ops:
  7.2 252.6 %all-gather.10.cloned.1.call-start = ((), (), s32[]{:S(2)}) async-start(), calls=%async_computation.12 | async-start | bytes 1622016 | tf_op jit(solution)/shard_map/all_gather | solution.py:188
  7.9 256.7 %all-gather.12.cloned.1.call-start = ((), (), s32[]{:S(2)}) async-start(), calls=%async_computation.13 | async-start | bytes 2162688 | tf_op jit(solution)/shard_map/all_gather | solution.py:190
  8.7 258.4 %all-gather.14.cloned.1.call-start = ((), (), s32[]{:S(2)}) async-start(), calls=%async_computation.14 | async-start | bytes 2162688 | tf_op jit(solution)/shard_map/all_gather | solution.py:191
  9.4 300.5 %all-gather.16.cloned.1.call-start = ((), (), s32[]{:S(2)}) async-start(), calls=%async_computation.15 | async-start | bytes 3649536 | tf_op jit(solution)/shard_map/all_gather | solution.py:182
  10.0 330.0 %all-gather.18.cloned.1.call-start = ((), (), s32[]{:S(2)}) async-start(), calls=%async_computation.16 | async-start | bytes 1216512 | tf_op jit(solution)/shard_map/all_gather | solution.py:183
  10.6 361.0 %all-gather.20.cloned.1.call-start = ((), (), s32[]{:S(2)}) async-start(), calls=%async_computation.17 | async-start | bytes 4866048 | tf_op jit(solution)/shard_map/all_gather | solution.py:184
  11.1 425.9 %all-gather.22.cloned.1.call-start = ((), (), s32[]{:S(2)}) async-start(), calls=%async_computation.18 | async-start | bytes 4866048 | tf_op jit(solution)/shard_map/all_gather | solution.py:185
  11.9 856.4 %reduce-scatter.46.cloned.1.call-start = ((), (), s32[]{:S(2)}) async-start(), calls=%async_computation.30 | async-start | bytes 1081344
  77.5 93.8 %copy-start.68 = (f32[768]{0:T(1024)}, f32[768]{0:T(1024)S(1)}, u32[]{:S(2)}) copy-start(f32[768]{0:T(1024)S(1)} %get-tuple-element.40) | copy-start | bytes 9220
  77.5 93.8 %copy-start.88 = (f32[768]{0:T(1024)}, f32[768]{0:T(1024)S(1)}, u32[]{:S(2)}) copy-start(f32[768]{0:T(1024)S(1)} %get-tuple-element.39) | copy-start | bytes 9220
  77.7 52.3 %copy-start.25 = (bf16[231,512]{1,0:T(8,128)(2,1)S(1)}, bf16[231,512]{1,0:T(8,128)(2,1)}, u32[]{:S(2)}) copy-start(bf16[231,512]{1,0:T(8,128)(2,1)} %param.19) | copy-start | bytes 709636
  77.8 93.6 %copy-start.64 = (f32[600]{0:T(1024)}, f32[600]{0:T(1024)S(1)}, u32[]{:S(2)}) copy-start(f32[600]{0:T(1024)S(1)} %broadcast_multiply_fusion.5) | copy-start | bytes 7204
  77.8 52.7 %copy-start.114 = (s32[3,4]{1,0:T(4,128)S(1)}, s32[3,4]{1,0:T(4,128)}, u32[]{:S(2)}) copy-start(s32[3,4]{1,0:T(4,128)} %param.34) | copy-start | bytes 148
  77.8 53.0 %copy-start.96 = (bf16[1,16,512]{2,1,0:T(8,128)(2,1)S(1)}, bf16[1,16,512]{2,1,0:T(8,128)(2,1)}, u32[]{:S(2)}) copy-start(bf16[1,16,512]{2,1,0:T(8,128)(2,1)} %param.27) | copy-start | bytes 49156
  78.2 93.5 %copy-start.71 = (f32[600]{0:T(1024)}, f32[600]{0:T(1024)S(1)}, u32[]{:S(2)}) copy-start(f32[600]{0:T(1024)S(1)} %add_rsqrt_fusion.1) | copy-start | bytes 7204
  130.1 43.4 %copy-start.79 = (f32[512]{0:T(512)}, f32[512]{0:T(512)S(1)}, u32[]{:S(2)}) copy-start(f32[512]{0:T(512)S(1)} %get-tuple-element.48) | copy-start | bytes 6148
  130.1 134.6 %copy-start.81 = (f32[512]{0:T(512)}, f32[512]{0:T(512)S(1)}, u32[]{:S(2)}) copy-start(f32[512]{0:T(512)S(1)} %get-tuple-element.41) | copy-start | bytes 6148
  130.1 134.6 %copy-start.86 = (f32[512]{0:T(512)}, f32[512]{0:T(512)S(1)}, u32[]{:S(2)}) copy-start(f32[512]{0:T(512)S(1)} %get-tuple-element.43) | copy-start | bytes 6148
  130.2 43.2 %copy-start.94 = (f32[231]{0:T(256)}, f32[231]{0:T(256)S(1)}, u32[]{:S(2)}) copy-start(f32[231]{0:T(256)S(1)} %broadcast_multiply_fusion.11) | copy-start | bytes 2776
  170.5 93.3 %copy-start.19 = (bf16[1,512,512]{2,1,0:T(8,128)(2,1)}, bf16[1,512,512]{2,1,0:T(8,128)(2,1)S(1)}, u32[]{:S(2)}) copy-start(bf16[1,512,512]{2,1,0:T(8,128)(2,1)S(1)} %all_gather.47) | copy-start | bytes 1572868
  171.9 98.2 %copy-start.84 = (s32[3,4]{1,0:T(4,128)}, s32[3,4]{1,0:T(4,128)S(1)}, u32[]{:S(2)}) copy-start(s32[3,4]{1,0:T(4,128)S(1)} %broadcast_add_fusion) | copy-start | bytes 148
  173.6 90.3 %copy-start.13 = (f32[3,77,512]{2,1,0:T(8,128)}, f32[3,77,512]{2,1,0:T(8,128)S(1)}, u32[]{:S(2)}) copy-start(f32[3,77,512]{2,1,0:T(8,128)S(1)} %reshape.398) | copy-start | bytes 1419268
  270.6 357.0 %copy-start.85 = (f32[12]{0:T(128)}, f32[12]{0:T(128)S(1)}, u32[]{:S(2)}) copy-start(f32[12]{0:T(128)S(1)} %rsqrt.62) | copy-start | bytes 148
  371.6 65.4 %copy-start.99 = (f32[3072]{0:T(1024)S(1)}, f32[3072]{0:T(1024)}, u32[]{:S(2)}) copy-start(f32[3072]{0:T(1024)} %convert_element_type.300) | copy-start | bytes 36868
  379.8 65.8 %copy-start.91 = (f32[768]{0:T(1024)S(1)}, f32[768]{0:T(1024)}, u32[]{:S(2)}) copy-start(f32[768]{0:T(1024)} %get-tuple-element.33) | copy-start | bytes 9220
  445.6 47.9 %copy-start.26 = (bf16[384,512]{1,0:T(8,128)(2,1)S(1)}, bf16[384,512]{1,0:T(8,128)(2,1)}, u32[]{:S(2)}) copy-start(bf16[384,512]{1,0:T(8,128)(2,1)} %reshape.427) | copy-start | bytes 1179652
  446.3 54.1 %copy-start.41 = (f32[12,512]{1,0:T(8,128)}, f32[12,512]{1,0:T(8,128)S(1)}, u32[]{:S(2)}) copy-start(f32[12,512]{1,0:T(8,128)S(1)} %get-tuple-element.85) | copy-start | bytes 73732
  446.3 45.8 %copy-start.97 = (f32[12]{0:T(128)}, f32[12]{0:T(128)S(1)}, u32[]{:S(2)}) copy-start(f32[12]{0:T(128)S(1)} %add_rsqrt_fusion.5) | copy-start | bytes 148
  493.4 106.5 %copy-start.95 = (f32[231]{0:T(256)S(1)}, f32[231]{0:T(256)}, u32[]{:S(2)}) copy-start(f32[231]{0:T(256)} %copy-done.94) | copy-start | bytes 2776
  494.5 133.1 %copy-start.45 = (f32[384,12]{0,1:T(8,128)}, f32[384,12]{0,1:T(8,128)S(1)}, u32[]{:S(2)}) copy-start(f32[384,12]{0,1:T(8,128)S(1)} %get-tuple-element.89) | copy-start | bytes 55300
  494.7 132.9 %copy-start.27 = (bf16[384,512]{1,0:T(8,128)(2,1)S(1)}, bf16[384,512]{1,0:T(8,128)(2,1)}, u32[]{:S(2)}) copy-start(bf16[384,512]{1,0:T(8,128)(2,1)} %reshape.425) | copy-start | bytes 1179652
  578.1 14.0 collective-permute-start.10
  579.3 15.6 collective-permute-start.11
  582.0 5.1 collective-permute-start.15
  583.3 18.7 collective-permute-start.12
  585.2 21.1 collective-permute-start.13
  587.1 21.1 collective-permute-start.14
  592.1 18.0 collective-permute-start.8
  594.9 18.1 collective-permute-start.9
  602.0 44.1 %collective-permute-start = (f32[16,512]{1,0:T(8,128)}, f32[16,512]{1,0:T(8,128)}, u32[]{:S(2)}, u32[]{:S(2)}) collective-permute-start(f32[16,512]{1,0:T(8,128)} %get-tuple-element.58), channel_id=1, source_target_pairs={{0,1},{1,2},{2,3},{3,4},{4,5},{5,6},{6,7},{7,8},{8,9},{9,10},{10,1... | collective-permute-start | bytes 98312
  606.3 42.4 %collective-permute-start.1 = (f32[16,512]{1,0:T(8,128)}, f32[16,512]{1,0:T(8,128)}, u32[]{:S(2)}, u32[]{:S(2)}) collective-permute-start(f32[16,512]{1,0:T(8,128)} %get-tuple-element.58), channel_id=1, source_target_pairs={{0,2},{1,3},{2,4},{3,5},{4,6},{5,7},{6,8},{7,9},{8,10},{9,11},{10,... | collective-permute-start | bytes 98312
  608.2 44.0 %collective-permute-start.2 = (f32[16,512]{1,0:T(8,128)}, f32[16,512]{1,0:T(8,128)}, u32[]{:S(2)}, u32[]{:S(2)}) collective-permute-start(f32[16,512]{1,0:T(8,128)} %get-tuple-element.58), channel_id=1, source_target_pairs={{0,3},{1,4},{2,5},{3,6},{4,7},{5,8},{6,9},{7,10},{8,11},{9,12},{10... | collective-permute-start | bytes 98312
  610.1 42.1 %collective-permute-start.3 = (f32[16,512]{1,0:T(8,128)}, f32[16,512]{1,0:T(8,128)}, u32[]{:S(2)}, u32[]{:S(2)}) collective-permute-start(f32[16,512]{1,0:T(8,128)} %get-tuple-element.58), channel_id=1, source_target_pairs={{0,4},{1,5},{2,6},{3,7},{4,8},{5,9},{6,10},{7,11},{8,12},{9,13},{1... | collective-permute-start | bytes 98312
  613.0 31.7 %collective-permute-start.7 = (f32[12,512]{1,0:T(8,128)}, f32[12,512]{1,0:T(8,128)}, u32[]{:S(2)}, u32[]{:S(2)}) collective-permute-start(f32[12,512]{1,0:T(8,128)} %slice.139), channel_id=1, source_target_pairs={{0,8},{1,9},{2,10},{3,11},{4,12},{5,13},{6,14},{7,15},{8,16},{9,17... | collective-permute-start | bytes 73736
  644.7 7.5 collective-permute-start.4
  646.1 6.1 collective-permute-start.5
  648.7 3.5 collective-permute-start.6
  668.3 232.5 %reduce-scatter.42.cloned.1.call-start = ((), (), s32[]{:S(2)}) async-start(), calls=%async_computation.28 | async-start | bytes 1622016
  687.5 347.9 %reduce-scatter.44.cloned.1.call-start = ((), (), s32[]{:S(2)}) async-start(), calls=%async_computation.29 | async-start | bytes 270336
  697.0 472.0 %reduce-scatter.34.cloned.1.call-start = ((), (), s32[]{:S(2)}) async-start(), calls=%async_computation.24 | async-start | bytes 1081344 | tf_op jit(solution)/shard_map/reduce_scatter | solution.py:369
  699.4 569.1 %reduce-scatter.40.cloned.1.call-start = ((), (), s32[]{:S(2)}) async-start(), calls=%async_computation.27 | async-start | bytes 1622016 | tf_op jit(solution)/shard_map/reduce_scatter | solution.py:374
  701.8 671.5 %reduce-scatter.26.cloned.1.call-start = ((), (), s32[]{:S(2)}) async-start(), calls=%async_computation.20 | async-start | bytes 2433024 | tf_op jit(solution)/shard_map/reduce_scatter | solution.py:363
  715.2 764.6 %reduce-scatter.32.cloned.1.call-start = ((), (), s32[]{:S(2)}) async-start(), calls=%async_computation.23 | async-start | bytes 3244032 | tf_op jit(solution)/shard_map/reduce_scatter | solution.py:368
  718.8 903.7 %reduce-scatter.36.cloned.1.call-start = ((), (), s32[]{:S(2)}) async-start(), calls=%async_computation.25 | async-start | bytes 4325376 | tf_op jit(solution)/shard_map/reduce_scatter | solution.py:370
  723.1 1039.1 %reduce-scatter.38.cloned.1.call-start = ((), (), s32[]{:S(2)}) async-start(), calls=%async_computation.26 | async-start | bytes 4325376 | tf_op jit(solution)/shard_map/reduce_scatter | solution.py:371
  728.5 1154.8 %reduce-scatter.24.cloned.1.call-start = ((), (), s32[]{:S(2)}) async-start(), calls=%async_computation.19 | async-start | bytes 7299072 | tf_op jit(solution)/shard_map/reduce_scatter | solution.py:362
  729.2 79.7 %copy-start.75 = (f32[12,50]{1,0:T(8,128)}, f32[12,50]{1,0:T(8,128)S(1)}, u32[]{:S(2)}) copy-start(f32[12,50]{1,0:T(8,128)S(1)} %rsqrt.66) | copy-start | bytes 7204
  729.3 79.6 %copy-start.77 = (f32[12,50]{1,0:T(8,128)}, f32[12,50]{1,0:T(8,128)S(1)}, u32[]{:S(2)}) copy-start(f32[12,50]{1,0:T(8,128)S(1)} %div.105) | copy-start | bytes 7204
  781.6 1243.9 %reduce-scatter.28.cloned.1.call-start = ((), (), s32[]{:S(2)}) async-start(), calls=%async_computation.21 | async-start | bytes 9732096 | tf_op jit(solution)/shard_map/reduce_scatter | solution.py:364
  791.0 1375.5 %reduce-scatter.30.cloned.1.call-start = ((), (), s32[]{:S(2)}) async-start(), calls=%async_computation.22 | async-start | bytes 9732096 | tf_op jit(solution)/shard_map/reduce_scatter | solution.py:365
  809.0 47.5 %copy-start.116 = (f32[3,77]{1,0:T(4,128)S(1)}, f32[3,77]{1,0:T(4,128)}, u32[]{:S(2)}) copy-start(f32[3,77]{1,0:T(4,128)} %get-tuple-element.28) | copy-start | bytes 2776
  809.0 47.5 %copy-start.115 = (f32[3,77]{1,0:T(4,128)S(1)}, f32[3,77]{1,0:T(4,128)}, u32[]{:S(2)}) copy-start(f32[3,77]{1,0:T(4,128)} %get-tuple-element.29) | copy-start | bytes 2776
  809.0 47.5 %copy-start.80 = (f32[512]{0:T(512)S(1)}, f32[512]{0:T(512)}, u32[]{:S(2)}) copy-start(f32[512]{0:T(512)} %copy-done.79) | copy-start | bytes 6148
  816.8 43.2 %copy-start.76 = (f32[12,50]{1,0:T(8,128)S(1)}, f32[12,50]{1,0:T(8,128)}, u32[]{:S(2)}) copy-start(f32[12,50]{1,0:T(8,128)} %copy-done.75) | copy-start | bytes 7204
  (91 other events, 669.2 us)
Sparse Core Ops, SparseCore 0:
  10.9 57.9 all-gather.9
  71.7 55.3 all-gather.11
  130.0 56.2 all-gather.13
  189.1 60.9 all-gather.15
  252.8 53.0 all-gather.17
  308.7 62.8 all-gather.19
  374.5 62.4 all-gather.21
  668.4 133.1 reduce-scatter.45
  807.6 93.0 reduce-scatter.41
  902.9 132.4 reduce-scatter.43
  1038.2 130.7 reduce-scatter.33
  1175.5 92.9 reduce-scatter.39
  1275.2 98.0 reduce-scatter.25
  1379.2 100.5 reduce-scatter.31
  1482.5 140.0 reduce-scatter.35
  1625.2 136.9 reduce-scatter.37
  1768.3 114.9 reduce-scatter.23
  1890.6 134.8 reduce-scatter.27
  2032.0 134.4 reduce-scatter.29
where the time goes:
time: 2190 us; the launch traced here: 2170 us
  waiting for transfers between devices  1380 us (63%)
  blocking collectives  405 us (18%)
  matrix products  156 us (7%)
  local copies, waits for them, and re-layouts  147 us (7%)
  starting transfers between devices  39.6 us (2%)
    unnamed x38, waiting for transfers between devices  169 us
    reduce_scatter x1, waiting for transfers between devices, local(): lax.psum_scatter(txt_local[2], 'dp', scatter_dimension=1, tiled=True)  143 us
    reduce_scatter x1, waiting for transfers between devices, local(): lax.psum_scatter(img_local[2], 'dp', scatter_dimension=1, tiled=True)  142 us
    reduce_scatter x1, waiting for transfers between devices, local(): lax.psum_scatter(img_local[3], 'dp', scatter_dimension=1, tiled=True)  141 us
    reduce_scatter x1, waiting for transfers between devices, local(): lax.psum_scatter(txt_local[3], 'dp', scatter_dimension=1, tiled=True)  140 us
    reduce_scatter x1, waiting for transfers between devices, local(): lax.psum_scatter(txt_local[1], 'dp', scatter_dimension=1, tiled=True)  132 us
    reduce_scatter x1, waiting for transfers between devices, local(): lax.psum_scatter(img_local[0], 'dp', scatter_dimension=1, tiled=True)  121 us
    unnamed x2, blocking collectives  115 us
  transfers between devices with their start and end apart: 35, of which 13 were waited for; matrix products, arithmetic and copies ran while one was open for 13% of the time, Pallas kernels for 0%

commit v1 on v0

--- a/solution.py
+++ b/solution.py
@@ -1,6 +1,8 @@
 import jax
 import jax.numpy as jnp
 from jax import lax
+from jax.experimental import pallas as pl
+from jax.experimental.pallas import tpu as pltpu
 from jax.sharding import PartitionSpec as P
 
 HD = 64
@@ -199,7 +201,7 @@
     return tuple((stacked[layer_index] for stacked in stacks))
 
 
-def local(
+def local_plain(
     picture_patch_inputs,
     caption_packed_inputs,
     picture_attend_entry_weight,
@@ -394,6 +396,1032 @@
     )
 
 
+F32 = jnp.float32
+BF16 = jnp.bfloat16
+Z_PEERS = (8, 16, 24)
+PLANE_PEERS = (2, 4, 6)
+LINE_PEERS = (1, 8, 9, 16, 17, 24, 25)
+ALL_PEERS = (1, 2, 4, 6, 8, 9, 16, 17, 24, 25)
+PAD = 16
+N_SEMS = 300
+
+
+def fits(mesh):
+    return mesh.size == 32
+
+
+def dot(left, right):
+    return lax.dot_general(left, right, (((1,), (0,)), ((), ())), preferred_element_type=F32)
+
+
+def dot_nt(left, right):
+    return lax.dot_general(left, right, (((1,), (1,)), ((), ())), preferred_element_type=F32)
+
+
+def dot_tn(left, right):
+    return lax.dot_general(left, right, (((0,), (0,)), ((), ())), preferred_element_type=F32)
+
+
+def split_two(values):
+    high = values.astype(BF16)
+    return high, (values - high.astype(F32)).astype(BF16)
+
+
+def iota(shape, dim):
+    return lax.broadcasted_iota(jnp.int32, shape, dim)
+
+
+def expand_heads(rows):
+    lanes = iota(rows.shape, 1) // HD
+    heads = rows.shape[1] // HD
+    zero = jnp.zeros_like(rows)
+    return jnp.concatenate([jnp.where(lanes == head, rows, zero) for head in range(heads)], 0)
+
+
+def join_heads(stacked):
+    heads = stacked.shape[1] // HD
+    lanes = iota((PAD, stacked.shape[1]), 1) // HD
+    total = jnp.zeros((PAD, stacked.shape[1]), F32)
+    for head in range(heads):
+        total = jnp.where(lanes == head, stacked[PAD * head : PAD * (head + 1)], total)
+    return total
+
+
+def small_norm(hidden, gain, shift):
+    centred = hidden - jnp.mean(hidden, -1, keepdims=True)
+    inverse = lax.rsqrt(jnp.mean(centred * centred, -1, keepdims=True) + 1e-05)
+    normed = centred * inverse
+    return normed, inverse, normed * gain + shift
+
+
+def col_sum(values):
+    return jnp.sum(values, 0, keepdims=True)
+
+
+class Tower:
+    def __init__(self, width, tokens, rows, block, real_tokens, extra):
+        self.width = width
+        self.tokens = tokens
+        self.real_tokens = real_tokens
+        self.rows = rows
+        self.chip_rows = 2 * rows
+        self.block = block
+        self.group = 4 * block
+        self.heads = width // HD
+        self.queries = PAD * self.heads
+        self.extra = extra
+        self.packed = 2 * width + extra + 4 * self.group
+        self.row_pad = -(-rows // 16) * 16
+
+    def scratch(self):
+        d, n, r, g, b, cr = self.width, self.tokens, self.queries, self.group, self.block, self.chip_rows
+        v = pltpu.VMEM
+        out = dict(
+            pk=v((2, self.row_pad, self.packed), BF16),
+            pr=v((self.row_pad, self.packed), BF16),
+            w1=v((2, 16 * cr, d), BF16),
+            w2=v((2, 16 * cr, d), BF16),
+            mf=v((4, cr, g), BF16),
+            fa=v((4, 4, cr, g), BF16),
+            wp=v((4, b, d), BF16),
+            vecs=v((8, d), F32),
+            bias=v((8, g), F32),
+            xh=v((n, d), F32),
+            inv=v((n, 128), F32),
+            a=v((n, d), BF16),
+            p32=v((r, n), F32),
+            lh=v((2 * r + 2 * PAD, n), BF16),
+            rh=v((2 * r + 2 * PAD, d), BF16),
+            q=v((PAD, d), BF16),
+            ci=v((2, 4, PAD, d), BF16),
+            hpf=v((2, 4, PAD, d), F32),
+            hps=v((2, 4, PAD, d), BF16),
+            hr=v((7, PAD, d), BF16),
+            dcs=v((2, 4, PAD, d), BF16),
+            dcr=v((7, PAD, d), BF16),
+            u=v((8 * PAD, g), F32),
+            m=v((8 * PAD, g), BF16),
+            gpf=v((4, b, d), F32),
+            gpb=v((4, b, d), BF16),
+            gpr=v((3, b, d), BF16),
+            gff=v((4, 4, cr, g), F32),
+            gfb=v((4, 4, cr, g), BF16),
+            gfr=v((3, 4, cr, g), BF16),
+            gf2=v((4, cr, g), BF16),
+            gf3=v((4, cr, g), F32),
+            gf3r=v((4, cr, g), BF16),
+            gf4=v((4, self.rows, g), F32),
+            in1t=v((d, 256), BF16),
+            in1r=v((4, 4 * cr, 256), BF16),
+            in2t=v((d, r), BF16),
+            in2r=v((4, 4 * cr, r), BF16),
+            qg=v((4, PAD, d), BF16),
+            wg=v((4, PAD, d), BF16),
+            dog=v((4, PAD, d), BF16),
+            dqg=v((4, PAD, d), BF16),
+            r1f=v((4, cr, 2 * d + 2 * self.extra), F32),
+            r1b=v((4, cr, 2 * d + 2 * self.extra), BF16),
+            r1r=v((3, cr, 2 * d + 2 * self.extra), BF16),
+            r1s=v((cr, 2 * d + 2 * self.extra), F32),
+            r1p=v((self.rows, 2 * d + 2 * self.extra), F32),
+            r2f=v((4, cr, 2 * d), F32),
+            r2b=v((4, cr, 2 * d), BF16),
+            r2r=v((3, cr, 2 * d), BF16),
+            r2s=v((cr, 2 * d), F32),
+            r2p=v((self.rows, 2 * d), F32),
+            da=v((n, d), F32),
+            gp=v((n, d), F32),
+            g2=v((2, 4, PAD, d), F32),
+            dbs=v((8, g), F32),
+            dbr=v((3, 8, g), F32),
+        )
+        return out
+
+
+SHARED = dict(
+    vb=((2, 16, PAD, 128), BF16),
+    w3=((2, 768, 256), BF16),
+    eb=((2, 2, 16, PAD, 512), BF16),
+    sc=((2, 4, 2, PAD, 128), F32),
+    gtxt=((512, 512), F32),
+    gimg=((512, 512), F32),
+    drb=((2, 4, PAD, 512), BF16),
+    vz=((8, 1280), F32),
+    vzr=((3, 8, 1280), F32),
+    vp=((8, 1280), F32),
+    vpr=((3, 8, 1280), F32),
+    vc=((8, 1280), F32),
+    vcr=((8, 1280), F32),
+)
+INPUTS = (
+    "ix", "tx", "iqkv", "iout", "ifc", "iproj", "ivec", "ifcb", "tqkv", "tout", "tfc", "tproj", "tvec", "tfcb",
+    "map", "sharp", "counts", "match",
+)
+OUTPUTS = (
+    "loss", "dls", "dxi", "dxt", "diqkv", "diout", "difc", "diproj", "divec", "difcb", "dtqkv", "dtout", "dtfc",
+    "dtproj", "dtvec", "dtfcb", "dmap",
+)
+
+
+class Step:
+    def __init__(self, ti, tt, images, names, refs):
+        self.ref = dict(zip(names, refs, strict=True))
+        self.ti, self.tt, self.images = ti, tt, images
+        me = lax.axis_index("dp")
+        self.bits = [lax.rem(me // (1 << bit), 2) for bit in range(5)]
+        self.me = me
+        self.core = lax.rem(me, 2)
+        self.chip = me // 2
+        self.plane = lax.rem(me // 2, 4)
+        self.zed = me // 8
+        self.used = 0
+        self.copies = []
+
+    def at_peer(self, mask):
+        total = 0
+        for bit in range(5):
+            value = 1 - self.bits[bit] if mask >> bit & 1 else self.bits[bit]
+            total = total + value * (1 << bit)
+        return total
+
+    def send(self, src, dst, mask):
+        index = self.used
+        self.used += 1
+        copy = pltpu.make_async_remote_copy(
+            src_ref=src,
+            dst_ref=dst,
+            send_sem=self.ref["ssem"].at[index],
+            recv_sem=self.ref["rsem"].at[index],
+            device_id=(self.at_peer(mask),),
+            device_id_type=pl.DeviceIdType.MESH,
+        )
+        copy.start()
+        self.copies.append(copy)
+        return copy
+
+    def barrier(self):
+        semaphore = pltpu.get_barrier_semaphore()
+        for mask in ALL_PEERS:
+            pl.semaphore_signal(
+                semaphore, inc=1, device_id=(self.at_peer(mask),), device_id_type=pl.DeviceIdType.MESH
+            )
+        pl.semaphore_wait(semaphore, len(ALL_PEERS))
+
+    def gather_begin(self, slot, whole):
+        here = slot(self.chip)
+        to_z = [self.send(here, here, mask) for mask in Z_PEERS]
+        arriving = [self.send(here, here, mask) for mask in PLANE_PEERS]
+        return dict(slot=slot, whole=whole, to_z=to_z, arriving=arriving)
+
+    def gather_middle(self, state):
+        for copy, mask in zip(state["to_z"], Z_PEERS, strict=True):
+            copy.wait_recv()
+            there = state["slot"](self.at_peer(mask) // 2)
+            state["arriving"] += [self.send(there, there, peer) for peer in PLANE_PEERS]
+
+    def gather_end(self, state):
+        for copy in state["arriving"]:
+            copy.wait_recv()
+        state["last"] = self.send(state["whole"], state["whole"], 1)
+
+    def gather_done(self, state):
+        state["last"].wait_recv()
+
+    def line_gather(self, buffer):
+        here = buffer.at[self.core, self.zed]
+        return [self.send(here, here, mask) for mask in LINE_PEERS]
+
+    def line_scatter(self, parts, landing):
+        copies = []
+        for slot, mask in enumerate(LINE_PEERS):
+            peer = self.at_peer(mask)
+            copies.append(self.send(parts.at[lax.rem(peer, 2), peer // 8], landing.at[slot], mask))
+        return copies
+
+    def wait(self, copies):
+        for copy in copies:
+            copy.wait_recv()
+
+    def run(self):
+        ti, tt = self.ti, self.tt
+        self.pack(ti, "i", map_ref=self.ref["map"])
+        self.pack(tt, "t")
+        self.pack_vectors()
+        self.barrier()
+        self.pair = {
+            t: self.send(self.ref[t + "pk"].at[1 - self.core], self.ref[t + "pr"], 1) for t in ("i", "t")
+        }
+        vb = self.ref["vb"]
+        vectors = self.gather_begin(lambda chip: vb.at[self.core, chip], vb.at[self.core])
+        self.standardize(tt, "t", 0, tt.tokens)
+        chunk = {}
+        self.merge(ti, "i")
+        self.merge(tt, "t")
+        chunk["i1"] = self.begin_chunk(ti, "i", "w1")
+        chunk["t1"] = self.begin_chunk(tt, "t", "w1")
+        chunk["i2"] = self.begin_chunk(ti, "i", "w2")
+        chunk["t2"] = self.begin_chunk(tt, "t", "w2")
+        w3 = self.ref["w3"]
+        chunk["map"] = self.gather_begin(
+            lambda chip: w3.at[self.core, pl.ds(pl.multiple_of(chip * ti.chip_rows, 16), ti.chip_rows)],
+            w3.at[self.core],
+        )
+        widen = {t: self.widen_begin(tower, t) for t, tower in (("i", ti), ("t", tt))}
+        self.standardize(ti, "i", 0, ti.tokens)
+        self.gather_middle(vectors)
+        for name in ("i1", "t1", "i2", "t2", "map"):
+            self.gather_middle(chunk[name])
+        self.gather_end(vectors)
+        self.gather_done(vectors)
+        self.unpack_vectors()
+        self.queries(ti, "i")
+        self.queries(tt, "t")
+        self.gather_end(chunk["i1"])
+        self.gather_end(chunk["t1"])
+        for t, tower in (("i", ti), ("t", tt)):
+            self.widen_middle(tower, t, widen[t])
+        self.gather_done(chunk["i1"])
+        self.attend(ti, "i")
+        self.gather_end(chunk["i2"])
+        self.gather_done(chunk["t1"])
+        self.attend(tt, "t")
+        self.gather_end(chunk["t2"])
+        self.gather_done(chunk["i2"])
+        line = {}
+        line["i"] = self.mix(ti, "i")
+        self.gather_done(chunk["t2"])
+        line["t"] = self.mix(tt, "t")
+        self.gather_end(chunk["map"])
+        scattered = {}
+        for t, tower in (("i", ti), ("t", tt)):
+            self.wait(widen[t])
+            self.wait(line[t])
+            scattered[t] = self.feed(tower, t)
+        self.gather_done(chunk["map"])
+        for t, tower in (("i", ti), ("t", tt)):
+            self.wait(scattered[t])
+            self.embed(tower, t)
+        eb, sc = self.ref["eb"], self.ref["sc"]
+        rows = self.gather_begin(lambda chip: eb.at[:, self.core, chip], eb.at[:, self.core])
+        scales = self.line_gather(sc)
+        early = {t: self.early_operands(tower, t) for t, tower in (("i", ti), ("t", tt))}
+        self.gather_middle(rows)
+        self.gather_end(rows)
+        self.gather_done(rows)
+        self.wait(scales)
+        self.contrast()
+        scattered = {t: self.feed_back(tower, t) for t, tower in (("i", ti), ("t", tt))}
+        sent = {t: self.feed_weights(tower, t) for t, tower in (("i", ti), ("t", tt))}
+        middle = {}
+        for t, tower in (("i", ti), ("t", tt)):
+            self.wait(scattered[t])
+            middle[t] = self.attend_back(tower, t)
+        late = {t: self.attend_back_end(tower, t) for t, tower in (("i", ti), ("t", tt))}
+        for t, tower in (("i", ti), ("t", tt)):
+            self.input_gradient(tower, t)
+        first = self.vector_sum_begin()
+        for t, tower in (("i", ti), ("t", tt)):
+            self.feed_weights_middle(tower, t, sent[t])
+        for t, tower in (("i", ti), ("t", tt)):
+            self.round_one(tower, t, early[t], middle[t])
+        second = self.vector_sum_middle(first)
+        for t, tower in (("i", ti), ("t", tt)):
+            self.round_two(tower, t, late[t])
+        third = self.vector_sum_end(second)
+        for t, tower in (("i", ti), ("t", tt)):
+            self.feed_weights_end(tower, t, sent[t])
+            self.rounds_end(tower, t)
+        self.vector_sum_done(third)
+        for t, tower in (("i", ti), ("t", tt)):
+            self.rounds_done(tower, t)
+        for copy in self.copies:
+            copy.wait_send()
+
+    def pack(self, tower, t, map_ref=None):
+        pk, qkv, out, fc = (self.ref[t + name] for name in ("pk", "qkv", "out", "fc"))
+        d, b = tower.width, tower.block
+        pad = tower.row_pad - tower.rows
+
+        def padded(values):
+            values = values.astype(F32)
+            if pad:
+                values = jnp.concatenate([values, jnp.zeros((pad, values.shape[1]), F32)], 0)
+            return values.astype(BF16)
+
+        pk[0, :, 0:d] = padded(qkv[:, 0:d])
+        pk[1, :, 0:d] = padded(qkv[:, d : 2 * d])
+        pk[0, :, d : 2 * d] = padded(qkv[:, 2 * d : 3 * d])
+        pk[1, :, d : 2 * d] = padded(out[...])
+        if tower.extra:
+            for half in range(2):
+                cols = slice(half * tower.extra, (half + 1) * tower.extra)
+                pk[half, :, 2 * d : 2 * d + tower.extra] = padded(map_ref[:, cols])
+        base = 2 * d + tower.extra
+        values = padded(fc[...]).astype(F32)
+        for half in range(2):
+            for zed in range(4):
+                pieces = []
+                for plane in range(4):
+                    device = 8 * zed + 2 * plane + half
+                    pieces.append(values[:, b * device : b * (device + 1)])
+                start = base + zed * tower.group
+                pk[half, :, start : start + tower.group] = jnp.concatenate(pieces, 1).astype(BF16)
+
+    def pack_vectors(self):
+        ivec, tvec, ifcb, tfcb, match = (self.ref[n] for n in ("ivec", "tvec", "ifcb", "tfcb", "match"))
+        wi, wt = ivec.shape[1], tvec.shape[1]
+
+        def widen(values, at, rows):
+            values = values.astype(F32)
+            parts = [values, jnp.zeros((values.shape[0], 128 - at - values.shape[1]), F32)]
+            if at:
+                parts = [jnp.zeros((values.shape[0], at), F32)] + parts
+            return jnp.concatenate(parts, 1)
+
+        top = widen(ivec[...], 0, 8) + widen(tvec[...], 32, 8)
+        row = iota((8, 128), 0)
+        bottom = jnp.where(row == 0, widen(ifcb[...], 0, 1), 0.0)
+        bottom = bottom + jnp.where(row == 1, widen(tfcb[...], 0, 1), 0.0)
+        block = jnp.concatenate([top, bottom], 0)
+        row, lane = iota((PAD, 128), 0), iota((PAD, 128), 1)
+        for caption in range(self.images):
+            image = match[caption]
+            device = image // self.images
+            high = lax.rem(device, 2) * 16 + device // 2
+            low = image - device * self.images
+            block = jnp.where((row == caption) & (lane == 120), high.astype(F32), block)
+            block = jnp.where((row == caption) & (lane == 121), low.astype(F32), block)
+        self.ref["vb"][self.core, self.chip] = block.astype(BF16)
+
+    def unpack_vectors(self):
+        vb = self.ref["vb"]
+        for core in range(2):
+            for chip in range(16):
+                block = vb[core, chip].astype(F32)
+                device = 2 * chip + core
+                for t, tower, at in (("i", self.ti, 0), ("t", self.tt, 32)):
+                    rows = tower.rows
+                    self.ref[t + "vecs"][:, rows * device : rows * (device + 1)] = block[0:8, at : at + rows]
+        for plane in range(4):
+            block = vb[self.core, 4 * self.zed + plane].astype(F32)
+            for t, tower, row in (("i", self.ti, 8), ("t", self.tt, 9)):
+                b = tower.block
+                self.ref[t + "bias"][0:1, b * plane : b * (plane + 1)] = block[row : row + 1, 0:b]
+
+    def standardize(self, tower, t, start, stop):
+        x, xh, inv = (self.ref[t + name] for name in ("x", "xh", "inv"))
+        step = 32
+
+        def body(index, carry):
+            rows = pl.ds(pl.multiple_of(index * step, step), step)
+            hidden = x[rows, :].astype(F32)
+            centred = hidden - jnp.mean(hidden, -1, keepdims=True)
+            inverse = lax.rsqrt(jnp.mean(centred * centred, -1, keepdims=True) + 1e-05)
+            xh[rows, :] = centred * inverse
+            inv[rows, :] = jnp.broadcast_to(inverse, (step, 128))
+            return carry
+
+        lax.fori_loop(start // step, stop // step, body, 0)
+
+    def merge(self, tower, t):
+        self.pair[t].wait_recv()
+        pk, pr = self.ref[t + "pk"], self.ref[t + "pr"]
+        d, g = tower.width, tower.group
+        rows = pl.ds(pl.multiple_of(self.chip * tower.chip_rows, 16), tower.chip_rows)
+        first = self.core == 0
+
+        def merged(cols):
+            own = pk[self.core, :, cols].astype(F32)
+            got = pr[:, cols].astype(F32)
+            upper = jnp.where(first, own, got)[: tower.rows]
+            lower = jnp.where(first, got, own)[: tower.rows]
+            return jnp.concatenate([upper, lower], 0).astype(BF16)
+
+        self.ref[t + "w1"][self.core, rows, :] = merged(slice(0, d))
+        self.ref[t + "w2"][self.core, rows, :] = merged(slice(d, 2 * d))
+        base = 2 * d
+        if tower.extra:
+            self.ref["w3"][self.core, rows, :] = merged(slice(base, base + tower.extra))
+            base += tower.extra
+        for zed in range(4):
+            self.ref[t + "mf"][zed] = merged(slice(base + zed * g, base + (zed + 1) * g))
+
+    def begin_chunk(self, tower, t, name):
+        buffer = self.ref[t + name]
+        rows = tower.chip_rows
+        return self.gather_begin(
+            lambda chip: buffer.at[self.core, pl.ds(pl.multiple_of(chip * rows, 16), rows)],
+            buffer.at[self.core],
+        )
+
+    def widen_begin(self, tower, t):
+        mf, fa = self.ref[t + "mf"], self.ref[t + "fa"]
+        copies = []
+        for mask in Z_PEERS:
+            copies.append(self.send(mf.at[self.at_peer(mask) // 8], fa.at[self.zed, self.plane], mask))
+        fa[self.zed, self.plane] = mf[self.zed]
+        return copies
+
+    def widen_middle(self, tower, t, copies):
+        fa, wp, proj = self.ref[t + "fa"], self.ref[t + "wp"], self.ref[t + "proj"]
+        self.wait(copies)
+        copies.clear()
+        for mask in PLANE_PEERS:
+            part = fa.at[:, self.plane]
+            copies.append(self.send(part, part, mask))
+        for mask in PLANE_PEERS:
+            copies.append(self.send(proj, wp.at[self.plane], mask))
+        wp[self.plane] = proj[...]
+
+    def queries(self, tower, t):
+        a, xh, vec = self.ref[t + "a"], self.ref[t + "xh"], self.ref[t + "vecs"]
+        step = 32
+
+        def body(index, carry):
+            rows = pl.ds(pl.multiple_of(index * step, step), step)
+            a[rows, :] = (xh[rows, :] * vec[0:1, :] + vec[1:2, :]).astype(BF16)
+            return carry
+
+        lax.fori_loop(0, tower.tokens // step, body, 0)
+        n = tower.tokens
+        row, token = iota((PAD, n), 0), iota((PAD, n), 1)
+        if t == "i":
+            real = row < self.images
+            at = jnp.where(real, row * TOK_I, -1)
+            low, high = jnp.where(real, row * TOK_I, -1), jnp.where(real, (row + 1) * TOK_I, -1)
+        else:
+            counts = self.ref["counts"]
+            column = iota((PAD, 1), 0)
+            low, high = jnp.full((PAD, 1), -1, jnp.int32), jnp.full((PAD, 1), -1, jnp.int32)
+            for line in range(counts.shape[0]):
+                end = line * TOK_T
+                for member in range(CAP_ROW):
+                    begin, end = end, end + counts[line, member]
+                    chosen = column == line * CAP_ROW + member
+                    low, high = jnp.where(chosen, begin, low), jnp.where(chosen, end, high)
+            at = jnp.where(high > 0, high - 1, -1)
+        chosen = (token == at).astype(F32).astype(BF16)
+        lh, r = self.ref[t + "lh"], tower.queries
+        lh[2 * r : 2 * r + PAD, :] = chosen
+        lh[2 * r + PAD : 2 * r + 2 * PAD, :] = chosen
+        seen = ((token >= low) & (token < high)).astype(F32)
+        self.ref[t + "seen"] = seen
+        self.ref[t + "x0"] = dot(chosen, self.ref[t + "x"][...])
+        self.ref[t + "a0"] = dot(chosen, a[...]).astype(BF16)
+
+    def attend(self, tower, t):
+        w1, vec, a = self.ref[t + "w1"], self.ref[t + "vecs"], self.ref[t + "a"]
+        p32, lh, rh = self.ref[t + "p32"], self.ref[t + "lh"], self.ref[t + "rh"]
+        r = tower.queries
+        q = (dot(self.ref[t + "a0"], w1[0]) + vec[2:3, :]).astype(BF16)
+        self.ref[t + "q"][...] = q
+        qt = dot_nt(expand_heads(q), w1[1]).astype(BF16)
+        rh[0:r, :] = qt
+        scores = dot_nt(qt, a[...]) * 0.125
+        seen = jnp.concatenate([self.ref[t + "seen"]] * tower.heads, 0) > 0.5
+        scores = jnp.where(seen, scores, -1000000000.0)
+        top = jnp.max(scores, -1, keepdims=True)
+        raw = jnp.where(seen, jnp.exp(scores - top), 0.0)
+        total = jnp.sum(raw, -1, keepdims=True)
+        probs = raw / jnp.where(total > 0.0, total, 1.0)
+        p32[...] = probs
+        low = probs.astype(BF16)
+        lh[r : 2 * r, :] = low
+        self.ref[t + "pa"] = dot(low, a[...])
+
+    def mix(self, tower, t):
+        w2, vec, ci = self.ref[t + "w2"], self.ref[t + "vecs"], self.ref[t + "ci"]
+        context = (join_heads(dot(self.ref[t + "pa"].astype(BF16), w2[0])) + vec[3:4, :]).astype(BF16)
+        self.ref[t + "o"] = context
+        middle = self.ref[t + "x0"] + (dot(context, w2[1]) + vec[4:5, :])
+        normed, inverse, second = small_norm(middle, vec[5:6, :], vec[6:7, :])
+        self.ref[t + "h1"], self.ref[t + "xh2"], self.ref[t + "inv2"] = middle, normed, inverse
+        ci[self.core, self.zed] = second.astype(BF16)
+        return self.line_gather(ci)
+
+    def feed(self, tower, t):
+        ci, fa, wp, bias = (self.ref[t + name] for name in ("ci", "fa", "wp", "bias"))
+        hpf, hps = self.ref[t + "hpf"], self.ref[t + "hps"]
+        d, g = tower.width, tower.group
+        c = ci[...].reshape(8 * PAD, d)
+        up = dot(c, fa[...].reshape(d, g)) + bias[0:1, :]
+        active = (up * jax.nn.sigmoid(1.702 * up)).astype(BF16)
+        self.ref[t + "u"][...] = up
+        self.ref[t + "m"][...] = active
+        part = dot(active, wp[...].reshape(g, d)).reshape(2, 4, PAD, d)
+        hpf[...] = part
+        hps[...] = part.astype(BF16)
+        return self.line_scatter(hps, self.ref[t + "hr"])
+
+    def line_total(self, own, landing):
+        total = own
+        for slot in range(len(LINE_PEERS)):
+            total = total + landing[slot].astype(F32)
+        return total
+
+    def embed(self, tower, t):
+        vec = self.ref[t + "vecs"]
+        total = self.line_total(self.ref[t + "hpf"][self.core, self.zed], self.ref[t + "hr"])
+        hidden = self.ref[t + "h1"] + (total + vec[7:8, :])
+        which = 0 if t == "i" else 1
+        if t == "i":
+            pooled = hidden.astype(BF16)
+            self.ref["pooled"] = pooled
+            w3 = self.ref["w3"]
+            raw = jnp.concatenate([dot(pooled, w3[0]), dot(pooled, w3[1])], 1)
+        else:
+            raw = hidden
+        scale = lax.rsqrt(jnp.sum(raw * raw, -1, keepdims=True) + 1e-06)
+        self.ref["eb"][which, self.core, self.chip] = (raw * scale).astype(BF16)
+        self.ref["sc"][self.core, self.zed, which] = jnp.broadcast_to(scale, (PAD, 128))
+
+    def to_z_line(self, block, landing):
+        rows = landing.shape[1]
+        copies = []
+        for mask in Z_PEERS:
+            start = pl.multiple_of(self.at_peer(mask) // 8 * rows, 16)
+            copies.append(self.send(block.at[pl.ds(start, rows)], landing.at[self.zed], mask))
+        landing[self.zed] = block[pl.ds(pl.multiple_of(self.zed * rows, 16), rows), :]
+        return copies
+
+    def share_z_line(self, buffer, values):
+        buffer[self.zed] = values
+        here = buffer.at[self.zed]
+        return [self.send(here, here, mask) for mask in Z_PEERS]
+
+    def early_operands(self, tower, t):
+        d, r = tower.width, tower.queries
+        parts = [self.ref[t + "pa"], self.ref[t + "o"].astype(F32), self.ref[t + "a0"].astype(F32)]
+        if t == "i":
+            parts.append(self.ref["pooled"].astype(F32))
+        rest = 256 - r - PAD * (len(parts) - 1)
+        parts.append(jnp.zeros((rest, d), F32))
+        self.ref[t + "in1t"][...] = jnp.concatenate(parts, 0).T.astype(BF16)
+        copies = self.to_z_line(self.ref[t + "in1t"], self.ref[t + "in1r"])
+        return copies + self.share_z_line(self.ref[t + "qg"], self.ref[t + "q"][...])
+
+    def contrast(self):
+        eb, vb, sc = self.ref["eb"], self.ref["vb"], self.ref["sc"]
+        gtxt, gimg = self.ref["gtxt"], self.ref["gimg"]
+        total = self.images * 32
+        e_img, e_txt = eb[0].reshape(512, 512), eb[1].reshape(512, 512)
+        sharp = jnp.exp(jnp.full((8, 128), self.ref["sharp"][0], F32))[0:1, 0:1]
+        logits = sharp * dot_nt(e_txt, e_img)
+        marks = vb[...].reshape(512, 128).astype(F32)
+        target = marks[:, 120:121] * float(PAD) + marks[:, 121:122]
+        row, col = iota((512, 512), 0), iota((512, 512), 1)
+        real_row, real_col = lax.rem(row, PAD) < self.images, lax.rem(col, PAD) < self.images
+        real = real_row & real_col
+        hit = real & (col.astype(F32) == target)
+        powers = jnp.where(real, jnp.exp(logits), 0.0)
+        row_sum, col_sums = jnp.sum(powers, 1, keepdims=True), col_sum(powers)
+        real_line = lax.rem(iota((512, 1), 0), PAD) < self.images
+        real_lane = lax.rem(iota((1, 512), 1), PAD) < self.images
+        row_sum, col_sums = jnp.where(real_line, row_sum, 1.0), jnp.where(real_lane, col_sums, 1.0)
+        grad = powers * ((1.0 / row_sum + 1.0 / col_sums) * (0.5 / total))
+        grad = grad - jnp.where(hit, 1.0 / total, 0.0)
+        safe = jnp.where(real, logits, 0.0)
+        logs = jnp.sum(jnp.log(row_sum), 0, keepdims=True) + jnp.sum(jnp.log(col_sums), 1, keepdims=True)
+
+        def whole(values):
+            return jnp.sum(jnp.sum(values, 1, keepdims=True), 0, keepdims=True)
+
+        self.ref["loss"][...] = logs * (0.5 / total) - whole(jnp.where(hit, safe, 0.0)) * (1.0 / total)
+        self.ref["dls"][...] = whole(grad * safe)
+        gtxt[...] = grad
+        gimg[...] = grad.T
+        for which, t, rows, others in ((0, "i", gimg, e_txt), (1, "t", gtxt, e_img)):
+            parts, own, scales = [], [], []
+            for core in range(2):
+                for zed in range(4):
+                    chip = 4 * zed + self.plane
+                    start = pl.multiple_of((core * 16 + chip) * PAD, PAD)
+                    parts.append(rows[pl.ds(start, PAD), :])
+                    own.append(eb[which, core, chip].astype(F32))
+                    scales.append(sc[core, zed, which])
+            part, unit = jnp.concatenate(parts, 0), jnp.concatenate(own, 0)
+            scale = jnp.concatenate(scales, 0)[:, 0:1]
+            high, low = split_two(part)
+            d_unit = sharp * (dot(high, others) + dot(low, others))
+            d_raw = scale * (d_unit - unit * jnp.sum(d_unit * unit, -1, keepdims=True))
+            if t == "i":
+                w3 = self.ref["w3"]
+                rounded = d_raw.astype(BF16)
+                self.ref["drb"][...] = rounded.reshape(2, 4, PAD, 512)
+                d_raw = dot_nt(rounded[:, 0:256], w3[0]) + dot_nt(rounded[:, 256:512], w3[1])
+            self.ref[t + "g2"][...] = d_raw.reshape(2, 4, PAD, d_raw.shape[1])
+
+    def feed_back(self, tower, t):
+        d, g = tower.width, tower.group
+        fa, wp, u, dcs, hpf = (self.ref[t + name] for name in ("fa", "wp", "u", "dcs", "hpf"))
+        branch = self.ref[t + "g2"][...].reshape(8 * PAD, d).astype(BF16)
+        up = u[...]
+        gate = jax.nn.sigmoid(1.702 * up)
+        d_active = dot_nt(branch, wp[...].reshape(g, d))
+        d_up = (d_active * (gate + 1.702 * up * gate * (1.0 - gate))).astype(BF16)
+        part = dot_nt(d_up, fa[...].reshape(d, g)).reshape(2, 4, PAD, d)
+        hpf[...] = part
+        dcs[...] = part.astype(BF16)
+        copies = self.line_scatter(dcs, self.ref[t + "dcr"])
+        self.ref[t + "du"], self.ref[t + "y"] = d_up, branch
+        return copies
+
+    def feed_weights(self, tower, t):
+        d, g, b, cr = tower.width, tower.group, tower.block, tower.chip_rows
+        m, ci = self.ref[t + "m"], self.ref[t + "ci"]
+        gpf, gpb, gpr = (self.ref[t + name] for name in ("gpf", "gpb", "gpr"))
+        gff, gfb, gfr = (self.ref[t + name] for name in ("gff", "gfb", "gfr"))
+        dbs, dbr = self.ref[t + "dbs"], self.ref[t + "dbr"]
+        d_up, branch = self.ref[t + "du"], self.ref[t + "y"]
+        grad = dot_tn(ci[...].reshape(8 * PAD, d), d_up).reshape(4, 4, cr, g)
+        gff[...] = grad
+        gfb[...] = grad.astype(BF16)
+        wide = []
+        for slot, mask in enumerate(PLANE_PEERS):
+            wide.append(self.send(gfb.at[:, lax.rem(self.at_peer(mask) // 2, 4)], gfr.at[slot], mask))
+        grad = dot_tn(m[...], branch).reshape(4, b, d)
+        gpf[...] = grad
+        gpb[...] = grad.astype(BF16)
+        dbs[...] = jnp.broadcast_to(col_sum(d_up.astype(F32)), (8, g))
+        narrow = []
+        for slot, mask in enumerate(PLANE_PEERS):
+            narrow.append(self.send(gpb.at[lax.rem(self.at_peer(mask) // 2, 4)], gpr.at[slot], mask))
+            narrow.append(self.send(dbs, dbr.at[slot], mask))
+        return dict(wide=wide, narrow=narrow)
+
+    def feed_weights_middle(self, tower, t, sent):
+        b = tower.block
+        gpf, gpr = self.ref[t + "gpf"], self.ref[t + "gpr"]
+        gff, gfr, gf2, gf3r = (self.ref[t + name] for name in ("gff", "gfr", "gf2", "gf3r"))
+        self.wait(sent["wide"])
+        total = gff[:, self.plane]
+        for slot in range(3):
+            total = total + gfr[slot].astype(F32)
+        gf2[...] = total.astype(BF16)
+        self.ref[t + "gf3"][...] = total
+        sent["line"] = []
+        for mask in Z_PEERS:
+            sent["line"].append(self.send(gf2.at[self.at_peer(mask) // 8], gf3r.at[self.zed], mask))
+        self.wait(sent["narrow"])
+        total = gpf[self.plane]
+        for slot in range(3):
+            total = total + gpr[slot].astype(F32)
+        self.ref["d" + t + "proj"][...] = total
+        bias = self.ref[t + "dbs"][0:1, :]
+        for slot in range(3):
+            bias = bias + self.ref[t + "dbr"][slot, 0:1, :]
+        mine = jnp.zeros((1, b), F32)
+        for plane in range(4):
+            mine = jnp.where(self.plane == plane, bias[:, b * plane : b * (plane + 1)], mine)
+        self.ref["d" + t + "fcb"][...] = mine
+
+    def feed_weights_end(self, tower, t, sent):
+        gf3, gf3r, gf4 = (self.ref[t + name] for name in ("gf3", "gf3r", "gf4"))
+        self.wait(sent["line"])
+        own = gf3[self.zed]
+        for zed in range(4):
+            gf3[zed] = jnp.where(self.zed == zed, own, gf3r[zed].astype(F32))
+        rows = tower.rows
+        start = pl.multiple_of((1 - self.core) * rows, 8)
+        sent["last"] = self.send(gf3.at[:, pl.ds(start, rows)], gf4, 1)
+        self.ref[t + "fc_last"] = sent["last"]
+
+    def attend_back(self, tower, t):
+        vec, w2 = self.ref[t + "vecs"], self.ref[t + "w2"]
+        g2 = self.ref[t + "g2"][self.core, self.zed]
+        total = self.line_total(self.ref[t + "hpf"][self.core, self.zed], self.ref[t + "dcr"])
+        normed, inverse = self.ref[t + "xh2"], self.ref[t + "inv2"]
+        scaled = total * vec[5:6, :]
+        inner = (
+            scaled
+            - jnp.mean(scaled, -1, keepdims=True)
+            - normed * jnp.mean(scaled * normed, -1, keepdims=True)
+        )
+        g1 = g2 + inverse * inner
+        branch = g1.astype(BF16)
+        d_context = dot_nt(branch, w2[1]).astype(BF16)
+        self.ref[t + "g1"], self.ref[t + "do"] = g1, d_context
+        self.ref[t + "sums"] = dict(
+            dg2=col_sum(total * normed),
+            db2=col_sum(total),
+            dbo=col_sum(branch.astype(F32)),
+            dbp=col_sum(g2.astype(BF16).astype(F32)),
+            dbv=col_sum(d_context.astype(F32)),
+        )
+        copies = self.share_z_line(self.ref[t + "wg"], branch)
+        return copies + self.share_z_line(self.ref[t + "dog"], d_context)
+
+    def attend_back_end(self, tower, t):
+        r = tower.queries
+        w1, w2, a = self.ref[t + "w1"], self.ref[t + "w2"], self.ref[t + "a"]
+        p32, lh, rh = self.ref[t + "p32"], self.ref[t + "lh"], self.ref[t + "rh"]
+        dvt = dot_nt(expand_heads(self.ref[t + "do"]), w2[0]).astype(BF16)
+        rh[r : 2 * r, :] = dvt
+        d_probs = dot_nt(dvt, a[...])
+        probs = p32[...]
+        weighted = probs * d_probs
+        d_scores = (weighted - probs * jnp.sum(weighted, -1, keepdims=True)).astype(BF16)
+        d_scores = (d_scores.astype(F32) * 0.125).astype(BF16)
+        lh[0:r, :] = d_scores
+        moved = dot(d_scores, a[...])
+        self.ref[t + "in2t"][...] = moved.T.astype(BF16)
+        copies = self.to_z_line(self.ref[t + "in2t"], self.ref[t + "in2r"])
+        d_query = join_heads(dot(moved.astype(BF16), w1[1])).astype(BF16)
+        copies += self.share_z_line(self.ref[t + "dqg"], d_query)
+        self.ref[t + "sums"]["dbq"] = col_sum(d_query.astype(F32))
+        high, low = split_two(dot_nt(d_query, w1[0]))
+        rh[2 * r : 2 * r + PAD, :] = high
+        rh[2 * r + PAD : 2 * r + 2 * PAD, :] = low
+        return copies
+
+    def input_gradient(self, tower, t):
+        r, d = tower.queries, tower.width
+        lh, rh, da, gp, xh, inv, vec = (
+            self.ref[t + name] for name in ("lh", "rh", "da", "gp", "xh", "inv", "vecs")
+        )
+        out = self.ref["dx" + t]
+        da[...] = dot_tn(lh[...], rh[...])
+        high, low = split_two(self.ref[t + "g1"])
+        gp[...] = dot_tn(lh[2 * r : 2 * r + 2 * PAD, :], jnp.concatenate([high, low], 0))
+        step = 32
+
+        def body(index, carry):
+            rows = pl.ds(pl.multiple_of(index * step, step), step)
+            z, normed = da[rows, :], xh[rows, :]
+            scaled = z * vec[0:1, :]
+            inner = (
+                scaled
+                - jnp.mean(scaled, -1, keepdims=True)
+                - normed * jnp.mean(scaled * normed, -1, keepdims=True)
+            )
+            out[rows, :] = inv[rows, 0:1] * inner + gp[rows, :]
+            return (
+                carry[0] + jnp.sum((z * normed).reshape(step // 8, 8, d), 0),
+                carry[1] + jnp.sum(z.reshape(step // 8, 8, d), 0),
+            )
+
+        zero = jnp.zeros((8, d), F32)
+        gain, shift = lax.fori_loop(0, tower.tokens // step, body, (zero, zero))
+        sums = self.ref[t + "sums"]
+        rows = [col_sum(gain), col_sum(shift)]
+        rows += [sums[name] for name in ("dbq", "dbv", "dbo", "dg2", "db2", "dbp")]
+        self.ref[t + "rows"] = jnp.concatenate(rows, 0)
+
+    def vector_sum_begin(self):
+        vz, vzr = self.ref["vz"], self.ref["vzr"]
+        vz[...] = jnp.concatenate([self.ref["irows"], self.ref["trows"]], 1)
+        return [self.send(vz, vzr.at[slot], mask) for slot, mask in enumerate(Z_PEERS)]
+
+    def vector_sum_middle(self, copies):
+        self.wait(copies)
+        vz, vzr, vp, vpr = (self.ref[name] for name in ("vz", "vzr", "vp", "vpr"))
+        vp[...] = vz[...] + vzr[0] + vzr[1] + vzr[2]
+        return [self.send(vp, vpr.at[slot], mask) for slot, mask in enumerate(PLANE_PEERS)]
+
+    def vector_sum_end(self, copies):
+        self.wait(copies)
+        vp, vpr, vc, vcr = (self.ref[name] for name in ("vp", "vpr", "vc", "vcr"))
+        vc[...] = vp[...] + vpr[0] + vpr[1] + vpr[2]
+        return [self.send(vc, vcr, 1)]
+
+    def vector_sum_done(self, copies):
+        self.wait(copies)
+        total = self.ref["vc"][...] + self.ref["vcr"][...]
+        at = 0
+        for t, tower in (("i", self.ti), ("t", self.tt)):
+            d, rows = tower.width, tower.rows
+            values = total[:, at : at + d]
+            at += d
+            high, rest = split_two(values)
+            rest_high, rest_low = split_two(values - high.astype(F32))
+            pick = iota((d, 128), 0) == iota((d, 128), 1) + self.me * rows
+            pick = pick.astype(F32).astype(BF16)
+            picked = dot(high, pick) + dot(rest_high, pick) + dot(rest_low, pick)
+            self.ref["d" + t + "vec"][...] = picked[:, 0:rows]
+
+    def place(self, rows, at, tower):
+        parts = []
+        if at:
+            parts.append(jnp.zeros((at, rows.shape[1]), BF16))
+        parts.append(rows)
+        if 256 - at - rows.shape[0]:
+            parts.append(jnp.zeros((256 - at - rows.shape[0], rows.shape[1]), BF16))
+        return jnp.concatenate(parts, 0)
+
+    def in_plane(self, tower, t, name, grad):
+        f, b, landing = (self.ref[t + name + suffix] for suffix in ("f", "b", "r"))
+        grad = grad.reshape(4, tower.chip_rows, grad.shape[1])
+        f[...] = grad
+        b[...] = grad.astype(BF16)
+        copies = []
+        for slot, mask in enumerate(PLANE_PEERS):
+            copies.append(self.send(b.at[lax.rem(self.at_peer(mask) // 2, 4)], landing.at[slot], mask))
+        self.ref[t + name + "copies"] = copies
+
+    def round_one(self, tower, t, early, middle):
+        r = tower.queries
+        in1r, dog, wg, drb = self.ref[t + "in1r"], self.ref[t + "dog"], self.ref[t + "wg"], self.ref["drb"]
+        self.wait(early)
+        self.wait(middle)
+        value = out = proj = 0.0
+        for zed in range(4):
+            operand = in1r[zed]
+            value = value + dot(operand, self.place(expand_heads(dog[zed]), 0, tower))
+            out = out + dot(operand, self.place(wg[zed], r, tower))
+            if tower.extra:
+                proj = proj + dot(operand, self.place(drb[self.core, zed], r + 2 * PAD, tower))
+        parts = [value, out] + ([proj] if tower.extra else [])
+        self.in_plane(tower, t, "r1", jnp.concatenate(parts, 1))
+
+    def round_two(self, tower, t, late):
+        r = tower.queries
+        in1r, in2r, qg, dqg = (self.ref[t + name] for name in ("in1r", "in2r", "qg", "dqg"))
+        self.wait(late)
+        query = key = 0.0
+        for zed in range(4):
+            query = query + dot(in1r[zed], self.place(dqg[zed], r + PAD, tower))
+            key = key + dot(in2r[zed], expand_heads(qg[zed]))
+        self.in_plane(tower, t, "r2", jnp.concatenate([query, key], 1))
+
+    def rounds_end(self, tower, t):
+        rows = tower.rows
+        for name in ("r1", "r2"):
+            f, landing, total, last = (self.ref[t + name + suffix] for suffix in ("f", "r", "s", "p"))
+            self.wait(self.ref[t + name + "copies"])
+            values = f[self.plane]
+            for slot in range(3):
+                values = values + landing[slot].astype(F32)
+            total[...] = values
+            start = pl.multiple_of((1 - self.core) * rows, 8)
+            self.ref[t + name + "last"] = self.send(total.at[pl.ds(start, rows)], last, 1)
+
+    def rounds_done(self, tower, t):
+        rows, d, b, g = tower.rows, tower.width, tower.block, tower.group
+        start = pl.multiple_of(self.core * rows, 8)
+        done = {}
+        for name in ("r1", "r2"):
+            self.ref[t + name + "last"].wait_recv()
+            done[name] = self.ref[t + name + "s"][pl.ds(start, rows), :] + self.ref[t + name + "p"][...]
+        qkv = self.ref["d" + t + "qkv"]
+        qkv[:, 0 : 2 * d] = done["r2"]
+        qkv[:, 2 * d : 3 * d] = done["r1"][:, 0:d]
+        self.ref["d" + t + "out"][...] = done["r1"][:, d : 2 * d]
+        if tower.extra:
+            self.ref["dmap"][...] = done["r1"][:, 2 * d :]
+        self.ref[t + "fc_last"].wait_recv()
+        gf3, gf4, out = self.ref[t + "gf3"], self.ref[t + "gf4"], self.ref["d" + t + "fc"]
+        for zed in range(4):
+            own, got = gf3[zed, pl.ds(start, rows), :], gf4[zed]
+            for half in range(2):
+                values = jnp.where(self.core == half, own, got)
+                for plane in range(4):
+                    device = 8 * zed + 2 * plane + half
+                    out[:, b * device : b * (device + 1)] = values[:, b * plane : b * (plane + 1)]
+
+
+def local_fused(
+    picture_patch_inputs,
+    caption_packed_inputs,
+    picture_attend_entry_weight,
+    picture_attend_exit_weight,
+    picture_widening_weight,
+    picture_narrowing_weight,
+    picture_affine_entries,
+    picture_widening_offset,
+    caption_attend_entry_weight,
+    caption_attend_exit_weight,
+    caption_widening_weight,
+    caption_narrowing_weight,
+    caption_affine_entries,
+    caption_widening_offset,
+    picture_feature_mapping,
+    sharpness_exponent,
+    caption_token_counts,
+    matching_picture_index,
+):
+    n_img, d_img = picture_patch_inputs.shape
+    n_txt, d_txt = caption_packed_inputs.shape
+    pad_img, pad_txt = -(-n_img // 128) * 128, -(-n_txt // 128) * 128
+    ti = Tower(
+        d_img, pad_img, picture_attend_entry_weight.shape[1], picture_widening_offset.shape[1], n_img,
+        picture_feature_mapping.shape[1] // 2,
+    )
+    tt = Tower(d_txt, pad_txt, caption_attend_entry_weight.shape[1], caption_widening_offset.shape[1], n_txt, 0)
+    args = (
+        jnp.pad(picture_patch_inputs, ((0, pad_img - n_img), (0, 0))),
+        jnp.pad(caption_packed_inputs, ((0, pad_txt - n_txt), (0, 0))),
+        picture_attend_entry_weight[0],
+        picture_attend_exit_weight[0],
+        picture_widening_weight[0],
+        picture_narrowing_weight[0],
+        picture_affine_entries[0],
+        picture_widening_offset,
+        caption_attend_entry_weight[0],
+        caption_attend_exit_weight[0],
+        caption_widening_weight[0],
+        caption_narrowing_weight[0],
+        caption_affine_entries[0],
+        caption_widening_offset,
+        picture_feature_mapping,
+        sharpness_exponent.reshape(1),
+        caption_token_counts,
+        matching_picture_index,
+    )
+    names, shapes = [], []
+    for t, tower in (("i", ti), ("t", tt)):
+        for name, shape in tower.scratch().items():
+            names.append(t + name)
+            shapes.append(shape)
+    for name, (shape, kind) in SHARED.items():
+        names.append(name)
+        shapes.append(pltpu.VMEM(shape, kind))
+    names += ["ssem", "rsem"]
+    shapes += [pltpu.SemaphoreType.DMA((N_SEMS,)), pltpu.SemaphoreType.DMA((N_SEMS,))]
+    images = n_img // TOK_I
+
+    def kernel(*refs):
+        Step(ti, tt, images, list(INPUTS) + list(OUTPUTS) + names, refs).run()
+
+    def out(*shape):
+        return jax.ShapeDtypeStruct(shape, F32)
+
+    scalars = ("sharp", "counts", "match")
+    results = pl.pallas_call(
+        kernel,
+        out_shape=(
+            out(1, 1), out(1, 1), out(pad_img, d_img), out(pad_txt, d_txt),
+            out(ti.rows, 3 * d_img), out(ti.rows, d_img), out(ti.rows, 32 * ti.block), out(ti.block, d_img),
+            out(8, ti.rows), out(1, ti.block),
+            out(tt.rows, 3 * d_txt), out(tt.rows, d_txt), out(tt.rows, 32 * tt.block), out(tt.block, d_txt),
+            out(8, tt.rows), out(1, tt.block), out(ti.rows, 2 * ti.extra),
+        ),
+        in_specs=[
+            pl.BlockSpec(memory_space=pltpu.SMEM if name in scalars else pltpu.VMEM) for name in INPUTS
+        ],
+        out_specs=tuple(pl.BlockSpec(memory_space=pltpu.VMEM) for _ in OUTPUTS),
+        scratch_shapes=shapes,
+        compiler_params=pltpu.CompilerParams(
+            collective_id=0, has_side_effects=True, vmem_limit_bytes=60 * 2**20
+        ),
+        name="contrastive_step",
+    )(*args)
+    got = dict(zip(OUTPUTS, results, strict=True))
+    stacked = ("iqkv", "iout", "ifc", "iproj", "ivec", "tqkv", "tout", "tfc", "tproj", "tvec")
+    final = []
+    for name in OUTPUTS:
+        value = got[name]
+        if name in ("loss", "dls"):
+            value = value.reshape(())
+        elif name == "dxi":
+            value = value[:n_img]
+        elif name == "dxt":
+            value = value[:n_txt]
+        elif name[1:] in stacked:
+            value = value[None]
+        final.append(value)
+    return tuple(final)
+
+
 def solution(mesh):
     placed = (
         P("dp", None),
@@ -416,7 +1444,7 @@
         P("dp"),
     )
     return jax.shard_map(
-        local,
+        local_fused if fits(mesh) else local_plain,
         mesh=mesh,
         in_specs=placed,
         out_specs=(

time: 2190 us -> 179 us (0.08)
  waiting for transfers between devices: 1380 us -> 0 us
  blocking collectives: 405 us -> 0 us
  Pallas kernels: 0 us -> 157 us
  matrix products: 156 us -> 0 us
  local copies, waits for them, and re-layouts: 147 us -> 15.8 us
  starting transfers between devices: 39.6 us -> 0 us
    reduce_scatter x9 -> x0, waiting for transfers between devices: 1130 us -> none  [the longest x1 143 us: local(): lax.psum_scatter(txt_local[2], 'dp', scatter_dimension=1, tiled=True)]
    all_gather x6 -> x0, blocking collectives: 251 us -> none  [the longest x1 45.9 us: gather_first(): lax.all_gather(picture_feature_mapping, 'dp', axis=0, tiled=True)]
    unnamed x38 -> x0, waiting for transfers between devices: 169 us -> none
    pallas_call x0 -> x1, Pallas kernels: none -> 157 us  [local_fused(): pl.pallas_call(kernel, out_shape=(out(1, 1), out(1, 1), out(pad_img, d_im...]
    dot_general x47 -> x0, matrix products: 156 us -> none  [the longest x2 16.2 us: block_backward(): jnp.einsum('stf,std->fd', activated, branch, preferred_element_type=jnp.f...]
    unnamed x2 -> x0, blocking collectives: 115 us -> none
    all_gather x7 -> x0, waiting for transfers between devices: 85.2 us -> none  [the longest x1 57.2 us: gather_first(): lax.all_gather(img_stack[3], 'dp', axis=1, tiled=True)]
    unnamed x261 -> x41, local copies, waits for them, and re-layouts: 54.6 us -> 8.2 us
  transfers between devices with their start and end apart: 35 -> 0, of which waited for: 13 -> 0; matrix products, arithmetic and copies ran while one was open for 13% -> 0% of each run, Pallas kernels for 0% -> 0%
where the time goes in v1:
time: 179 us; the launch traced here: 178 us
  Pallas kernels  157 us (88%)
  local copies, waits for them, and re-layouts  15.8 us (9%)
  between operations  4.98 us (3%)
    pallas_call x1, Pallas kernels, local_fused(): pl.pallas_call(kernel, out_shape=(out(1, 1), out(1, 1), out(pad_img, d_im...  157 us
    unnamed x41, local copies, waits for them, and re-layouts  8.2 us

profile of v1, /device:TPU:0, one launch (start us, length us, event | category | flops | bytes accessed | tf_op | source)
XLA Modules:
  0.0 178.0 jit_solution(10909761698088275058)
XLA Ops:
  1.3 1.7 pad.9.refs_1_
  3.0 2.2 %pad.8.refs_0_ = bf16[640,768]{1,0:T(8,128)(2,1)} pad(bf16[600,768]{1,0:T(8,128)(2,1)} %param.18, bf16[]{:T(256)} %constant.2.clone.1), padding=0_40x0_0 | pad | bytes 1904642 | tf_op jit(solution)/shard_map/jit(_pad)/pad | solution.py:1351
  5.2 157.2 %contrastive_step.1 = (f32[1,1]{1,0:T(1,128)}, f32[1,1]{1,0:T(1,128)}, f32[640,768]{1,0:T(8,128)}, f32[256,512]{1,0:T(8,128)}, f32[24,2304]{1,0:T(8,128)}, /*ind...) custom-call(bf16[640,768]{1,0:T(8,128)(2,1)} %pad.8.refs_0_, ...), custom_call_target="tpu_custom_call" | custom-call | tf_op jit(solution)/shard_map/contrastive_step/pallas_call | solution.py:1389
  162.4 0.0 copy-start
  162.4 0.0 copy-start.3
  162.4 0.0 copy-start.7
  162.4 0.0 copy-start.2
  162.4 2.9 %slice.6 = f32[600,768]{1,0:T(8,128)} slice(f32[640,768]{1,0:T(8,128)} %get-tuple-element.36), slice={[0:600], [0:768]} | slice | bytes 3686400 | tf_op jit(solution)/shard_map/slice | solution.py:1416
  165.4 0.0 copy-done
  165.4 0.0 copy-start.1
  165.4 0.0 copy-start.11
  165.4 0.0 copy-start.13
  165.4 0.0 copy-start.6
  165.4 0.0 copy-start.9
  165.4 0.0 copy-start.5
  165.4 0.0 copy-start.4
  165.4 0.0 copy-start.10
  165.4 0.0 copy-start.12
  165.4 0.0 copy-start.8
  165.4 0.8 slice.7
  167.6 0.0 copy-done.3
  167.6 0.7 copy.53
  168.2 0.0 copy-done.7
  168.3 0.6 copy.54
  168.9 0.0 copy-done.2
  168.9 0.7 copy.55
  169.6 0.0 copy-done.1
  169.6 0.7 copy.56
  170.3 0.0 copy-done.11
  170.3 0.6 copy.57
  170.9 0.0 copy-done.13
  170.9 0.5 copy.58
  171.4 0.0 copy-done.6
  171.4 0.6 copy.59
  172.1 0.0 copy-done.9
  172.1 0.6 copy.60
  172.7 0.0 copy-done.5
  172.7 0.7 copy.61
  173.3 0.0 copy-done.4
  173.4 0.7 copy.62
  174.0 0.0 copy-done.10
  174.0 0.6 copy.63
  174.6 0.0 copy-done.12
  174.6 0.5 copy.64
  175.1 0.0 copy-done.8
  175.1 0.6 copy.65
Async XLA Ops:
  162.4 3.0 %copy-start = (f32[256,512]{1,0:T(8,128)S(1)}, f32[256,512]{1,0:T(8,128)}, u32[]{:S(2)}) copy-start(f32[256,512]{1,0:T(8,128)} %get-tuple-element.37) | copy-start | bytes 1572868
  162.4 5.2 %copy-start.3 = (f32[24,2304]{1,0:T(8,128)S(1)}, f32[24,2304]{1,0:T(8,128)}, u32[]{:S(2)}) copy-start(f32[24,2304]{1,0:T(8,128)} %get-tuple-element.38) | copy-start | bytes 663556
  162.4 5.8 %copy-start.7 = (f32[24,768]{1,0:T(8,128)S(1)}, f32[24,768]{1,0:T(8,128)}, u32[]{:S(2)}) copy-start(f32[24,768]{1,0:T(8,128)} %get-tuple-element.39) | copy-start | bytes 221188
  162.4 6.5 %copy-start.2 = (f32[24,3072]{1,0:T(8,128)S(1)}, f32[24,3072]{1,0:T(8,128)}, u32[]{:S(2)}) copy-start(f32[24,3072]{1,0:T(8,128)} %get-tuple-element.40) | copy-start | bytes 884740
  165.4 4.2 %copy-start.1 = (f32[96,768]{1,0:T(8,128)S(1)}, f32[96,768]{1,0:T(8,128)}, u32[]{:S(2)}) copy-start(f32[96,768]{1,0:T(8,128)} %get-tuple-element.41) | copy-start | bytes 884740
  165.4 5.0 %copy-start.11 = (f32[8,24]{1,0:T(8,128)S(1)}, f32[8,24]{1,0:T(8,128)}, u32[]{:S(2)}) copy-start(f32[8,24]{1,0:T(8,128)} %get-tuple-element.42) | copy-start | bytes 2308
  165.4 5.5 %copy-start.13 = (f32[1,96]{1,0:T(1,128)S(1)}, f32[1,96]{1,0:T(1,128)}, u32[]{:S(2)}) copy-start(f32[1,96]{1,0:T(1,128)} %get-tuple-element.77) | copy-start | bytes 1156
  165.4 6.1 %copy-start.6 = (f32[16,1536]{1,0:T(8,128)S(1)}, f32[16,1536]{1,0:T(8,128)}, u32[]{:S(2)}) copy-start(f32[16,1536]{1,0:T(8,128)} %get-tuple-element.44) | copy-start | bytes 294916
  165.4 6.7 %copy-start.9 = (f32[16,512]{1,0:T(8,128)S(1)}, f32[16,512]{1,0:T(8,128)}, u32[]{:S(2)}) copy-start(f32[16,512]{1,0:T(8,128)} %get-tuple-element.45) | copy-start | bytes 98308
  165.4 7.3 %copy-start.5 = (f32[16,2048]{1,0:T(8,128)S(1)}, f32[16,2048]{1,0:T(8,128)}, u32[]{:S(2)}) copy-start(f32[16,2048]{1,0:T(8,128)} %get-tuple-element.46) | copy-start | bytes 393220
  165.4 7.9 %copy-start.4 = (f32[64,512]{1,0:T(8,128)S(1)}, f32[64,512]{1,0:T(8,128)}, u32[]{:S(2)}) copy-start(f32[64,512]{1,0:T(8,128)} %get-tuple-element.47) | copy-start | bytes 393220
  165.4 8.6 %copy-start.10 = (f32[8,16]{1,0:T(8,128)S(1)}, f32[8,16]{1,0:T(8,128)}, u32[]{:S(2)}) copy-start(f32[8,16]{1,0:T(8,128)} %get-tuple-element.48) | copy-start | bytes 1540
  165.4 9.2 %copy-start.12 = (f32[1,64]{1,0:T(1,128)S(1)}, f32[1,64]{1,0:T(1,128)}, u32[]{:S(2)}) copy-start(f32[1,64]{1,0:T(1,128)} %get-tuple-element.83) | copy-start | bytes 772
  165.4 9.7 %copy-start.8 = (f32[24,512]{1,0:T(8,128)S(1)}, f32[24,512]{1,0:T(8,128)}, u32[]{:S(2)}) copy-start(f32[24,512]{1,0:T(8,128)} %get-tuple-element.84) | copy-start | bytes 147460

commit v2 on v0

--- a/solution.py
+++ b/solution.py
@@ -1,6 +1,8 @@
 import jax
 import jax.numpy as jnp
 from jax import lax
+from jax.experimental import pallas as pl
+from jax.experimental.pallas import tpu as pltpu
 from jax.sharding import PartitionSpec as P
 
 HD = 64
@@ -199,7 +201,7 @@
     return tuple((stacked[layer_index] for stacked in stacks))
 
 
-def local(
+def local_plain(
     picture_patch_inputs,
     caption_packed_inputs,
     picture_attend_entry_weight,
@@ -394,6 +396,1219 @@
     )
 
 
+F32 = jnp.float32
+BF16 = jnp.bfloat16
+Z_PEERS = (8, 16, 24)
+PLANE_PEERS = (2, 4, 6)
+ALL_PEERS = (1, 2, 3, 4, 5, 6, 7, 8, 9, 16, 17, 24, 25)
+PAD = 16
+N_SEMS = 100
+STEP_ROWS = 32
+
+
+def fits(mesh):
+    return mesh.size == 32
+
+
+def dot(left, right):
+    return lax.dot_general(left, right, (((1,), (0,)), ((), ())), preferred_element_type=F32)
+
+
+def dot_nt(left, right):
+    return lax.dot_general(left, right, (((1,), (1,)), ((), ())), preferred_element_type=F32)
+
+
+def dot_tn(left, right):
+    return lax.dot_general(left, right, (((0,), (0,)), ((), ())), preferred_element_type=F32)
+
+
+def split_two(values):
+    high = values.astype(BF16)
+    return high, (values - high.astype(F32)).astype(BF16)
+
+
+def iota(shape, dim):
+    return lax.broadcasted_iota(jnp.int32, shape, dim)
+
+
+def expand_heads(rows):
+    lanes = iota(rows.shape, 1) // HD
+    heads = rows.shape[1] // HD
+    zero = jnp.zeros_like(rows)
+    return jnp.concatenate([jnp.where(lanes == head, rows, zero) for head in range(heads)], 0)
+
+
+def join_heads(stacked):
+    heads = stacked.shape[1] // HD
+    lanes = iota((PAD, stacked.shape[1]), 1) // HD
+    total = jnp.zeros((PAD, stacked.shape[1]), F32)
+    for head in range(heads):
+        total = jnp.where(lanes == head, stacked[PAD * head : PAD * (head + 1)], total)
+    return total
+
+
+def small_norm(hidden, gain, shift):
+    centred = hidden - jnp.mean(hidden, -1, keepdims=True)
+    inverse = lax.rsqrt(jnp.mean(centred * centred, -1, keepdims=True) + 1e-05)
+    normed = centred * inverse
+    return normed, inverse, normed * gain + shift
+
+
+def small_norm_back(upstream, normed, inverse, gain):
+    scaled = upstream * gain
+    return inverse * (
+        scaled
+        - jnp.mean(scaled, -1, keepdims=True)
+        - normed * jnp.mean(scaled * normed, -1, keepdims=True)
+    )
+
+
+def col_sum(values):
+    return jnp.sum(values, 0, keepdims=True)
+
+
+class Tower:
+    def __init__(self, along_z, width, real_tokens, rows, block, extra):
+        self.along_z = along_z
+        self.width = width
+        self.real_tokens = real_tokens
+        self.tokens = -(-real_tokens // 128) * 128
+        self.rows = rows
+        self.chip_rows = 2 * rows
+        self.block = block
+        self.group = 4 * block
+        self.heads = width // HD
+        self.queries = PAD * self.heads
+        self.extra = extra
+        self.packed = 2 * width + extra + 4 * self.group
+        self.row_pad = -(-rows // 16) * 16
+        self.group_peers = Z_PEERS if along_z else PLANE_PEERS
+        self.copy_peers = PLANE_PEERS if along_z else Z_PEERS
+        self.line_peers = (1,) + tuple(mask + core for mask in self.group_peers for core in range(2))
+        self.sums = {}
+
+    def chip_of(self, group, copy):
+        return 4 * group + copy if self.along_z else 4 * copy + group
+
+    def device_of(self, group, copy, core):
+        return 2 * self.chip_of(group, copy) + core
+
+    def group_of(self, device):
+        return device // 8 if self.along_z else lax.rem(device // 2, 4)
+
+    def copy_of(self, device):
+        return lax.rem(device // 2, 4) if self.along_z else device // 8
+
+    def chips_of_group(self, ref, group):
+        return ref.at[group] if self.along_z else ref.at[:, group]
+
+    def chips_of_copy(self, ref, copy):
+        return ref.at[:, copy] if self.along_z else ref.at[copy]
+
+    def scratch(self):
+        d, n, r, g, b, cr = self.width, self.tokens, self.queries, self.group, self.block, self.chip_rows
+        c1, c2 = 2 * d + 2 * self.extra, 2 * d
+        v = pltpu.VMEM
+        return dict(
+            pk=v((2, self.row_pad, self.packed), BF16),
+            pr=v((self.row_pad, self.packed), BF16),
+            w1=v((2, 16 * cr, d), BF16),
+            w2=v((2, 16 * cr, d), BF16),
+            mf=v((4, cr, g), BF16),
+            fa=v((4, 4, cr, g), BF16),
+            wp=v((4, b, d), BF16),
+            vecs=v((8, d), F32),
+            bias=v((8, g), F32),
+            xp=v((n, d), BF16),
+            xh=v((n, d), F32),
+            inv=v((n, 128), F32),
+            a=v((n, d), BF16),
+            p32=v((r, n), F32),
+            lh=v((2 * r + 2 * PAD, n), BF16),
+            rh=v((2 * r + 2 * PAD, d), BF16),
+            ci=v((8, PAD, d), BF16),
+            hpf=v((8, PAD, d), F32),
+            hps=v((8, PAD, d), BF16),
+            hr=v((7, PAD, d), BF16),
+            dcf=v((8, PAD, d), F32),
+            dcs=v((8, PAD, d), BF16),
+            dcr=v((7, PAD, d), BF16),
+            sc=v((8, PAD, 128), F32),
+            u=v((8 * PAD, g), F32),
+            m=v((8 * PAD, g), BF16),
+            gpf=v((4, b, d), F32),
+            gpb=v((4, b, d), BF16),
+            gpr=v((3, b, d), BF16),
+            gff=v((4, 4, cr, g), F32),
+            gfb=v((4, 4, cr, g), BF16),
+            gfr=v((3, 4, cr, g), BF16),
+            gf2=v((4, cr, g), BF16),
+            gf3=v((4, cr, g), F32),
+            gf3r=v((4, cr, g), BF16),
+            gf4=v((4, self.rows, g), F32),
+            in1t=v((4, 4, cr, 256), BF16),
+            in1r=v((4, 4, cr, 256), BF16),
+            in2t=v((4, 4, cr, r), BF16),
+            in2r=v((4, 4, cr, r), BF16),
+            qg=v((4, PAD, d), BF16),
+            wg=v((4, PAD, d), BF16),
+            dog=v((4, PAD, d), BF16),
+            dqg=v((4, PAD, d), BF16),
+            r1f=v((4, cr, c1), F32),
+            r1b=v((4, cr, c1), BF16),
+            r1r=v((3, cr, c1), BF16),
+            r1s=v((cr, c1), F32),
+            r1p=v((self.rows, c1), F32),
+            r2f=v((4, cr, c2), F32),
+            r2b=v((4, cr, c2), BF16),
+            r2r=v((3, cr, c2), BF16),
+            r2s=v((cr, c2), F32),
+            r2p=v((self.rows, c2), F32),
+            da=v((n, d), F32),
+            gp=v((n, d), F32),
+            dxs=v((self.real_tokens, d), F32),
+            g2=v((8, PAD, d), F32),
+            dbs=v((8, g), F32),
+            dbr=v((3, 8, g), F32),
+        )
+
+
+def shared_scratch(ti, tt):
+    v = pltpu.VMEM
+    wide = ti.width + tt.width
+    e = tt.width
+    rows = 32 * PAD
+    return dict(
+        vb=v((2, 16, PAD, 128), BF16),
+        w3=v((2, ti.width, ti.extra), BF16),
+        eb=v((2, 2, 16, PAD, e), BF16),
+        gtxt=v((rows, rows), F32),
+        gimg=v((rows, rows), F32),
+        drb=v((8, PAD, e), BF16),
+        vz=v((8, wide), F32),
+        vzr=v((3, 8, wide), F32),
+        vp=v((8, wide), F32),
+        vpr=v((3, 8, wide), F32),
+        vc=v((8, wide), F32),
+        vcr=v((8, wide), F32),
+    )
+
+
+class Group:
+    def __init__(self, step):
+        self.step = step
+        self.index = step.used
+        step.used += 1
+        step.groups.append(self)
+
+    def copy(self, src, dst, mask):
+        return pltpu.make_async_remote_copy(
+            src_ref=src,
+            dst_ref=dst,
+            send_sem=self.step.ssem.at[self.index],
+            recv_sem=self.step.rsem.at[self.index],
+            device_id=(self.step.at_peer(mask),),
+            device_id_type=pl.DeviceIdType.MESH,
+        )
+
+    def send(self, src, dst, mask):
+        self.copy(src, dst, mask).start()
+
+    def wait(self, view):
+        self.view = view
+        self.copy(view, view, 1).wait_recv()
+
+    def finish(self):
+        self.copy(self.view, self.view, 1).wait_send()
+
+
+class Gather:
+    def __init__(self, step, slot, span, whole, relay):
+        self.step, self.slot, self.span, self.whole, self.relayed = step, slot, span, whole, relay
+        self.own = self.step.chip
+
+    def chip(self, mask):
+        return self.step.at_peer(mask) // 2
+
+    def spread(self, group, chip):
+        here = self.slot(chip)
+        for mask in PLANE_PEERS[:2] if self.relayed else PLANE_PEERS:
+            group.send(here, here, mask)
+
+    def begin_z(self):
+        self.g_z = Group(self.step)
+        here = self.slot(self.own)
+        for mask in Z_PEERS:
+            self.g_z.send(here, here, mask)
+
+    def begin_plane(self):
+        self.g_own = Group(self.step)
+        self.spread(self.g_own, self.own)
+
+    def middle(self):
+        self.g_z.wait(self.span(3))
+        self.g_mid = Group(self.step)
+        for mask in Z_PEERS:
+            self.spread(self.g_mid, self.chip(mask))
+
+    def hand_on(self, mask):
+        for half, near, to in ((0, 2, 4), (1, 4, 2)):
+            there = self.slot(self.chip(near | mask), half)
+            self.g_relay.send(there, there, to)
+
+    def relay_own(self):
+        self.g_own.wait(self.span(2))
+        self.g_relay = Group(self.step)
+        self.hand_on(0)
+
+    def relay(self):
+        self.g_mid.wait(self.span(6))
+        for mask in Z_PEERS:
+            self.hand_on(mask)
+
+    def end(self):
+        if self.relayed:
+            self.g_relay.wait(self.span(4))
+        else:
+            self.g_own.wait(self.span(3))
+            self.g_mid.wait(self.span(9))
+        self.g_core = Group(self.step)
+        self.g_core.send(self.whole, self.whole, 1)
+
+    def done(self):
+        self.g_core.wait(self.whole)
+
+
+class Step:
+    def __init__(self, ti, tt, images):
+        self.ti, self.tt, self.images = ti, tt, images
+        me = lax.axis_index("dp")
+        self.bits = [lax.rem(me // (1 << bit), 2) for bit in range(5)]
+        self.me = me
+        self.core = lax.rem(me, 2)
+        self.chip = me // 2
+        self.plane = lax.rem(me // 2, 4)
+        self.zed = me // 8
+        for t in (ti, tt):
+            t.g, t.r = (self.zed, self.plane) if t.along_z else (self.plane, self.zed)
+            t.spot = self.core * 4 + t.g
+        self.used = 0
+        self.groups = []
+
+    def at_peer(self, mask):
+        total = 0
+        for bit in range(5):
+            value = 1 - self.bits[bit] if mask >> bit & 1 else self.bits[bit]
+            total = total + value * (1 << bit)
+        return total
+
+    def barrier(self):
+        semaphore = pltpu.get_barrier_semaphore()
+        for mask in ALL_PEERS:
+            pl.semaphore_signal(
+                semaphore, inc=1, device_id=(self.at_peer(mask),), device_id_type=pl.DeviceIdType.MESH
+            )
+        pl.semaphore_wait(semaphore, len(ALL_PEERS))
+
+    def row_gather(self, buffer, rows):
+        cols = buffer.shape[2] // 2
+
+        def slot(chip, half=None):
+            at = pl.ds(pl.multiple_of(chip * rows, 16), rows)
+            if half is None:
+                return buffer.at[self.core, at]
+            return buffer.at[self.core, at, half * cols : (half + 1) * cols]
+
+        return Gather(
+            self, slot, lambda count: buffer.at[self.core, 0 : count * rows], buffer.at[self.core], True
+        )
+
+    def line_gather(self, t, buffer):
+        group = Group(self)
+        here = buffer.at[t.spot]
+        for mask in t.line_peers:
+            group.send(here, here, mask)
+        return group
+
+    def line_scatter(self, t, parts, landing):
+        group = Group(self)
+        for slot, mask in enumerate(t.line_peers):
+            peer = self.at_peer(mask)
+            group.send(parts.at[lax.rem(peer, 2) * 4 + t.group_of(peer)], landing.at[slot], mask)
+        return group
+
+    def to_group(self, t, block, landing):
+        group = Group(self)
+        for mask in t.group_peers:
+            group.send(t.chips_of_group(block, t.group_of(self.at_peer(mask))), landing.at[t.g], mask)
+        landing[t.g] = t.chips_of_group(block, t.g)[...]
+        return group
+
+    def share_group(self, t, buffer, values):
+        group = Group(self)
+        buffer[t.g] = values
+        here = buffer.at[t.g]
+        for mask in t.group_peers:
+            group.send(here, here, mask)
+        return group
+
+    def to_copies(self, t, block, landing):
+        group = Group(self)
+        for slot, mask in enumerate(t.copy_peers):
+            group.send(block.at[t.copy_of(self.at_peer(mask))], landing.at[slot], mask)
+        return group
+
+    def run(self):
+        ti, tt = self.ti, self.tt
+        both = (ti, tt)
+        self.pack(ti)
+        self.pack(tt)
+        self.pack_vectors()
+        self.barrier()
+        for t in both:
+            t.pair = Group(self)
+            t.pair.send(t.pk.at[1 - self.core], t.pr, 1)
+        vb, eb = self.vb, self.eb
+        vectors = Gather(
+            self,
+            lambda chip: vb.at[self.core, chip],
+            lambda count: vb.at[self.core, 0:count],
+            vb.at[self.core],
+            False,
+        )
+        vectors.begin_z()
+        vectors.begin_plane()
+        for t in both:
+            t.first = self.row_gather(t.w1, t.chip_rows)
+            t.second = self.row_gather(t.w2, t.chip_rows)
+        third = self.row_gather(self.w3, ti.chip_rows)
+        for t in both:
+            self.merge(t)
+            t.first.begin_z()
+            t.first.begin_plane()
+        for t in both:
+            t.second.begin_z()
+        for t in both:
+            self.widen_begin(t)
+        third.begin_z()
+        self.standardize(tt)
+        vectors.middle()
+        for t in both:
+            t.first.middle()
+        for t in both:
+            t.first.relay_own()
+        for t in both:
+            t.second.begin_plane()
+        for t in both:
+            t.second.middle()
+        self.standardize(ti)
+        for t in both:
+            t.first.relay()
+        for t in both:
+            t.second.relay_own()
+        for t in both:
+            self.widen_middle(t)
+        vectors.end()
+        third.begin_plane()
+        third.middle()
+        vectors.done()
+        self.unpack_vectors()
+        self.queries(ti)
+        self.queries(tt)
+        for t in both:
+            t.first.end()
+        for t in both:
+            t.second.relay()
+        third.relay_own()
+        ti.first.done()
+        self.attend(ti)
+        tt.first.done()
+        self.attend(tt)
+        for t in both:
+            t.second.end()
+        third.relay()
+        for t in both:
+            t.second.done()
+            self.mix(t)
+        third.end()
+        for t in both:
+            self.feed(t)
+        third.done()
+        for t in both:
+            self.embed(t)
+        rows = Gather(
+            self,
+            lambda chip: eb.at[:, self.core, chip],
+            lambda count: eb.at[:, self.core, 0:count],
+            eb.at[:, self.core],
+            False,
+        )
+        rows.begin_z()
+        rows.begin_plane()
+        for t in both:
+            t.scales = self.line_gather(t, t.sc)
+        rows.middle()
+        for t in both:
+            self.early_operands(t)
+        rows.end()
+        rows.done()
+        for t in both:
+            t.scales.wait(t.sc.at[0:7])
+        self.contrast()
+        for t in both:
+            self.feed_back(t)
+        for t in both:
+            self.feed_weights(t)
+        for t in both:
+            self.attend_back(t)
+        for t in both:
+            self.attend_back_end(t)
+        for t in both:
+            self.input_gradient(t)
+        copies = self.vector_sum_begin()
+        for t in both:
+            self.feed_weights_middle(t)
+        for t in both:
+            self.round_one(t)
+        copies = self.vector_sum_middle(copies)
+        for t in both:
+            self.round_two(t)
+        copies = self.vector_sum_end(copies)
+        for t in both:
+            self.feed_weights_end(t)
+        for t in both:
+            self.rounds_end(t)
+        self.vector_sum_done(copies)
+        for t in both:
+            self.rounds_done(t)
+        for t in both:
+            self.copy_out(t).wait()
+        for group in self.groups:
+            group.finish()
+
+    def pack(self, t):
+        pk, qkv, out, fc = t.pk, t.qkv, t.out, t.fc
+        d, b = t.width, t.block
+        pad = t.row_pad - t.rows
+
+        def padded(values):
+            values = values.astype(F32)
+            if pad:
+                values = jnp.concatenate([values, jnp.zeros((pad, values.shape[1]), F32)], 0)
+            return values.astype(BF16)
+
+        pk[0, :, 0:d] = padded(qkv[:, 0:d])
+        pk[1, :, 0:d] = padded(qkv[:, d : 2 * d])
+        pk[0, :, d : 2 * d] = padded(qkv[:, 2 * d : 3 * d])
+        pk[1, :, d : 2 * d] = padded(out[...])
+        if t.extra:
+            for half in range(2):
+                cols = slice(half * t.extra, (half + 1) * t.extra)
+                pk[half, :, 2 * d : 2 * d + t.extra] = padded(self.map[:, cols])
+        base = 2 * d + t.extra
+        values = padded(fc[...]).astype(F32)
+        for half in range(2):
+            for group in range(4):
+                pieces = []
+                for copy in range(4):
+                    device = t.device_of(group, copy, half)
+                    pieces.append(values[:, b * device : b * (device + 1)])
+                start = base + group * t.group
+                pk[half, :, start : start + t.group] = jnp.concatenate(pieces, 1).astype(BF16)
+
+    def pack_vectors(self):
+        def widen(values, at):
+            values = values.astype(F32)
+            parts = [values, jnp.zeros((values.shape[0], 128 - at - values.shape[1]), F32)]
+            if at:
+                parts = [jnp.zeros((values.shape[0], at), F32)] + parts
+            return jnp.concatenate(parts, 1)
+
+        top = widen(self.ti.vec[...], 0) + widen(self.tt.vec[...], 32)
+        row = iota((8, 128), 0)
+        bottom = jnp.where(row == 0, widen(self.ti.fcb[...], 0), 0.0)
+        bottom = bottom + jnp.where(row == 1, widen(self.tt.fcb[...], 0), 0.0)
+        block = jnp.concatenate([top, bottom], 0)
+        row, lane = iota((PAD, 128), 0), iota((PAD, 128), 1)
+        for caption in range(self.images):
+            image = self.match[caption]
+            device = image // self.images
+            high = lax.rem(device, 2) * 16 + device // 2
+            low = image - device * self.images
+            block = jnp.where((row == caption) & (lane == 120), high.astype(F32), block)
+            block = jnp.where((row == caption) & (lane == 121), low.astype(F32), block)
+        self.vb[self.core, self.chip] = block.astype(BF16)
+
+    def unpack_vectors(self):
+        vb = self.vb
+        for core in range(2):
+            for chip in range(16):
+                block = vb[core, chip].astype(F32)
+                device = 2 * chip + core
+                for t, at in ((self.ti, 0), (self.tt, 32)):
+                    rows = t.rows
+                    t.vecs[:, rows * device : rows * (device + 1)] = block[0:8, at : at + rows]
+        for t, row in ((self.ti, 8), (self.tt, 9)):
+            for copy in range(4):
+                block = vb[self.core, t.chip_of(t.g, copy)].astype(F32)
+                b = t.block
+                t.bias[0:1, b * copy : b * (copy + 1)] = block[row : row + 1, 0:b]
+
+    def standardize(self, t):
+        x, xp, xh, inv = t.x, t.xp, t.xh, t.inv
+        step = STEP_ROWS
+        full = t.real_tokens // step
+
+        def norm(hidden, rows):
+            xp[rows, :] = hidden.astype(BF16)
+            centred = hidden - jnp.mean(hidden, -1, keepdims=True)
+            inverse = lax.rsqrt(jnp.mean(centred * centred, -1, keepdims=True) + 1e-05)
+            xh[rows, :] = centred * inverse
+            inv[rows, :] = jnp.broadcast_to(inverse, (step, 128))
+
+        def body(index, carry):
+            rows = pl.ds(pl.multiple_of(index * step, step), step)
+            norm(x[rows, :].astype(F32), rows)
+            return carry
+
+        lax.fori_loop(0, full, body, 0)
+        start, rest = full * step, t.real_tokens - full * step
+        if rest:
+            last = x[start : t.real_tokens, :].astype(F32)
+            last = jnp.concatenate([last, jnp.zeros((step - rest, t.width), F32)], 0)
+            norm(last, slice(start, start + step))
+            start += step
+        while start < t.tokens:
+            norm(jnp.zeros((step, t.width), F32), slice(start, start + step))
+            start += step
+
+    def merge(self, t):
+        t.pair.wait(t.pr)
+        pk, pr = t.pk, t.pr
+        d, g = t.width, t.group
+        rows = pl.ds(pl.multiple_of(self.chip * t.chip_rows, 16), t.chip_rows)
+        first = self.core == 0
+
+        def merged(cols):
+            own = pk[self.core, :, cols].astype(F32)
+            got = pr[:, cols].astype(F32)
+            upper = jnp.where(first, own, got)[: t.rows]
+            lower = jnp.where(first, got, own)[: t.rows]
+            return jnp.concatenate([upper, lower], 0).astype(BF16)
+
+        t.w1[self.core, rows, :] = merged(slice(0, d))
+        t.w2[self.core, rows, :] = merged(slice(d, 2 * d))
+        base = 2 * d
+        if t.extra:
+            self.w3[self.core, rows, :] = merged(slice(base, base + t.extra))
+            base += t.extra
+        for group in range(4):
+            t.mf[group] = merged(slice(base + group * g, base + (group + 1) * g))
+
+    def widen_begin(self, t):
+        t.widen = Group(self)
+        for mask in t.group_peers:
+            t.widen.send(t.mf.at[t.group_of(self.at_peer(mask))], t.fa.at[self.zed, self.plane], mask)
+        t.fa[self.zed, self.plane] = t.mf[t.g]
+
+    def widen_middle(self, t):
+        t.widen.wait(t.mf.at[0:3])
+        t.widen, t.narrow = Group(self), Group(self)
+        part = t.chips_of_copy(t.fa, t.r)
+        for mask in t.copy_peers:
+            t.widen.send(part, part, mask)
+        for mask in t.copy_peers:
+            t.narrow.send(t.proj, t.wp.at[t.r], mask)
+        t.wp[t.r] = t.proj[...]
+
+    def queries(self, t):
+        a, xh, vec = t.a, t.xh, t.vecs
+        step = STEP_ROWS
+
+        def body(index, carry):
+            rows = pl.ds(pl.multiple_of(index * step, step), step)
+            a[rows, :] = (xh[rows, :] * vec[0:1, :] + vec[1:2, :]).astype(BF16)
+            return carry
+
+        lax.fori_loop(0, t.tokens // step, body, 0)
+        n = t.tokens
+        row, token = iota((PAD, n), 0), iota((PAD, n), 1)
+        if t is self.ti:
+            real = row < self.images
+            at = jnp.where(real, row * TOK_I, -1)
+            low, high = jnp.where(real, row * TOK_I, -1), jnp.where(real, (row + 1) * TOK_I, -1)
+        else:
+            counts = self.counts
+            column = iota((PAD, 1), 0)
+            low, high = jnp.full((PAD, 1), -1, jnp.int32), jnp.full((PAD, 1), -1, jnp.int32)
+            for line in range(counts.shape[0]):
+                end = line * TOK_T
+                for member in range(CAP_ROW):
+                    begin, end = end, end + counts[line, member]
+                    chosen = column == line * CAP_ROW + member
+                    low, high = jnp.where(chosen, begin, low), jnp.where(chosen, end, high)
+            at = jnp.where(high > 0, high - 1, -1)
+        chosen = (token == at).astype(F32).astype(BF16)
+        lh, r = t.lh, t.queries
+        lh[2 * r : 2 * r + PAD, :] = chosen
+        lh[2 * r + PAD : 2 * r + 2 * PAD, :] = chosen
+        t.seen = ((token >= low) & (token < high)).astype(F32)
+        t.x0 = dot(chosen, t.xp[...])
+        t.a0 = dot(chosen, a[...]).astype(BF16)
+
+    def attend(self, t):
+        w1, vec, a, r = t.w1, t.vecs, t.a, t.queries
+        t.q = (dot(t.a0, w1[0]) + vec[2:3, :]).astype(BF16)
+        qt = dot_nt(expand_heads(t.q), w1[1]).astype(BF16)
+        t.rh[0:r, :] = qt
+        scores = dot_nt(qt, a[...]) * 0.125
+        seen = jnp.concatenate([t.seen] * t.heads, 0) > 0.5
+        scores = jnp.where(seen, scores, -1000000000.0)
+        top = jnp.max(scores, -1, keepdims=True)
+        raw = jnp.where(seen, jnp.exp(scores - top), 0.0)
+        total = jnp.sum(raw, -1, keepdims=True)
+        probs = raw / jnp.where(total > 0.0, total, 1.0)
+        t.p32[...] = probs
+        low = probs.astype(BF16)
+        t.lh[r : 2 * r, :] = low
+        t.pa = dot(low, a[...])
+
+    def mix(self, t):
+        w2, vec = t.w2, t.vecs
+        context = (join_heads(dot(t.pa.astype(BF16), w2[0])) + vec[3:4, :]).astype(BF16)
+        t.o = context
+        t.h1 = t.x0 + (dot(context, w2[1]) + vec[4:5, :])
+        t.xh2, t.inv2, second = small_norm(t.h1, vec[5:6, :], vec[6:7, :])
+        t.ci[t.spot] = second.astype(BF16)
+        t.line = self.line_gather(t, t.ci)
+
+    def feed(self, t):
+        d, g = t.width, t.group
+        t.widen.wait(t.fa.at[0:3])
+        t.narrow.wait(t.wp.at[0:3])
+        t.line.wait(t.ci.at[0:7])
+        c = t.ci[...].reshape(8 * PAD, d)
+        up = dot(c, t.fa[...].reshape(d, g)) + t.bias[0:1, :]
+        active = (up * jax.nn.sigmoid(1.702 * up)).astype(BF16)
+        t.u[...] = up
+        t.m[...] = active
+        part = dot(active, t.wp[...].reshape(g, d)).reshape(8, PAD, d)
+        t.hpf[...] = part
+        t.hps[...] = part.astype(BF16)
+        t.line = self.line_scatter(t, t.hps, t.hr)
+
+    def line_total(self, t, own, landing):
+        t.line.wait(landing)
+        total = own[t.spot]
+        for slot in range(7):
+            total = total + landing[slot].astype(F32)
+        return total
+
+    def embed(self, t):
+        hidden = t.h1 + (self.line_total(t, t.hpf, t.hr) + t.vecs[7:8, :])
+        which = 1
+        raw = hidden
+        if t is self.ti:
+            which = 0
+            self.pooled = hidden.astype(BF16)
+            raw = jnp.concatenate([dot(self.pooled, self.w3[0]), dot(self.pooled, self.w3[1])], 1)
+        scale = lax.rsqrt(jnp.sum(raw * raw, -1, keepdims=True) + 1e-06)
+        self.eb[which, self.core, self.chip] = (raw * scale).astype(BF16)
+        t.sc[t.spot] = jnp.broadcast_to(scale, (PAD, 128))
+
+    def early_operands(self, t):
+        d, r = t.width, t.queries
+        parts = [t.pa, t.o.astype(F32), t.a0.astype(F32)]
+        if t is self.ti:
+            parts.append(self.pooled.astype(F32))
+        rest = 256 - r - PAD * (len(parts) - 1)
+        parts.append(jnp.zeros((rest, d), F32))
+        t.in1t[...] = jnp.concatenate(parts, 0).T.astype(BF16).reshape(4, 4, t.chip_rows, 256)
+        t.c_in1 = self.to_group(t, t.in1t, t.in1r)
+        t.c_q = self.share_group(t, t.qg, t.q)
+
+    def contrast(self):
+        eb, gtxt, gimg = self.eb, self.gtxt, self.gimg
+        size = 32 * PAD
+        total = self.images * 32
+        e_img, e_txt = eb[0].reshape(size, eb.shape[-1]), eb[1].reshape(size, eb.shape[-1])
+        sharp = jnp.exp(jnp.full((8, 128), self.sharp[0], F32))[0:1, 0:1]
+        logits = sharp * dot_nt(e_txt, e_img)
+        marks = self.vb[...].reshape(size, 128).astype(F32)
+        target = marks[:, 120:121] * float(PAD) + marks[:, 121:122]
+        row, col = iota((size, size), 0), iota((size, size), 1)
+        real = (lax.rem(row, PAD) < self.images) & (lax.rem(col, PAD) < self.images)
+        hit = real & (col.astype(F32) == target)
+        powers = jnp.where(real, jnp.exp(logits), 0.0)
+        row_sum, col_sums = jnp.sum(powers, 1, keepdims=True), col_sum(powers)
+        real_line = lax.rem(iota((size, 1), 0), PAD) < self.images
+        real_lane = lax.rem(iota((1, size), 1), PAD) < self.images
+        row_sum, col_sums = jnp.where(real_line, row_sum, 1.0), jnp.where(real_lane, col_sums, 1.0)
+        grad = powers * ((1.0 / row_sum + 1.0 / col_sums) * (0.5 / total))
+        grad = grad - jnp.where(hit, 1.0 / total, 0.0)
+        safe = jnp.where(real, logits, 0.0)
+        logs = jnp.sum(jnp.log(row_sum), 0, keepdims=True) + jnp.sum(jnp.log(col_sums), 1, keepdims=True)
+
+        def whole(values):
+            return jnp.sum(jnp.sum(values, 1, keepdims=True), 0, keepdims=True)
+
+        self.loss[...] = logs * (0.5 / total) - whole(jnp.where(hit, safe, 0.0)) * (1.0 / total)
+        self.dls[...] = whole(grad * safe)
+        gtxt[...] = grad
+        gimg[...] = grad.T
+        for which, t, rows, others in ((0, self.ti, gimg, e_txt), (1, self.tt, gtxt, e_img)):
+            parts, own = [], []
+            for core in range(2):
+                for group in range(4):
+                    chip = t.chip_of(group, t.r)
+                    start = pl.multiple_of((core * 16 + chip) * PAD, PAD)
+                    parts.append(rows[pl.ds(start, PAD), :])
+                    own.append(eb[which, core, chip].astype(F32))
+            part, unit = jnp.concatenate(parts, 0), jnp.concatenate(own, 0)
+            scale = t.sc[...].reshape(8 * PAD, 128)[:, 0:1]
+            high, low = split_two(part)
+            d_unit = sharp * (dot(high, others) + dot(low, others))
+            d_raw = scale * (d_unit - unit * jnp.sum(d_unit * unit, -1, keepdims=True))
+            if t is self.ti:
+                w3, half = self.w3, t.extra
+                rounded = d_raw.astype(BF16)
+                self.drb[...] = rounded.reshape(self.drb.shape)
+                d_raw = dot_nt(rounded[:, 0:half], w3[0]) + dot_nt(rounded[:, half : 2 * half], w3[1])
+            t.g2[...] = d_raw.reshape(t.g2.shape)
+
+    def feed_back(self, t):
+        d, g = t.width, t.group
+        t.y = t.g2[...].reshape(8 * PAD, d).astype(BF16)
+        up = t.u[...]
+        gate = jax.nn.sigmoid(1.702 * up)
+        d_active = dot_nt(t.y, t.wp[...].reshape(g, d))
+        t.du = (d_active * (gate + 1.702 * up * gate * (1.0 - gate))).astype(BF16)
+        part = dot_nt(t.du, t.fa[...].reshape(d, g)).reshape(8, PAD, d)
+        t.dcf[...] = part
+        t.dcs[...] = part.astype(BF16)
+        t.line = self.line_scatter(t, t.dcs, t.dcr)
+
+    def feed_weights(self, t):
+        d, g, b, cr = t.width, t.group, t.block, t.chip_rows
+        grad = dot_tn(t.ci[...].reshape(8 * PAD, d), t.du).reshape(4, 4, cr, g)
+        t.gff[...] = grad
+        t.gfb[...] = grad.astype(BF16)
+        t.c_wide, t.c_narrow, t.c_bias = Group(self), Group(self), Group(self)
+        for slot, mask in enumerate(t.copy_peers):
+            t.c_wide.send(t.chips_of_copy(t.gfb, t.copy_of(self.at_peer(mask))), t.gfr.at[slot], mask)
+        grad = dot_tn(t.m[...], t.y).reshape(4, b, d)
+        t.gpf[...] = grad
+        t.gpb[...] = grad.astype(BF16)
+        t.dbs[...] = jnp.broadcast_to(col_sum(t.du.astype(F32)), (8, g))
+        for slot, mask in enumerate(t.copy_peers):
+            t.c_narrow.send(t.gpb.at[t.copy_of(self.at_peer(mask))], t.gpr.at[slot], mask)
+            t.c_bias.send(t.dbs, t.dbr.at[slot], mask)
+
+    def feed_weights_middle(self, t):
+        b = t.block
+        t.c_wide.wait(t.gfr)
+        total = t.chips_of_copy(t.gff, t.r)[...]
+        for slot in range(3):
+            total = total + t.gfr[slot].astype(F32)
+        t.gf2[...] = total.astype(BF16)
+        t.gf3[...] = total
+        t.c_line = Group(self)
+        for mask in t.group_peers:
+            t.c_line.send(t.gf2.at[t.group_of(self.at_peer(mask))], t.gf3r.at[t.g], mask)
+        t.c_narrow.wait(t.gpr)
+        total = t.gpf[t.r]
+        for slot in range(3):
+            total = total + t.gpr[slot].astype(F32)
+        t.d_proj[...] = total
+        t.c_bias.wait(t.dbr)
+        bias = t.dbs[0:1, :]
+        for slot in range(3):
+            bias = bias + t.dbr[slot, 0:1, :]
+        mine = jnp.zeros((1, b), F32)
+        for copy in range(4):
+            mine = jnp.where(t.r == copy, bias[:, b * copy : b * (copy + 1)], mine)
+        t.d_fcb[...] = mine
+
+    def feed_weights_end(self, t):
+        t.c_line.wait(t.gf2.at[0:3])
+        own = t.gf3[t.g]
+        for group in range(4):
+            t.gf3[group] = jnp.where(t.g == group, own, t.gf3r[group].astype(F32))
+        start = pl.multiple_of((1 - self.core) * t.rows, 8)
+        t.c_fc = Group(self)
+        t.c_fc.send(t.gf3.at[:, pl.ds(start, t.rows)], t.gf4, 1)
+
+    def attend_back(self, t):
+        vec = t.vecs
+        total = self.line_total(t, t.dcf, t.dcr)
+        g2 = t.g2[t.spot]
+        t.g1 = g2 + small_norm_back(total, t.xh2, t.inv2, vec[5:6, :])
+        branch = t.g1.astype(BF16)
+        t.do = dot_nt(branch, t.w2[1]).astype(BF16)
+        t.sums.update(
+            dbv=col_sum(t.do.astype(F32)),
+            dbo=col_sum(branch.astype(F32)),
+            dg2=col_sum(total * t.xh2),
+            db2=col_sum(total),
+            dbp=col_sum(g2.astype(BF16).astype(F32)),
+        )
+        t.c_w = self.share_group(t, t.wg, branch)
+        t.c_do = self.share_group(t, t.dog, t.do)
+
+    def attend_back_end(self, t):
+        r, w1, a, lh, rh = t.queries, t.w1, t.a, t.lh, t.rh
+        dvt = dot_nt(expand_heads(t.do), t.w2[0]).astype(BF16)
+        rh[r : 2 * r, :] = dvt
+        d_probs = dot_nt(dvt, a[...])
+        probs = t.p32[...]
+        weighted = probs * d_probs
+        d_scores = (weighted - probs * jnp.sum(weighted, -1, keepdims=True)).astype(BF16)
+        d_scores = (d_scores.astype(F32) * 0.125).astype(BF16)
+        lh[0:r, :] = d_scores
+        moved = dot(d_scores, a[...])
+        t.in2t[...] = moved.T.astype(BF16).reshape(t.in2t.shape)
+        t.c_in2 = self.to_group(t, t.in2t, t.in2r)
+        d_query = join_heads(dot(moved.astype(BF16), w1[1])).astype(BF16)
+        t.c_dq = self.share_group(t, t.dqg, d_query)
+        t.sums.update(dbq=col_sum(d_query.astype(F32)))
+        high, low = split_two(dot_nt(d_query, w1[0]))
+        rh[2 * r : 2 * r + PAD, :] = high
+        rh[2 * r + PAD : 2 * r + 2 * PAD, :] = low
+
+    def copy_out(self, t):
+        return pltpu.make_async_copy(t.dxs, t.d_x, self.osem.at[0 if t is self.ti else 1])
+
+    def input_gradient(self, t):
+        r, d = t.queries, t.width
+        lh, da, gp, xh, inv, vec, out = t.lh, t.da, t.gp, t.xh, t.inv, t.vecs, t.dxs
+        da[...] = dot_tn(lh[...], t.rh[...])
+        high, low = split_two(t.g1)
+        gp[...] = dot_tn(lh[2 * r : 2 * r + 2 * PAD, :], jnp.concatenate([high, low], 0))
+        step = STEP_ROWS
+        full = t.real_tokens // step
+
+        def one(rows, carry):
+            z, normed = da[rows, :], xh[rows, :]
+            inner = small_norm_back(z, normed, inv[rows, 0:1], vec[0:1, :])
+            return inner + gp[rows, :], (
+                carry[0] + jnp.sum((z * normed).reshape(step // 8, 8, d), 0),
+                carry[1] + jnp.sum(z.reshape(step // 8, 8, d), 0),
+            )
+
+        def body(index, carry):
+            rows = pl.ds(pl.multiple_of(index * step, step), step)
+            out[rows, :], carry = one(rows, carry)
+            return carry
+
+        zero = jnp.zeros((8, d), F32)
+        carry = lax.fori_loop(0, full, body, (zero, zero))
+        start, rest = full * step, t.real_tokens - full * step
+        if rest:
+            last, carry = one(slice(start, start + step), carry)
+            out[start : start + rest, :] = last[:rest]
+        self.copy_out(t).start()
+        s = t.sums
+        rows = [col_sum(carry[0]), col_sum(carry[1])]
+        rows += [s.pop(name) for name in list(dict(dbq=0, dbv=0, dbo=0, dg2=0, db2=0, dbp=0))]
+        t.vector_rows = jnp.concatenate(rows, 0)
+
+    def vector_sum_begin(self):
+        self.vz[...] = jnp.concatenate([self.ti.vector_rows, self.tt.vector_rows], 1)
+        group = Group(self)
+        for slot, mask in enumerate(Z_PEERS):
+            group.send(self.vz, self.vzr.at[slot], mask)
+        return group
+
+    def vector_sum_middle(self, group):
+        group.wait(self.vzr)
+        self.vp[...] = self.vz[...] + self.vzr[0] + self.vzr[1] + self.vzr[2]
+        group = Group(self)
+        for slot, mask in enumerate(PLANE_PEERS):
+            group.send(self.vp, self.vpr.at[slot], mask)
+        return group
+
+    def vector_sum_end(self, group):
+        group.wait(self.vpr)
+        self.vc[...] = self.vp[...] + self.vpr[0] + self.vpr[1] + self.vpr[2]
+        group = Group(self)
+        group.send(self.vc, self.vcr, 1)
+        return group
+
+    def vector_sum_done(self, group):
+        group.wait(self.vcr)
+        total = self.vc[...] + self.vcr[...]
+        at = 0
+        for t in (self.ti, self.tt):
+            d, rows = t.width, t.rows
+            values = total[:, at : at + d]
+            at += d
+            high, rest = split_two(values)
+            rest_high, rest_low = split_two(values - high.astype(F32))
+            pick = iota((d, 128), 0) == iota((d, 128), 1) + self.me * rows
+            pick = pick.astype(F32).astype(BF16)
+            picked = dot(high, pick) + dot(rest_high, pick) + dot(rest_low, pick)
+            t.d_vec[...] = picked[:, 0:rows]
+
+    def place(self, rows, at):
+        parts = []
+        if at:
+            parts.append(jnp.zeros((at, rows.shape[1]), BF16))
+        parts.append(rows)
+        if 256 - at - rows.shape[0]:
+            parts.append(jnp.zeros((256 - at - rows.shape[0], rows.shape[1]), BF16))
+        return jnp.concatenate(parts, 0)
+
+    def round_one(self, t):
+        r = t.queries
+        t.c_in1.wait(t.in1r.at[0:3])
+        t.c_w.wait(t.wg.at[0:3])
+        t.c_do.wait(t.dog.at[0:3])
+        value = out = proj = 0.0
+        for group in range(4):
+            operand = t.in1r[group].reshape(4 * t.chip_rows, 256)
+            value = value + dot(operand, self.place(expand_heads(t.dog[group]), 0))
+            out = out + dot(operand, self.place(t.wg[group], r))
+            if t.extra:
+                proj = proj + dot(operand, self.place(self.drb[self.core * 4 + group], r + 2 * PAD))
+        parts = [value, out] + ([proj] if t.extra else [])
+        grad = jnp.concatenate(parts, 1).reshape(t.r1f.shape)
+        t.r1f[...] = grad
+        t.r1b[...] = grad.astype(BF16)
+        t.c_r1 = self.to_copies(t, t.r1b, t.r1r)
+
+    def round_two(self, t):
+        r = t.queries
+        t.c_q.wait(t.qg.at[0:3])
+        t.c_in2.wait(t.in2r.at[0:3])
+        t.c_dq.wait(t.dqg.at[0:3])
+        query = key = 0.0
+        for group in range(4):
+            operand = t.in1r[group].reshape(4 * t.chip_rows, 256)
+            query = query + dot(operand, self.place(t.dqg[group], r + PAD))
+            key = key + dot(t.in2r[group].reshape(4 * t.chip_rows, r), expand_heads(t.qg[group]))
+        grad = jnp.concatenate([query, key], 1).reshape(t.r2f.shape)
+        t.r2f[...] = grad
+        t.r2b[...] = grad.astype(BF16)
+        t.c_r2 = self.to_copies(t, t.r2b, t.r2r)
+
+    def rounds_end(self, t):
+        start = pl.multiple_of((1 - self.core) * t.rows, 8)
+        t.c_last = []
+        for group, f, landing, total, last in (
+            (t.c_r1, t.r1f, t.r1r, t.r1s, t.r1p),
+            (t.c_r2, t.r2f, t.r2r, t.r2s, t.r2p),
+        ):
+            group.wait(landing)
+            values = f[t.r]
+            for slot in range(3):
+                values = values + landing[slot].astype(F32)
+            total[...] = values
+            pair = Group(self)
+            pair.send(total.at[pl.ds(start, t.rows)], last, 1)
+            t.c_last.append(pair)
+
+    def rounds_done(self, t):
+        rows, d, b = t.rows, t.width, t.block
+        start = pl.multiple_of(self.core * rows, 8)
+        done = []
+        for pair, total, last in zip(t.c_last, (t.r1s, t.r2s), (t.r1p, t.r2p), strict=True):
+            pair.wait(last)
+            done.append(total[pl.ds(start, rows), :] + last[...])
+        t.d_qkv[:, 0 : 2 * d] = done[1]
+        t.d_qkv[:, 2 * d : 3 * d] = done[0][:, 0:d]
+        t.d_out[...] = done[0][:, d : 2 * d]
+        if t.extra:
+            self.dmap[...] = done[0][:, 2 * d :]
+        t.c_fc.wait(t.gf4)
+        for group in range(4):
+            own, got = t.gf3[group, pl.ds(start, rows), :], t.gf4[group]
+            for half in range(2):
+                values = jnp.where(self.core == half, own, got)
+                for copy in range(4):
+                    device = t.device_of(group, copy, half)
+                    t.d_fc[:, b * device : b * (device + 1)] = values[:, b * copy : b * (copy + 1)]
+
+
+def set_all(target, names, refs):
+    for name, ref in zip(names, refs, strict=True):
+        setattr(target, name, ref)
+
+
+def hand_over(results):
+    count = len(results)
+
+    def kernel(*refs):
+        came, went = refs[3 * count], refs[3 * count + 1]
+        reads = [
+            pltpu.make_async_copy(refs[index], refs[2 * count + index], came.at[index])
+            for index in range(count)
+        ]
+        writes = [
+            pltpu.make_async_copy(refs[2 * count + index], refs[count + index], went.at[index])
+            for index in range(count)
+        ]
+        for read in reads:
+            read.start()
+        for read, write in zip(reads, writes, strict=True):
+            read.wait()
+            write.start()
+        for write in writes:
+            write.wait()
+
+    sems = pltpu.SemaphoreType.DMA((count,))
+    return pl.pallas_call(
+        kernel,
+        out_shape=tuple(jax.ShapeDtypeStruct(value.shape, value.dtype) for value in results),
+        in_specs=[pl.BlockSpec(memory_space=pl.ANY)] * count,
+        out_specs=tuple([pl.BlockSpec(memory_space=pl.ANY)] * count),
+        scratch_shapes=[pltpu.VMEM(value.shape, value.dtype) for value in results] + [sems, sems],
+        compiler_params=pltpu.CompilerParams(vmem_limit_bytes=60 * 2**20),
+        name="hand_over",
+    )(*results)
+
+
+def local_fused(
+    picture_patch_inputs,
+    caption_packed_inputs,
+    picture_attend_entry_weight,
+    picture_attend_exit_weight,
+    picture_widening_weight,
+    picture_narrowing_weight,
+    picture_affine_entries,
+    picture_widening_offset,
+    caption_attend_entry_weight,
+    caption_attend_exit_weight,
+    caption_widening_weight,
+    caption_narrowing_weight,
+    caption_affine_entries,
+    caption_widening_offset,
+    picture_feature_mapping,
+    sharpness_exponent,
+    caption_token_counts,
+    matching_picture_index,
+):
+    n_img, d_img = picture_patch_inputs.shape
+    n_txt, d_txt = caption_packed_inputs.shape
+    images = n_img // TOK_I
+    ti = Tower(
+        True,
+        d_img,
+        n_img,
+        picture_attend_entry_weight.shape[1],
+        picture_widening_offset.shape[1],
+        picture_feature_mapping.shape[1] // 2,
+    )
+    tt = Tower(
+        False, d_txt, n_txt, caption_attend_entry_weight.shape[1], caption_widening_offset.shape[1], 0
+    )
+    img_args = dict(
+        x=picture_patch_inputs,
+        qkv=picture_attend_entry_weight[0],
+        out=picture_attend_exit_weight[0],
+        fc=picture_widening_weight[0],
+        proj=picture_narrowing_weight[0],
+        vec=picture_affine_entries[0],
+        fcb=picture_widening_offset,
+    )
+    txt_args = dict(
+        x=caption_packed_inputs,
+        qkv=caption_attend_entry_weight[0],
+        out=caption_attend_exit_weight[0],
+        fc=caption_widening_weight[0],
+        proj=caption_narrowing_weight[0],
+        vec=caption_affine_entries[0],
+        fcb=caption_widening_offset,
+    )
+    more_args = dict(
+        map=picture_feature_mapping,
+        sharp=sharpness_exponent.reshape(1),
+        counts=caption_token_counts,
+        match=matching_picture_index,
+    )
+
+    def out(*shape):
+        return jax.ShapeDtypeStruct(shape, F32)
+
+    def tower_outs(t):
+        return dict(
+            d_x=out(t.real_tokens, t.width),
+            d_qkv=out(t.rows, 3 * t.width),
+            d_out=out(t.rows, t.width),
+            d_fc=out(t.rows, 32 * t.block),
+            d_proj=out(t.block, t.width),
+            d_vec=out(8, t.rows),
+            d_fcb=out(1, t.block),
+        )
+
+    more_outs = dict(loss=out(1, 1), dls=out(1, 1), dmap=out(ti.rows, 2 * ti.extra))
+    in_vmem, in_smem = pl.BlockSpec(memory_space=pltpu.VMEM), pl.BlockSpec(memory_space=pltpu.SMEM)
+    anywhere = pl.BlockSpec(memory_space=pl.ANY)
+    parts = [
+        (ti, img_args, [in_vmem] * 7),
+        (tt, txt_args, [in_vmem] * 7),
+        (None, more_args, [in_vmem, in_smem, in_smem, in_smem]),
+        (ti, tower_outs(ti), [anywhere] + [in_vmem] * 6),
+        (tt, tower_outs(tt), [anywhere] + [in_vmem] * 6),
+        (None, more_outs, [in_vmem] * 3),
+        (ti, ti.scratch(), None),
+        (tt, tt.scratch(), None),
+        (None, shared_scratch(ti, tt), None),
+        (
+            None,
+            dict(
+                ssem=pltpu.SemaphoreType.DMA((N_SEMS,)),
+                rsem=pltpu.SemaphoreType.DMA((N_SEMS,)),
+                osem=pltpu.SemaphoreType.DMA((2,)),
+            ),
+            None,
+        ),
+    ]
+
+    def kernel(*refs):
+        step = Step(ti, tt, images)
+        at = 0
+        for owner, values, _ in parts:
+            set_all(step if owner is None else owner, values, refs[at : at + len(values)])
+            at += len(values)
+        step.run()
+
+    def joined(chosen, field):
+        return [item for part in chosen for item in (part[field] if field == 2 else part[field].values())]
+
+    results = pl.pallas_call(
+        kernel,
+        out_shape=tuple(joined(parts[3:6], 1)),
+        in_specs=joined(parts[0:3], 2),
+        out_specs=tuple(joined(parts[3:6], 2)),
+        scratch_shapes=joined(parts[6:], 1),
+        compiler_params=pltpu.CompilerParams(
+            collective_id=0, has_side_effects=True, vmem_limit_bytes=60 * 2**20
+        ),
+        name="contrastive_step",
+    )(*joined(parts[0:3], 1))
+    results = hand_over(results)
+    img, txt, (loss, d_scale, d_map) = results[0:7], results[7:14], results[14:17]
+    return (
+        loss.reshape(()),
+        d_scale.reshape(()),
+        img[0],
+        txt[0],
+        img[1][None],
+        img[2][None],
+        img[3][None],
+        img[4][None],
+        img[5][None],
+        img[6],
+        txt[1][None],
+        txt[2][None],
+        txt[3][None],
+        txt[4][None],
+        txt[5][None],
+        txt[6],
+        d_map,
+    )
+
+
 def solution(mesh):
     placed = (
         P("dp", None),
@@ -416,7 +1631,7 @@
         P("dp"),
     )
     return jax.shard_map(
-        local,
+        local_fused if fits(mesh) else local_plain,
         mesh=mesh,
         in_specs=placed,
         out_specs=(

time: 2190 us -> 151 us (0.07)
  waiting for transfers between devices: 1380 us -> 0 us
  blocking collectives: 405 us -> 0 us
  matrix products: 156 us -> 0 us
  Pallas kernels: 0 us -> 149 us
  local copies, waits for them, and re-layouts: 147 us -> 0 us
  starting transfers between devices: 39.6 us -> 0 us
    reduce_scatter x9 -> x0, waiting for transfers between devices: 1130 us -> none  [the longest x1 143 us: local(): lax.psum_scatter(txt_local[2], 'dp', scatter_dimension=1, tiled=True)]
    all_gather x6 -> x0, blocking collectives: 251 us -> none  [the longest x1 45.9 us: gather_first(): lax.all_gather(picture_feature_mapping, 'dp', axis=0, tiled=True)]
    unnamed x38 -> x0, waiting for transfers between devices: 169 us -> none
    dot_general x47 -> x0, matrix products: 156 us -> none  [the longest x2 16.2 us: block_backward(): jnp.einsum('stf,std->fd', activated, branch, preferred_element_type=jnp.f...]
    pallas_call x0 -> x2, Pallas kernels: none -> 149 us  [the longest x1 144 us: local_fused(): pl.pallas_call(kernel, out_shape=tuple(joined(parts[3:6], 1)), in_specs=j...]
    unnamed x2 -> x0, blocking collectives: 115 us -> none
    all_gather x7 -> x0, waiting for transfers between devices: 85.2 us -> none  [the longest x1 57.2 us: gather_first(): lax.all_gather(img_stack[3], 'dp', axis=1, tiled=True)]
    unnamed x261 -> x0, local copies, waits for them, and re-layouts: 54.6 us -> none
  transfers between devices with their start and end apart: 35 -> 0, of which waited for: 13 -> 0; matrix products, arithmetic and copies ran while one was open for 13% -> 0% of each run, Pallas kernels for 0% -> 0%
where the time goes in v2:
time: 151 us
  Pallas kernels  149 us (99%)
    pallas_call x1, Pallas kernels, local_fused(): pl.pallas_call(kernel, out_shape=tuple(joined(parts[3:6], 1)), in_specs=j...  144 us
    pallas_call x1, Pallas kernels, hand_over(): pl.pallas_call(kernel, out_shape=tuple((jax.ShapeDtypeStruct(value.shape,...  4.75 us

profile of v2, /device:TPU:0, one launch (start us, length us, event | category | flops | bytes accessed | tf_op | source)
XLA Modules:
  0.0 150.6 jit_solution(15255583373078339971)
XLA Ops:
  1.3 144.4 %contrastive_step.1 = (f32[600,768]{1,0:T(8,128)}, f32[24,2304]{1,0:T(8,128)}, f32[24,768]{1,0:T(8,128)}, f32[24,3072]{1,0:T(8,128)}, f32[96,768]{1,0:T(8,128)},...) custom-call(bf16[600,768]{1,0:T(8,128)(2,1)} %refs_0_.1, ...), custom_call_target="tpu_custom_call" | custom-call | tf_op jit(solution)/shard_map/contrastive_step/pallas_call | solution.py:1578
  145.7 4.8 %hand_over.1 = (f32[600,768]{1,0:T(8,128)}, f32[24,2304]{1,0:T(8,128)}, f32[24,768]{1,0:T(8,128)}, f32[24,3072]{1,0:T(8,128)}, f32[96,768]{1,0:T(8,128)}, /*inde...) custom-call(f32[600,768]{1,0:T(8,128)} %get-tuple-element.51.refs_0_, ...), custom_call_target="tpu_custom_call" | custom-call | tf_op jit(solution)/shard_map/hand_over/pallas_call | solution.py:1459

commit v3 on v2

--- a/solution.py
+++ b/solution.py
@@ -400,7 +400,8 @@
 BF16 = jnp.bfloat16
 Z_PEERS = (8, 16, 24)
 PLANE_PEERS = (2, 4, 6)
-ALL_PEERS = (1, 2, 3, 4, 5, 6, 7, 8, 9, 16, 17, 24, 25)
+CHIP_PEERS = tuple(range(2, 32, 2))
+ALL_PEERS = (1, 3, 5, 7, 9, 17, 25) + CHIP_PEERS
 PAD = 16
 N_SEMS = 100
 STEP_ROWS = 32
@@ -467,9 +468,39 @@
     return jnp.sum(values, 0, keepdims=True)
 
 
+class Split:
+    def __init__(self, along_z):
+        self.along_z = along_z
+        self.group_peers = Z_PEERS if along_z else PLANE_PEERS
+        self.copy_peers = PLANE_PEERS if along_z else Z_PEERS
+        self.line_peers = (1,) + tuple(mask + core for mask in self.group_peers for core in range(2))
+
+    def stand(self, step):
+        self.g, self.r = (step.zed, step.plane) if self.along_z else (step.plane, step.zed)
+        self.spot = step.core * 4 + self.g
+
+    def chip_of(self, group, copy):
+        return 4 * group + copy if self.along_z else 4 * copy + group
+
+    def device_of(self, group, copy, core):
+        return 2 * self.chip_of(group, copy) + core
+
+    def group_of(self, device):
+        return device // 8 if self.along_z else lax.rem(device // 2, 4)
+
+    def copy_of(self, device):
+        return lax.rem(device // 2, 4) if self.along_z else device // 8
+
+    def chips_of_group(self, ref, group):
+        return ref.at[group] if self.along_z else ref.at[:, group]
+
+    def chips_of_copy(self, ref, copy):
+        return ref.at[:, copy] if self.along_z else ref.at[copy]
+
+
 class Tower:
     def __init__(self, along_z, width, real_tokens, rows, block, extra):
-        self.along_z = along_z
+        self.ff, self.at = Split(along_z), Split(along_z)
         self.width = width
         self.real_tokens = real_tokens
         self.tokens = -(-real_tokens // 128) * 128
@@ -482,28 +513,10 @@
         self.extra = extra
         self.packed = 2 * width + extra + 4 * self.group
         self.row_pad = -(-rows // 16) * 16
-        self.group_peers = Z_PEERS if along_z else PLANE_PEERS
-        self.copy_peers = PLANE_PEERS if along_z else Z_PEERS
-        self.line_peers = (1,) + tuple(mask + core for mask in self.group_peers for core in range(2))
+        self.fold = 1 if rows % 16 == 0 else 2
+        self.tiles = 4 * (self.queries // 128) + 2 * (self.queries % 128 // 64)
         self.sums = {}
-
-    def chip_of(self, group, copy):
-        return 4 * group + copy if self.along_z else 4 * copy + group
-
-    def device_of(self, group, copy, core):
-        return 2 * self.chip_of(group, copy) + core
-
-    def group_of(self, device):
-        return device // 8 if self.along_z else lax.rem(device // 2, 4)
-
-    def copy_of(self, device):
-        return lax.rem(device // 2, 4) if self.along_z else device // 8
-
-    def chips_of_group(self, ref, group):
-        return ref.at[group] if self.along_z else ref.at[:, group]
-
-    def chips_of_copy(self, ref, copy):
-        return ref.at[:, copy] if self.along_z else ref.at[copy]
+        self.c_r1 = self.c_r2 = None
 
     def scratch(self):
         d, n, r, g, b, cr = self.width, self.tokens, self.queries, self.group, self.block, self.chip_rows
@@ -533,12 +546,9 @@
             dcf=v((8, PAD, d), F32),
             dcs=v((8, PAD, d), BF16),
             dcr=v((7, PAD, d), BF16),
-            sc=v((8, PAD, 128), F32),
             u=v((8 * PAD, g), F32),
-            m=v((8 * PAD, g), BF16),
-            gpf=v((4, b, d), F32),
-            gpb=v((4, b, d), BF16),
-            gpr=v((3, b, d), BF16),
+            mt=v((4, b, 8 * PAD), BF16),
+            mtr=v((4, b, 8 * PAD), BF16),
             gff=v((4, 4, cr, g), F32),
             gfb=v((4, 4, cr, g), BF16),
             gfr=v((3, 4, cr, g), BF16),
@@ -546,24 +556,27 @@
             gf3=v((4, cr, g), F32),
             gf3r=v((4, cr, g), BF16),
             gf4=v((4, self.rows, g), F32),
-            in1t=v((4, 4, cr, 256), BF16),
-            in1r=v((4, 4, cr, 256), BF16),
-            in2t=v((4, 4, cr, r), BF16),
-            in2r=v((4, 4, cr, r), BF16),
-            qg=v((4, PAD, d), BF16),
+            in1t=v((self.tiles, 4, cr, 128), BF16),
+            in1r=v((4, self.tiles, cr, 128), BF16),
+            in2t=v((self.tiles, 4, cr, 128), BF16),
+            in2r=v((4, self.tiles, cr, 128), BF16),
+            ag=v((4, PAD, d), BF16),
             wg=v((4, PAD, d), BF16),
-            dog=v((4, PAD, d), BF16),
             dqg=v((4, PAD, d), BF16),
+            pg=v((4, PAD, d), BF16),
+            og=v((4, PAD, d), BF16),
+            in3t=v((4, 4, cr, 8 * PAD), BF16),
+            in4t=v((4, 4, cr, 8 * PAD), BF16),
             r1f=v((4, cr, c1), F32),
-            r1b=v((4, cr, c1), BF16),
-            r1r=v((3, cr, c1), BF16),
-            r1s=v((cr, c1), F32),
-            r1p=v((self.rows, c1), F32),
+            r1p=v((4, self.rows, c1), F32),
+            r1s=v((4, self.rows, c1), F32),
+            r1b=v((4, self.fold * self.rows, c1 // self.fold), BF16),
+            r1r=v((3, self.fold * self.rows, c1 // self.fold), BF16),
             r2f=v((4, cr, c2), F32),
-            r2b=v((4, cr, c2), BF16),
-            r2r=v((3, cr, c2), BF16),
-            r2s=v((cr, c2), F32),
-            r2p=v((self.rows, c2), F32),
+            r2p=v((4, self.rows, c2), F32),
+            r2s=v((4, self.rows, c2), F32),
+            r2b=v((4, self.fold * self.rows, c2 // self.fold), BF16),
+            r2r=v((3, self.fold * self.rows, c2 // self.fold), BF16),
             da=v((n, d), F32),
             gp=v((n, d), F32),
             dxs=v((self.real_tokens, d), F32),
@@ -575,7 +588,6 @@
 
 def shared_scratch(ti, tt):
     v = pltpu.VMEM
-    wide = ti.width + tt.width
     e = tt.width
     rows = 32 * PAD
     return dict(
@@ -585,12 +597,10 @@
         gtxt=v((rows, rows), F32),
         gimg=v((rows, rows), F32),
         drb=v((8, PAD, e), BF16),
-        vz=v((8, wide), F32),
-        vzr=v((3, 8, wide), F32),
-        vp=v((8, wide), F32),
-        vpr=v((3, 8, wide), F32),
-        vc=v((8, wide), F32),
-        vcr=v((8, wide), F32),
+        va=v((8, ti.width + tt.width), F32),
+        var=v((8, ti.width + tt.width), F32),
+        vs=v((16, 8, 128), F32),
+        vl=v((16, 8, 128), F32),
     )
 
 
@@ -690,8 +700,8 @@
         self.plane = lax.rem(me // 2, 4)
         self.zed = me // 8
         for t in (ti, tt):
-            t.g, t.r = (self.zed, self.plane) if t.along_z else (self.plane, self.zed)
-            t.spot = self.core * 4 + t.g
+            t.ff.stand(self)
+            t.at.stand(self)
         self.used = 0
         self.groups = []
 
@@ -723,39 +733,39 @@
             self, slot, lambda count: buffer.at[self.core, 0 : count * rows], buffer.at[self.core], True
         )
 
-    def line_gather(self, t, buffer):
+    def line_gather(self, split, buffer):
         group = Group(self)
-        here = buffer.at[t.spot]
-        for mask in t.line_peers:
+        here = buffer.at[split.spot]
+        for mask in split.line_peers:
             group.send(here, here, mask)
         return group
 
-    def line_scatter(self, t, parts, landing):
+    def line_scatter(self, split, parts, landing):
         group = Group(self)
-        for slot, mask in enumerate(t.line_peers):
+        for slot, mask in enumerate(split.line_peers):
             peer = self.at_peer(mask)
-            group.send(parts.at[lax.rem(peer, 2) * 4 + t.group_of(peer)], landing.at[slot], mask)
+            group.send(parts.at[lax.rem(peer, 2) * 4 + split.group_of(peer)], landing.at[slot], mask)
         return group
 
-    def to_group(self, t, block, landing):
+    def to_group(self, split, block, landing):
         group = Group(self)
-        for mask in t.group_peers:
-            group.send(t.chips_of_group(block, t.group_of(self.at_peer(mask))), landing.at[t.g], mask)
-        landing[t.g] = t.chips_of_group(block, t.g)[...]
+        for mask in split.group_peers:
+            group.send(block.at[:, split.group_of(self.at_peer(mask))], landing.at[split.g], mask)
+        landing[split.g] = block[:, split.g]
         return group
 
-    def share_group(self, t, buffer, values):
+    def share_group(self, split, buffer, values):
         group = Group(self)
-        buffer[t.g] = values
-        here = buffer.at[t.g]
-        for mask in t.group_peers:
+        buffer[split.g] = values
+        here = buffer.at[split.g]
+        for mask in split.group_peers:
             group.send(here, here, mask)
         return group
 
-    def to_copies(self, t, block, landing):
+    def to_copies(self, split, block, landing):
         group = Group(self)
-        for slot, mask in enumerate(t.copy_peers):
-            group.send(block.at[t.copy_of(self.at_peer(mask))], landing.at[slot], mask)
+        for slot, mask in enumerate(split.copy_peers):
+            group.send(block.at[split.copy_of(self.at_peer(mask))], landing.at[slot], mask)
         return group
 
     def run(self):
@@ -787,43 +797,45 @@
             t.first.begin_z()
             t.first.begin_plane()
         for t in both:
-            t.second.begin_z()
-        for t in both:
-            self.widen_begin(t)
-        third.begin_z()
+            self.narrow_begin(t)
         self.standardize(tt)
         vectors.middle()
+        self.standardize(ti)
+        for t in both:
+            t.first.relay_own()
+        for t in both:
+            t.second.begin_plane()
         for t in both:
             t.first.middle()
         for t in both:
-            t.first.relay_own()
-        for t in both:
-            t.second.begin_plane()
-        for t in both:
-            t.second.middle()
-        self.standardize(ti)
+            t.second.begin_z()
         for t in both:
             t.first.relay()
+        vectors.end()
         for t in both:
             t.second.relay_own()
-        for t in both:
-            self.widen_middle(t)
-        vectors.end()
-        third.begin_plane()
-        third.middle()
         vectors.done()
         self.unpack_vectors()
         self.queries(ti)
         self.queries(tt)
         for t in both:
+            t.second.middle()
+        for t in both:
+            self.widen_begin(t)
+        third.begin_z()
+        for t in both:
             t.first.end()
+        third.begin_plane()
         for t in both:
             t.second.relay()
+        for t in both:
+            t.first.done()
+            self.attend(t)
+            self.early_operands(t)
+        for t in both:
+            self.widen_middle(t)
+        third.middle()
         third.relay_own()
-        ti.first.done()
-        self.attend(ti)
-        tt.first.done()
-        self.attend(tt)
         for t in both:
             t.second.end()
         third.relay()
@@ -831,6 +843,8 @@
             t.second.done()
             self.mix(t)
         third.end()
+        for t in both:
+            t.c_o = self.share_group(t.at, t.og, t.o)
         for t in both:
             self.feed(t)
         third.done()
@@ -845,42 +859,44 @@
         )
         rows.begin_z()
         rows.begin_plane()
-        for t in both:
-            t.scales = self.line_gather(t, t.sc)
+        ti.c_p = self.share_group(ti.at, ti.pg, self.pooled)
         rows.middle()
-        for t in both:
-            self.early_operands(t)
         rows.end()
         rows.done()
-        for t in both:
-            t.scales.wait(t.sc.at[0:7])
         self.contrast()
         for t in both:
             self.feed_back(t)
         for t in both:
             self.feed_weights(t)
         for t in both:
+            self.feed_proj(t)
+        for t in both:
             self.attend_back(t)
         for t in both:
             self.attend_back_end(t)
         for t in both:
             self.input_gradient(t)
-        copies = self.vector_sum_begin()
+        self.vector_sum_begin()
+        for t in both:
+            self.round_one(t)
+        self.vector_sum_spread()
         for t in both:
             self.feed_weights_middle(t)
         for t in both:
-            self.round_one(t)
-        copies = self.vector_sum_middle(copies)
+            self.round_spread(t, 0)
         for t in both:
             self.round_two(t)
-        copies = self.vector_sum_end(copies)
+        for t in both:
+            self.round_spread(t, 1)
         for t in both:
             self.feed_weights_end(t)
-        for t in both:
-            self.rounds_end(t)
-        self.vector_sum_done(copies)
-        for t in both:
-            self.rounds_done(t)
+        self.vector_sum_done()
+        for t in both:
+            self.round_end(t, 0)
+        for t in both:
+            self.feed_weights_done(t)
+        for t in both:
+            self.round_end(t, 1)
         for t in both:
             self.copy_out(t).wait()
         for group in self.groups:
@@ -911,7 +927,7 @@
             for group in range(4):
                 pieces = []
                 for copy in range(4):
-                    device = t.device_of(group, copy, half)
+                    device = t.ff.device_of(group, copy, half)
                     pieces.append(values[:, b * device : b * (device + 1)])
                 start = base + group * t.group
                 pk[half, :, start : start + t.group] = jnp.concatenate(pieces, 1).astype(BF16)
@@ -950,7 +966,7 @@
                     t.vecs[:, rows * device : rows * (device + 1)] = block[0:8, at : at + rows]
         for t, row in ((self.ti, 8), (self.tt, 9)):
             for copy in range(4):
-                block = vb[self.core, t.chip_of(t.g, copy)].astype(F32)
+                block = vb[self.core, t.ff.chip_of(t.ff.g, copy)].astype(F32)
                 b = t.block
                 t.bias[0:1, b * copy : b * (copy + 1)] = block[row : row + 1, 0:b]
 
@@ -1007,19 +1023,22 @@
 
     def widen_begin(self, t):
         t.widen = Group(self)
-        for mask in t.group_peers:
-            t.widen.send(t.mf.at[t.group_of(self.at_peer(mask))], t.fa.at[self.zed, self.plane], mask)
-        t.fa[self.zed, self.plane] = t.mf[t.g]
+        for mask in t.ff.group_peers:
+            t.widen.send(t.mf.at[t.ff.group_of(self.at_peer(mask))], t.fa.at[self.zed, self.plane], mask)
+        t.fa[self.zed, self.plane] = t.mf[t.ff.g]
 
     def widen_middle(self, t):
         t.widen.wait(t.mf.at[0:3])
-        t.widen, t.narrow = Group(self), Group(self)
-        part = t.chips_of_copy(t.fa, t.r)
-        for mask in t.copy_peers:
+        t.widen = Group(self)
+        part = t.ff.chips_of_copy(t.fa, t.ff.r)
+        for mask in t.ff.copy_peers:
             t.widen.send(part, part, mask)
-        for mask in t.copy_peers:
-            t.narrow.send(t.proj, t.wp.at[t.r], mask)
-        t.wp[t.r] = t.proj[...]
+
+    def narrow_begin(self, t):
+        t.narrow = Group(self)
+        for mask in t.ff.copy_peers:
+            t.narrow.send(t.proj, t.wp.at[t.ff.r], mask)
+        t.wp[t.ff.r] = t.proj[...]
 
     def queries(self, t):
         a, xh, vec = t.a, t.xh, t.vecs
@@ -1079,8 +1098,8 @@
         t.o = context
         t.h1 = t.x0 + (dot(context, w2[1]) + vec[4:5, :])
         t.xh2, t.inv2, second = small_norm(t.h1, vec[5:6, :], vec[6:7, :])
-        t.ci[t.spot] = second.astype(BF16)
-        t.line = self.line_gather(t, t.ci)
+        t.ci[t.ff.spot] = second.astype(BF16)
+        t.line = self.line_gather(t.ff, t.ci)
 
     def feed(self, t):
         d, g = t.width, t.group
@@ -1089,17 +1108,22 @@
         t.line.wait(t.ci.at[0:7])
         c = t.ci[...].reshape(8 * PAD, d)
         up = dot(c, t.fa[...].reshape(d, g)) + t.bias[0:1, :]
-        active = (up * jax.nn.sigmoid(1.702 * up)).astype(BF16)
+        active = up * jax.nn.sigmoid(1.702 * up)
         t.u[...] = up
-        t.m[...] = active
+        t.mt[...] = active.T.astype(BF16).reshape(t.mt.shape)
+        active = active.astype(BF16)
         part = dot(active, t.wp[...].reshape(g, d)).reshape(8, PAD, d)
         t.hpf[...] = part
         t.hps[...] = part.astype(BF16)
-        t.line = self.line_scatter(t, t.hps, t.hr)
+        t.line = self.line_scatter(t.ff, t.hps, t.hr)
+        t.mtr[t.ff.r] = t.mt[t.ff.r]
+        t.c_m = Group(self)
+        for mask in t.ff.copy_peers:
+            t.c_m.send(t.mt.at[t.ff.copy_of(self.at_peer(mask))], t.mtr.at[t.ff.r], mask)
 
     def line_total(self, t, own, landing):
         t.line.wait(landing)
-        total = own[t.spot]
+        total = own[t.ff.spot]
         for slot in range(7):
             total = total + landing[slot].astype(F32)
         return total
@@ -1113,19 +1137,56 @@
             self.pooled = hidden.astype(BF16)
             raw = jnp.concatenate([dot(self.pooled, self.w3[0]), dot(self.pooled, self.w3[1])], 1)
         scale = lax.rsqrt(jnp.sum(raw * raw, -1, keepdims=True) + 1e-06)
-        self.eb[which, self.core, self.chip] = (raw * scale).astype(BF16)
-        t.sc[t.spot] = jnp.broadcast_to(scale, (PAD, 128))
+        row, lane = iota(raw.shape, 0), iota(raw.shape, 1)
+        across = col_sum(jnp.where(row == lane, scale, 0.0))
+        high = across.astype(BF16).astype(F32)
+        block = jnp.where(row == self.images, high, raw * scale)
+        block = jnp.where(row == self.images + 1, across - high, block)
+        self.eb[which, self.core, self.chip] = block.astype(BF16)
+
+    def by_rows(self, t, values, buffer):
+        turned = values.T.reshape(4, 4, t.chip_rows, t.queries)
+        whole = t.queries // 128
+        for tile in range(whole):
+            part = turned[:, :, :, 128 * tile : 128 * (tile + 1)].astype(BF16)
+            for copy in range(4):
+                buffer[4 * tile + copy] = part[:, copy] if t.at.along_z else part[copy]
+        if t.queries % 128:
+            rest = turned[:, :, :, 128 * whole :]
+            for pair in range(2):
+                if t.at.along_z:
+                    parts = [rest[:, 2 * pair], rest[:, 2 * pair + 1]]
+                else:
+                    parts = [rest[2 * pair], rest[2 * pair + 1]]
+                buffer[4 * whole + pair] = jnp.concatenate(parts, 2).astype(BF16)
+
+    def times_heads(self, t, landing, rows, out, start):
+        cr, d = t.chip_rows, t.width
+        whole = t.queries // 128
+        total, paired = 0.0, 0.0
+        for group in range(4):
+            wide = expand_heads(rows[PAD * group : PAD * (group + 1)])
+            for tile in range(whole):
+                operand = landing[group, 4 * tile : 4 * (tile + 1)].reshape(4 * cr, 128)
+                total = total + dot(operand, wide[128 * tile : 128 * (tile + 1)])
+            if t.queries % 128:
+                rest = wide[128 * whole :]
+                blank = jnp.zeros_like(rest)
+                rest = jnp.concatenate(
+                    [jnp.concatenate([rest, blank], 0), jnp.concatenate([blank, rest], 0)], 1
+                )
+                paired = paired + dot(landing[group, 4 * whole : 4 * whole + 2].reshape(2 * cr, 128), rest)
+        for z in range(4):
+            values = total[cr * z : cr * (z + 1)]
+            if t.queries % 128:
+                pair = paired[cr * (z // 2) : cr * (z // 2 + 1)]
+                values = values + pair[:, d * (z % 2) : d * (z % 2 + 1)]
+            out[z, :, start : start + d] = values
 
     def early_operands(self, t):
-        d, r = t.width, t.queries
-        parts = [t.pa, t.o.astype(F32), t.a0.astype(F32)]
-        if t is self.ti:
-            parts.append(self.pooled.astype(F32))
-        rest = 256 - r - PAD * (len(parts) - 1)
-        parts.append(jnp.zeros((rest, d), F32))
-        t.in1t[...] = jnp.concatenate(parts, 0).T.astype(BF16).reshape(4, 4, t.chip_rows, 256)
-        t.c_in1 = self.to_group(t, t.in1t, t.in1r)
-        t.c_q = self.share_group(t, t.qg, t.q)
+        self.by_rows(t, t.pa, t.in1t)
+        t.c_in1 = self.to_group(t.at, t.in1t, t.in1r)
+        t.c_a = self.share_group(t.at, t.ag, t.a0)
 
     def contrast(self):
         eb, gtxt, gimg = self.eb, self.gtxt, self.gimg
@@ -1156,25 +1217,41 @@
         self.dls[...] = whole(grad * safe)
         gtxt[...] = grad
         gimg[...] = grad.T
-        for which, t, rows, others in ((0, self.ti, gimg, e_txt), (1, self.tt, gtxt, e_img)):
-            parts, own = [], []
-            for core in range(2):
-                for group in range(4):
-                    chip = t.chip_of(group, t.r)
-                    start = pl.multiple_of((core * 16 + chip) * PAD, PAD)
-                    parts.append(rows[pl.ds(start, PAD), :])
-                    own.append(eb[which, core, chip].astype(F32))
-            part, unit = jnp.concatenate(parts, 0), jnp.concatenate(own, 0)
-            scale = t.sc[...].reshape(8 * PAD, 128)[:, 0:1]
-            high, low = split_two(part)
-            d_unit = sharp * (dot(high, others) + dot(low, others))
-            d_raw = scale * (d_unit - unit * jnp.sum(d_unit * unit, -1, keepdims=True))
+        for t in (self.ti, self.tt):
+            d_raw = self.raw_gradient(t, t.ff.r)
             if t is self.ti:
-                w3, half = self.w3, t.extra
-                rounded = d_raw.astype(BF16)
+                d_raw, rounded = self.through_map(d_raw)
                 self.drb[...] = rounded.reshape(self.drb.shape)
-                d_raw = dot_nt(rounded[:, 0:half], w3[0]) + dot_nt(rounded[:, half : 2 * half], w3[1])
             t.g2[...] = d_raw.reshape(t.g2.shape)
+
+    def raw_gradient(self, t, copy):
+        eb = self.eb
+        which, rows, others = (0, self.gimg, eb[1]) if t is self.ti else (1, self.gtxt, eb[0])
+        others = others.reshape(32 * PAD, eb.shape[-1])
+        sharp = jnp.exp(jnp.full((8, 128), self.sharp[0], F32))[0:1, 0:1]
+        parts, units, scales = [], [], []
+        for core in range(2):
+            for group in range(4):
+                chip = t.ff.chip_of(group, copy)
+                start = (core * 16 + chip) * PAD
+                if not isinstance(start, int):
+                    start = pl.multiple_of(start, PAD)
+                parts.append(rows[pl.ds(start, PAD), :])
+                block = eb[which, core, chip].astype(F32)
+                units.append(block)
+                row, lane = iota((PAD, 128), 0), iota((PAD, 128), 1)
+                spare = (row >= self.images) & (row < self.images + 2)
+                across = col_sum(jnp.where(spare, block[:, 0:128], 0.0))
+                scales.append(jnp.sum(jnp.where(row == lane, across, 0.0), 1, keepdims=True))
+        part, unit, scale = (jnp.concatenate(pieces, 0) for pieces in (parts, units, scales))
+        high, low = split_two(part)
+        d_unit = sharp * (dot(high, others) + dot(low, others))
+        return scale * (d_unit - unit * jnp.sum(d_unit * unit, -1, keepdims=True))
+
+    def through_map(self, d_raw):
+        w3, half = self.w3, self.ti.extra
+        rounded = d_raw.astype(BF16)
+        return dot_nt(rounded[:, 0:half], w3[0]) + dot_nt(rounded[:, half : 2 * half], w3[1]), rounded
 
     def feed_back(self, t):
         d, g = t.width, t.group
@@ -1186,54 +1263,55 @@
         part = dot_nt(t.du, t.fa[...].reshape(d, g)).reshape(8, PAD, d)
         t.dcf[...] = part
         t.dcs[...] = part.astype(BF16)
-        t.line = self.line_scatter(t, t.dcs, t.dcr)
+        t.line = self.line_scatter(t.ff, t.dcs, t.dcr)
 
     def feed_weights(self, t):
-        d, g, b, cr = t.width, t.group, t.block, t.chip_rows
+        d, g, cr = t.width, t.group, t.chip_rows
         grad = dot_tn(t.ci[...].reshape(8 * PAD, d), t.du).reshape(4, 4, cr, g)
         t.gff[...] = grad
         t.gfb[...] = grad.astype(BF16)
-        t.c_wide, t.c_narrow, t.c_bias = Group(self), Group(self), Group(self)
-        for slot, mask in enumerate(t.copy_peers):
-            t.c_wide.send(t.chips_of_copy(t.gfb, t.copy_of(self.at_peer(mask))), t.gfr.at[slot], mask)
-        grad = dot_tn(t.m[...], t.y).reshape(4, b, d)
-        t.gpf[...] = grad
-        t.gpb[...] = grad.astype(BF16)
+        t.c_wide, t.c_bias = Group(self), Group(self)
         t.dbs[...] = jnp.broadcast_to(col_sum(t.du.astype(F32)), (8, g))
-        for slot, mask in enumerate(t.copy_peers):
-            t.c_narrow.send(t.gpb.at[t.copy_of(self.at_peer(mask))], t.gpr.at[slot], mask)
+        for slot, mask in enumerate(t.ff.copy_peers):
+            copy = t.ff.copy_of(self.at_peer(mask))
+            t.c_wide.send(t.ff.chips_of_copy(t.gfb, copy), t.gfr.at[slot], mask)
             t.c_bias.send(t.dbs, t.dbr.at[slot], mask)
+
+    def feed_proj(self, t):
+        t.c_m.wait(t.mtr.at[0:3])
+        total = 0.0
+        for copy in range(4):
+            d_raw = self.raw_gradient(t, copy)
+            if t is self.ti:
+                d_raw = self.through_map(d_raw)[0]
+            total = total + dot(t.mtr[copy], d_raw.astype(BF16))
+        t.d_proj[...] = total
 
     def feed_weights_middle(self, t):
         b = t.block
         t.c_wide.wait(t.gfr)
-        total = t.chips_of_copy(t.gff, t.r)[...]
+        total = t.ff.chips_of_copy(t.gff, t.ff.r)[...]
         for slot in range(3):
             total = total + t.gfr[slot].astype(F32)
         t.gf2[...] = total.astype(BF16)
         t.gf3[...] = total
         t.c_line = Group(self)
-        for mask in t.group_peers:
-            t.c_line.send(t.gf2.at[t.group_of(self.at_peer(mask))], t.gf3r.at[t.g], mask)
-        t.c_narrow.wait(t.gpr)
-        total = t.gpf[t.r]
-        for slot in range(3):
-            total = total + t.gpr[slot].astype(F32)
-        t.d_proj[...] = total
+        for mask in t.ff.group_peers:
+            t.c_line.send(t.gf2.at[t.ff.group_of(self.at_peer(mask))], t.gf3r.at[t.ff.g], mask)
         t.c_bias.wait(t.dbr)
         bias = t.dbs[0:1, :]
         for slot in range(3):
             bias = bias + t.dbr[slot, 0:1, :]
         mine = jnp.zeros((1, b), F32)
         for copy in range(4):
-            mine = jnp.where(t.r == copy, bias[:, b * copy : b * (copy + 1)], mine)
+            mine = jnp.where(t.ff.r == copy, bias[:, b * copy : b * (copy + 1)], mine)
         t.d_fcb[...] = mine
 
     def feed_weights_end(self, t):
         t.c_line.wait(t.gf2.at[0:3])
-        own = t.gf3[t.g]
+        own = t.gf3[t.ff.g]
         for group in range(4):
-            t.gf3[group] = jnp.where(t.g == group, own, t.gf3r[group].astype(F32))
+            t.gf3[group] = jnp.where(t.ff.g == group, own, t.gf3r[group].astype(F32))
         start = pl.multiple_of((1 - self.core) * t.rows, 8)
         t.c_fc = Group(self)
         t.c_fc.send(t.gf3.at[:, pl.ds(start, t.rows)], t.gf4, 1)
@@ -1241,7 +1319,7 @@
     def attend_back(self, t):
         vec = t.vecs
         total = self.line_total(t, t.dcf, t.dcr)
-        g2 = t.g2[t.spot]
+        g2 = t.g2[t.ff.spot]
         t.g1 = g2 + small_norm_back(total, t.xh2, t.inv2, vec[5:6, :])
         branch = t.g1.astype(BF16)
         t.do = dot_nt(branch, t.w2[1]).astype(BF16)
@@ -1252,8 +1330,7 @@
             db2=col_sum(total),
             dbp=col_sum(g2.astype(BF16).astype(F32)),
         )
-        t.c_w = self.share_group(t, t.wg, branch)
-        t.c_do = self.share_group(t, t.dog, t.do)
+        t.c_w = self.share_group(t.at, t.wg, branch)
 
     def attend_back_end(self, t):
         r, w1, a, lh, rh = t.queries, t.w1, t.a, t.lh, t.rh
@@ -1266,10 +1343,10 @@
         d_scores = (d_scores.astype(F32) * 0.125).astype(BF16)
         lh[0:r, :] = d_scores
         moved = dot(d_scores, a[...])
-        t.in2t[...] = moved.T.astype(BF16).reshape(t.in2t.shape)
-        t.c_in2 = self.to_group(t, t.in2t, t.in2r)
+        self.by_rows(t, moved, t.in2t)
+        t.c_in2 = self.to_group(t.at, t.in2t, t.in2r)
         d_query = join_heads(dot(moved.astype(BF16), w1[1])).astype(BF16)
-        t.c_dq = self.share_group(t, t.dqg, d_query)
+        t.c_dq = self.share_group(t.at, t.dqg, d_query)
         t.sums.update(dbq=col_sum(d_query.astype(F32)))
         high, low = split_two(dot_nt(d_query, w1[0]))
         rh[2 * r : 2 * r + PAD, :] = high
@@ -1310,122 +1387,124 @@
         s = t.sums
         rows = [col_sum(carry[0]), col_sum(carry[1])]
         rows += [s.pop(name) for name in list(dict(dbq=0, dbv=0, dbo=0, dg2=0, db2=0, dbp=0))]
-        t.vector_rows = jnp.concatenate(rows, 0)
+        start = 0 if t is self.ti else self.ti.width
+        self.va[:, start : start + d] = jnp.concatenate(rows, 0)
 
     def vector_sum_begin(self):
-        self.vz[...] = jnp.concatenate([self.ti.vector_rows, self.tt.vector_rows], 1)
-        group = Group(self)
-        for slot, mask in enumerate(Z_PEERS):
-            group.send(self.vz, self.vzr.at[slot], mask)
-        return group
-
-    def vector_sum_middle(self, group):
-        group.wait(self.vzr)
-        self.vp[...] = self.vz[...] + self.vzr[0] + self.vzr[1] + self.vzr[2]
-        group = Group(self)
-        for slot, mask in enumerate(PLANE_PEERS):
-            group.send(self.vp, self.vpr.at[slot], mask)
-        return group
-
-    def vector_sum_end(self, group):
-        group.wait(self.vpr)
-        self.vc[...] = self.vp[...] + self.vpr[0] + self.vpr[1] + self.vpr[2]
-        group = Group(self)
-        group.send(self.vc, self.vcr, 1)
-        return group
-
-    def vector_sum_done(self, group):
-        group.wait(self.vcr)
-        total = self.vc[...] + self.vcr[...]
-        at = 0
-        for t in (self.ti, self.tt):
-            d, rows = t.width, t.rows
-            values = total[:, at : at + d]
-            at += d
-            high, rest = split_two(values)
-            rest_high, rest_low = split_two(values - high.astype(F32))
-            pick = iota((d, 128), 0) == iota((d, 128), 1) + self.me * rows
-            pick = pick.astype(F32).astype(BF16)
-            picked = dot(high, pick) + dot(rest_high, pick) + dot(rest_low, pick)
-            t.d_vec[...] = picked[:, 0:rows]
-
-    def place(self, rows, at):
-        parts = []
-        if at:
-            parts.append(jnp.zeros((at, rows.shape[1]), BF16))
-        parts.append(rows)
-        if 256 - at - rows.shape[0]:
-            parts.append(jnp.zeros((256 - at - rows.shape[0], rows.shape[1]), BF16))
-        return jnp.concatenate(parts, 0)
+        self.c_vec = Group(self)
+        self.c_vec.send(self.va, self.var, 1)
+
+    def vector_sum_spread(self):
+        self.c_vec.wait(self.var)
+        total = self.va[...] + self.var[...]
+        for chip in range(16):
+            pieces, at = [], 0
+            for t in (self.ti, self.tt):
+                cols = t.chip_rows
+                start = at + chip * cols
+                pieces += [total[:, start : start + cols], jnp.zeros((8, 64 - cols), F32)]
+                at += t.width
+            self.vs[chip] = jnp.concatenate(pieces, 1)
+        self.c_vec = Group(self)
+        for mask in CHIP_PEERS:
+            self.c_vec.send(self.vs.at[self.at_peer(mask) // 2], self.vl.at[self.chip], mask)
+        self.vl[self.chip] = self.vs[self.chip]
+
+    def vector_sum_done(self):
+        self.c_vec.wait(self.vl.at[0:15])
+        total = jnp.sum(self.vl[...], 0)
+        for t, lane in ((self.ti, 0), (self.tt, 64)):
+            rows = t.rows
+            halves = [total[:, lane + rows * core : lane + rows * (core + 1)] for core in range(2)]
+            t.d_vec[...] = jnp.where(self.core == 0, halves[0], halves[1])
+
+    def turn_members(self, t, first, second, buffer):
+        d = t.width
+        rows = [part[...].reshape(4 * PAD, d) for part in (first, second)]
+        buffer[...] = jnp.concatenate(rows, 0).astype(F32).T.astype(BF16).reshape(buffer.shape)
+        return t.at.chips_of_group(buffer, t.at.g)[...].reshape(4 * t.chip_rows, 8 * PAD)
 
     def round_one(self, t):
-        r = t.queries
         t.c_in1.wait(t.in1r.at[0:3])
         t.c_w.wait(t.wg.at[0:3])
-        t.c_do.wait(t.dog.at[0:3])
-        value = out = proj = 0.0
-        for group in range(4):
-            operand = t.in1r[group].reshape(4 * t.chip_rows, 256)
-            value = value + dot(operand, self.place(expand_heads(t.dog[group]), 0))
-            out = out + dot(operand, self.place(t.wg[group], r))
+        t.c_o.wait(t.og.at[0:3])
+        t.c_a.wait(t.ag.at[0:3])
+        d, cr = t.width, t.chip_rows
+        members = 4 * PAD
+        branch = t.wg[...].reshape(members, d)
+        self.times_heads(t, t.in1r, dot_nt(branch, t.w2[1]).astype(BF16), t.r1f, 0)
+        t.in3 = self.turn_members(t, t.og, t.ag, t.in3t)
+        out = dot(t.in3, jnp.concatenate([branch, jnp.zeros_like(branch)], 0))
+        t.r1f[:, :, d : 2 * d] = out.reshape(4, cr, d)
+        if t.extra:
+            t.c_p.wait(t.pg.at[0:3])
+            operand = self.turn_members(t, t.pg, t.pg, t.in4t)
+            units = self.drb[pl.ds(self.core * 4, 4)].reshape(members, 2 * t.extra)
+            proj = dot(operand, jnp.concatenate([units, jnp.zeros_like(units)], 0))
+            t.r1f[:, :, 2 * d :] = proj.reshape(4, cr, 2 * t.extra)
+        t.c_r1 = self.round_pair(t, t.r1f, t.r1p)
+
+    def round_two(self, t):
+        t.c_in2.wait(t.in2r.at[0:3])
+        d, cr = t.width, t.chip_rows
+        members = 4 * PAD
+        query = dot(t.ag[...].reshape(members, d), t.w1[0]) + t.vecs[2:3, :]
+        self.times_heads(t, t.in2r, query.astype(BF16), t.r2f, d)
+        t.c_dq.wait(t.dqg.at[0:3])
+        d_query = t.dqg[...].reshape(members, d)
+        d_query = jnp.concatenate([jnp.zeros_like(d_query), d_query], 0)
+        t.r2f[:, :, 0:d] = dot(t.in3, d_query).reshape(4, cr, d)
+        t.c_r2 = self.round_pair(t, t.r2f, t.r2p)
+
+    def round_pair(self, t, grad, landing):
+        start = pl.multiple_of((1 - self.core) * t.rows, 8)
+        group = Group(self)
+        group.send(grad.at[:, pl.ds(start, t.rows)], landing, 1)
+        return group
+
+    def round_spread(self, t, which):
+        group, grad, came, total, packed, landing = (
+            (t.c_r1, t.r1f, t.r1p, t.r1s, t.r1b, t.r1r),
+            (t.c_r2, t.r2f, t.r2p, t.r2s, t.r2b, t.r2r),
+        )[which]
+        group.wait(came)
+        start = pl.multiple_of(self.core * t.rows, 8)
+        values = grad[:, pl.ds(start, t.rows), :] + came[...]
+        total[...] = values
+        cols = values.shape[2] // t.fold
+        pieces = [values[:, :, cols * part : cols * (part + 1)] for part in range(t.fold)]
+        packed[...] = jnp.concatenate(pieces, 1).astype(BF16)
+        group = self.to_copies(t.at, packed, landing)
+        if which:
+            t.c_r2 = group
+        else:
+            t.c_r1 = group
+
+    def round_end(self, t, which):
+        group, total, landing = ((t.c_r1, t.r1s, t.r1r), (t.c_r2, t.r2s, t.r2r))[which]
+        group.wait(landing)
+        arrived = landing[0].astype(F32) + landing[1].astype(F32) + landing[2].astype(F32)
+        pieces = [arrived[t.rows * part : t.rows * (part + 1)] for part in range(t.fold)]
+        values = total[t.at.r] + jnp.concatenate(pieces, 1)
+        d = t.width
+        if which:
+            t.d_qkv[:, 0 : 2 * d] = values
+        else:
+            t.d_qkv[:, 2 * d : 3 * d] = values[:, 0:d]
+            t.d_out[...] = values[:, d : 2 * d]
             if t.extra:
-                proj = proj + dot(operand, self.place(self.drb[self.core * 4 + group], r + 2 * PAD))
-        parts = [value, out] + ([proj] if t.extra else [])
-        grad = jnp.concatenate(parts, 1).reshape(t.r1f.shape)
-        t.r1f[...] = grad
-        t.r1b[...] = grad.astype(BF16)
-        t.c_r1 = self.to_copies(t, t.r1b, t.r1r)
-
-    def round_two(self, t):
-        r = t.queries
-        t.c_q.wait(t.qg.at[0:3])
-        t.c_in2.wait(t.in2r.at[0:3])
-        t.c_dq.wait(t.dqg.at[0:3])
-        query = key = 0.0
-        for group in range(4):
-            operand = t.in1r[group].reshape(4 * t.chip_rows, 256)
-            query = query + dot(operand, self.place(t.dqg[group], r + PAD))
-            key = key + dot(t.in2r[group].reshape(4 * t.chip_rows, r), expand_heads(t.qg[group]))
-        grad = jnp.concatenate([query, key], 1).reshape(t.r2f.shape)
-        t.r2f[...] = grad
-        t.r2b[...] = grad.astype(BF16)
-        t.c_r2 = self.to_copies(t, t.r2b, t.r2r)
-
-    def rounds_end(self, t):
-        start = pl.multiple_of((1 - self.core) * t.rows, 8)
-        t.c_last = []
-        for group, f, landing, total, last in (
-            (t.c_r1, t.r1f, t.r1r, t.r1s, t.r1p),
-            (t.c_r2, t.r2f, t.r2r, t.r2s, t.r2p),
-        ):
-            group.wait(landing)
-            values = f[t.r]
-            for slot in range(3):
-                values = values + landing[slot].astype(F32)
-            total[...] = values
-            pair = Group(self)
-            pair.send(total.at[pl.ds(start, t.rows)], last, 1)
-            t.c_last.append(pair)
-
-    def rounds_done(self, t):
-        rows, d, b = t.rows, t.width, t.block
+                self.dmap[...] = values[:, 2 * d :]
+
+    def feed_weights_done(self, t):
+        rows, b = t.rows, t.block
         start = pl.multiple_of(self.core * rows, 8)
-        done = []
-        for pair, total, last in zip(t.c_last, (t.r1s, t.r2s), (t.r1p, t.r2p), strict=True):
-            pair.wait(last)
-            done.append(total[pl.ds(start, rows), :] + last[...])
-        t.d_qkv[:, 0 : 2 * d] = done[1]
-        t.d_qkv[:, 2 * d : 3 * d] = done[0][:, 0:d]
-        t.d_out[...] = done[0][:, d : 2 * d]
-        if t.extra:
-            self.dmap[...] = done[0][:, 2 * d :]
         t.c_fc.wait(t.gf4)
         for group in range(4):
             own, got = t.gf3[group, pl.ds(start, rows), :], t.gf4[group]
             for half in range(2):
                 values = jnp.where(self.core == half, own, got)
                 for copy in range(4):
-                    device = t.device_of(group, copy, half)
+                    device = t.ff.device_of(group, copy, half)
                     t.d_fc[:, b * device : b * (device + 1)] = values[:, b * copy : b * (copy + 1)]
 
 
@@ -1436,17 +1515,21 @@
 
 def hand_over(results):
     count = len(results)
+    cuts = []
+    for index, value in enumerate(results):
+        rows = value.shape[0]
+        step = 120 if rows > 120 and rows % 120 == 0 else rows
+        cuts += [(index, start, step) for start in range(0, rows, step)]
 
     def kernel(*refs):
         came, went = refs[3 * count], refs[3 * count + 1]
-        reads = [
-            pltpu.make_async_copy(refs[index], refs[2 * count + index], came.at[index])
-            for index in range(count)
-        ]
-        writes = [
-            pltpu.make_async_copy(refs[2 * count + index], refs[count + index], went.at[index])
-            for index in range(count)
-        ]
+        reads, writes = [], []
+        for at, (index, start, rows) in enumerate(cuts):
+            src, dst, mid = (refs[index + part * count] for part in range(3))
+            if rows != src.shape[0]:
+                src, dst, mid = (ref.at[start : start + rows] for ref in (src, dst, mid))
+            reads.append(pltpu.make_async_copy(src, mid, came.at[at]))
+            writes.append(pltpu.make_async_copy(mid, dst, went.at[at]))
         for read in reads:
             read.start()
         for read, write in zip(reads, writes, strict=True):
@@ -1455,7 +1538,7 @@
         for write in writes:
             write.wait()
 
-    sems = pltpu.SemaphoreType.DMA((count,))
+    sems = pltpu.SemaphoreType.DMA((len(cuts),))
     return pl.pallas_call(
         kernel,
         out_shape=tuple(jax.ShapeDtypeStruct(value.shape, value.dtype) for value in results),

time: 151 us -> 133 us (0.88)
  Pallas kernels: 149 us -> 131 us
    pallas_call x1, Pallas kernels: 144 us -> 127 us  [local_fused(): pl.pallas_call(kernel, out_shape=tuple(joined(parts[3:6], 1)), in_specs=j...]
where the time goes in v3:
time: 133 us
  Pallas kernels  131 us (98%)
  between operations  1.48 us (1%)
    pallas_call x1, Pallas kernels, local_fused(): pl.pallas_call(kernel, out_shape=tuple(joined(parts[3:6], 1)), in_specs=j...  127 us
    pallas_call x1, Pallas kernels, hand_over(): pl.pallas_call(kernel, out_shape=tuple((jax.ShapeDtypeStruct(value.shape,...  4.34 us

profile of v3, /device:TPU:0, one launch (start us, length us, event | category | flops | bytes accessed | tf_op | source)
XLA Modules:
  0.0 132.6 jit_solution(607455172324144446)
XLA Ops:
  1.3 126.8 %contrastive_step.1 = (f32[600,768]{1,0:T(8,128)}, f32[24,2304]{1,0:T(8,128)}, f32[24,768]{1,0:T(8,128)}, f32[24,3072]{1,0:T(8,128)}, f32[96,768]{1,0:T(8,128)},...) custom-call(bf16[600,768]{1,0:T(8,128)(2,1)} %refs_0_.1, ...), custom_call_target="tpu_custom_call" | custom-call | tf_op jit(solution)/shard_map/contrastive_step/pallas_call | solution.py:1661
  128.1 4.3 %hand_over.1 = (f32[600,768]{1,0:T(8,128)}, f32[24,2304]{1,0:T(8,128)}, f32[24,768]{1,0:T(8,128)}, f32[24,3072]{1,0:T(8,128)}, f32[96,768]{1,0:T(8,128)}, /*inde...) custom-call(f32[600,768]{1,0:T(8,128)} %get-tuple-element.51.refs_0_, ...), custom_call_target="tpu_custom_call" | custom-call | tf_op jit(solution)/shard_map/hand_over/pallas_call | solution.py:1542

commit v4 on v3

--- a/solution.py
+++ b/solution.py
@@ -403,7 +403,7 @@
 CHIP_PEERS = tuple(range(2, 32, 2))
 ALL_PEERS = (1, 3, 5, 7, 9, 17, 25) + CHIP_PEERS
 PAD = 16
-N_SEMS = 100
+N_SEMS = 84
 STEP_ROWS = 32
 
 
@@ -515,6 +515,7 @@
         self.row_pad = -(-rows // 16) * 16
         self.fold = 1 if rows % 16 == 0 else 2
         self.tiles = 4 * (self.queries // 128) + 2 * (self.queries % 128 // 64)
+        self.near = 2 if along_z else 3
         self.sums = {}
         self.c_r1 = self.c_r2 = None
 
@@ -797,6 +798,11 @@
             t.first.begin_z()
             t.first.begin_plane()
         for t in both:
+            t.second.begin_z()
+        for t in both:
+            self.widen_begin(t)
+        third.begin_z()
+        for t in both:
             self.narrow_begin(t)
         self.standardize(tt)
         vectors.middle()
@@ -807,8 +813,6 @@
             t.second.begin_plane()
         for t in both:
             t.first.middle()
-        for t in both:
-            t.second.begin_z()
         for t in both:
             t.first.relay()
         vectors.end()
@@ -821,19 +825,16 @@
         for t in both:
             t.second.middle()
         for t in both:
-            self.widen_begin(t)
-        third.begin_z()
-        for t in both:
             t.first.end()
         third.begin_plane()
+        for t in both:
+            self.widen_middle(t)
         for t in both:
             t.second.relay()
         for t in both:
             t.first.done()
             self.attend(t)
             self.early_operands(t)
-        for t in both:
-            self.widen_middle(t)
         third.middle()
         third.relay_own()
         for t in both:
@@ -842,6 +843,10 @@
         for t in both:
             t.second.done()
             self.mix(t)
+        for t in both:
+            self.narrow_middle(t)
+        for t in both:
+            self.widen_relay(t)
         third.end()
         for t in both:
             t.c_o = self.share_group(t.at, t.og, t.o)
@@ -1031,14 +1036,31 @@
         t.widen.wait(t.mf.at[0:3])
         t.widen = Group(self)
         part = t.ff.chips_of_copy(t.fa, t.ff.r)
-        for mask in t.ff.copy_peers:
+        for mask in t.ff.copy_peers[: t.near]:
             t.widen.send(part, part, mask)
 
     def narrow_begin(self, t):
         t.narrow = Group(self)
-        for mask in t.ff.copy_peers:
+        for mask in t.ff.copy_peers[: t.near]:
             t.narrow.send(t.proj, t.wp.at[t.ff.r], mask)
         t.wp[t.ff.r] = t.proj[...]
+
+    def narrow_middle(self, t):
+        t.narrow.wait(t.wp.at[0 : t.near])
+        if t.ff.along_z:
+            t.narrow_far, half = Group(self), t.block // 2
+            for part, near, to in ((0, 2, 4), (1, 4, 2)):
+                rows = pl.ds(part * half, half)
+                there = t.wp.at[t.ff.copy_of(self.at_peer(near)), rows]
+                t.narrow_far.send(there, there, to)
+
+    def widen_relay(self, t):
+        t.widen.wait(t.fa.at[0 : t.near])
+        if t.ff.along_z:
+            t.widen_far = Group(self)
+            for part, near, to in ((0, 2, 4), (1, 4, 2)):
+                there = t.fa.at[2 * part : 2 * part + 2, t.ff.copy_of(self.at_peer(near))]
+                t.widen_far.send(there, there, to)
 
     def queries(self, t):
         a, xh, vec = t.a, t.xh, t.vecs
@@ -1103,8 +1125,9 @@
 
     def feed(self, t):
         d, g = t.width, t.group
-        t.widen.wait(t.fa.at[0:3])
-        t.narrow.wait(t.wp.at[0:3])
+        if t.ff.along_z:
+            t.widen_far.wait(t.fa.at[0])
+            t.narrow_far.wait(t.wp.at[0])
         t.line.wait(t.ci.at[0:7])
         c = t.ci[...].reshape(8 * PAD, d)
         up = dot(c, t.fa[...].reshape(d, g)) + t.bias[0:1, :]

time: 133 us -> 125 us (0.940)
  Pallas kernels: 131 us -> 124 us
    pallas_call x1, Pallas kernels: 127 us -> 119 us  [local_fused(): pl.pallas_call(kernel, out_shape=tuple(joined(parts[3:6], 1)), in_specs=j...]
where the time goes in v4:
time: 125 us
  Pallas kernels  124 us (99%)
  between operations  1.48 us (1%)
    pallas_call x1, Pallas kernels, local_fused(): pl.pallas_call(kernel, out_shape=tuple(joined(parts[3:6], 1)), in_specs=j...  119 us
    pallas_call x1, Pallas kernels, hand_over(): pl.pallas_call(kernel, out_shape=tuple((jax.ShapeDtypeStruct(value.shape,...  4.34 us

profile of v4, /device:TPU:0, one launch (start us, length us, event | category | flops | bytes accessed | tf_op | source)
XLA Modules:
  0.0 125.1 jit_solution(14199898163530719258)
XLA Ops:
  1.3 119.3 %contrastive_step.1 = (f32[600,768]{1,0:T(8,128)}, f32[24,2304]{1,0:T(8,128)}, f32[24,768]{1,0:T(8,128)}, f32[24,3072]{1,0:T(8,128)}, f32[96,768]{1,0:T(8,128)},...) custom-call(bf16[600,768]{1,0:T(8,128)(2,1)} %refs_0_.1, ...), custom_call_target="tpu_custom_call" | custom-call | tf_op jit(solution)/shard_map/contrastive_step/pallas_call | solution.py:1684
  120.6 4.3 %hand_over.1 = (f32[600,768]{1,0:T(8,128)}, f32[24,2304]{1,0:T(8,128)}, f32[24,768]{1,0:T(8,128)}, f32[24,3072]{1,0:T(8,128)}, f32[96,768]{1,0:T(8,128)}, /*inde...) custom-call(f32[600,768]{1,0:T(8,128)} %get-tuple-element.51.refs_0_, ...), custom_call_target="tpu_custom_call" | custom-call | tf_op jit(solution)/shard_map/hand_over/pallas_call | solution.py:1565

commit v5 on v4

--- a/solution.py
+++ b/solution.py
@@ -548,6 +548,7 @@
             dcs=v((8, PAD, d), BF16),
             dcr=v((7, PAD, d), BF16),
             u=v((8 * PAD, g), F32),
+            prj=v((b, d), F32),
             mt=v((4, b, 8 * PAD), BF16),
             mtr=v((4, b, 8 * PAD), BF16),
             gff=v((4, 4, cr, g), F32),
@@ -877,7 +878,6 @@
             self.feed_proj(t)
         for t in both:
             self.attend_back(t)
-        for t in both:
             self.attend_back_end(t)
         for t in both:
             self.input_gradient(t)
@@ -904,6 +904,7 @@
             self.round_end(t, 1)
         for t in both:
             self.copy_out(t).wait()
+            self.proj_out(t).wait()
         for group in self.groups:
             group.finish()
 
@@ -1308,7 +1309,8 @@
             if t is self.ti:
                 d_raw = self.through_map(d_raw)[0]
             total = total + dot(t.mtr[copy], d_raw.astype(BF16))
-        t.d_proj[...] = total
+        t.prj[...] = total
+        self.proj_out(t).start()
 
     def feed_weights_middle(self, t):
         b = t.block
@@ -1375,6 +1377,9 @@
         rh[2 * r : 2 * r + PAD, :] = high
         rh[2 * r + PAD : 2 * r + 2 * PAD, :] = low
 
+    def proj_out(self, t):
+        return pltpu.make_async_copy(t.prj, t.d_proj, self.osem.at[2 if t is self.ti else 3])
+
     def copy_out(self, t):
         return pltpu.make_async_copy(t.dxs, t.d_x, self.osem.at[0 if t is self.ti else 1])
 
@@ -1382,15 +1387,17 @@
         r, d = t.queries, t.width
         lh, da, gp, xh, inv, vec, out = t.lh, t.da, t.gp, t.xh, t.inv, t.vecs, t.dxs
         da[...] = dot_tn(lh[...], t.rh[...])
-        high, low = split_two(t.g1)
-        gp[...] = dot_tn(lh[2 * r : 2 * r + 2 * PAD, :], jnp.concatenate([high, low], 0))
+        image = t is self.ti
+        if not image:
+            high, low = split_two(t.g1)
+            gp[...] = dot_tn(lh[2 * r : 2 * r + 2 * PAD, :], jnp.concatenate([high, low], 0))
         step = STEP_ROWS
         full = t.real_tokens // step
 
         def one(rows, carry):
             z, normed = da[rows, :], xh[rows, :]
             inner = small_norm_back(z, normed, inv[rows, 0:1], vec[0:1, :])
-            return inner + gp[rows, :], (
+            return inner if image else inner + gp[rows, :], (
                 carry[0] + jnp.sum((z * normed).reshape(step // 8, 8, d), 0),
                 carry[1] + jnp.sum(z.reshape(step // 8, 8, d), 0),
             )
@@ -1406,6 +1413,10 @@
         if rest:
             last, carry = one(slice(start, start + step), carry)
             out[start : start + rest, :] = last[:rest]
+        if image:
+            for at in range(self.images):
+                place = slice(at * TOK_I, at * TOK_I + 1)
+                out[place, :] = out[place, :] + t.g1[at : at + 1]
         self.copy_out(t).start()
         s = t.sums
         rows = [col_sum(carry[0]), col_sum(carry[1])]
@@ -1653,8 +1664,8 @@
         (ti, img_args, [in_vmem] * 7),
         (tt, txt_args, [in_vmem] * 7),
         (None, more_args, [in_vmem, in_smem, in_smem, in_smem]),
-        (ti, tower_outs(ti), [anywhere] + [in_vmem] * 6),
-        (tt, tower_outs(tt), [anywhere] + [in_vmem] * 6),
+        (ti, tower_outs(ti), [anywhere] + [in_vmem] * 3 + [anywhere] + [in_vmem] * 2),
+        (tt, tower_outs(tt), [anywhere] + [in_vmem] * 3 + [anywhere] + [in_vmem] * 2),
         (None, more_outs, [in_vmem] * 3),
         (ti, ti.scratch(), None),
         (tt, tt.scratch(), None),
@@ -1664,7 +1675,7 @@
             dict(
                 ssem=pltpu.SemaphoreType.DMA((N_SEMS,)),
                 rsem=pltpu.SemaphoreType.DMA((N_SEMS,)),
-                osem=pltpu.SemaphoreType.DMA((2,)),
+                osem=pltpu.SemaphoreType.DMA((4,)),
             ),
             None,
         ),

time: 125 us -> 125 us (level)
  no operation moved by 1% of the time
where the time goes in v5:
time: 125 us
  Pallas kernels  123 us (98%)
  between operations  1.48 us (1%)
    pallas_call x1, Pallas kernels, local_fused(): pl.pallas_call(kernel, out_shape=tuple(joined(parts[3:6], 1)), in_specs=j...  119 us
    pallas_call x1, Pallas kernels, hand_over(): pl.pallas_call(kernel, out_shape=tuple((jax.ShapeDtypeStruct(value.shape,...  4.34 us

profile of v5, /device:TPU:0, one launch (start us, length us, event | category | flops | bytes accessed | tf_op | source)
XLA Modules:
  0.0 124.8 jit_solution(13615201523446846652)
XLA Ops:
  1.3 119.0 %contrastive_step.1 = (f32[600,768]{1,0:T(8,128)}, f32[24,2304]{1,0:T(8,128)}, f32[24,768]{1,0:T(8,128)}, f32[24,3072]{1,0:T(8,128)}, f32[96,768]{1,0:T(8,128)},...) custom-call(bf16[600,768]{1,0:T(8,128)(2,1)} %refs_0_.1, ...), custom_call_target="tpu_custom_call" | custom-call | tf_op jit(solution)/shard_map/contrastive_step/pallas_call | solution.py:1695
  120.3 4.3 %hand_over.1 = (f32[600,768]{1,0:T(8,128)}, f32[24,2304]{1,0:T(8,128)}, f32[24,768]{1,0:T(8,128)}, f32[24,3072]{1,0:T(8,128)}, f32[96,768]{1,0:T(8,128)}, /*inde...) custom-call(f32[600,768]{1,0:T(8,128)} %get-tuple-element.51.refs_0_, ...), custom_call_target="tpu_custom_call" | custom-call | tf_op jit(solution)/shard_map/hand_over/pallas_call | solution.py:1576
